TPU v7x, 32 devices: a whole 2x2x4 slice. The times are simulated.
32 devices in a mesh: seq: 4 (over y, x), fsdp: 8 (over z, core).
Axes of the slice: x: 2, y: 2, z: 4, core: 2. Of those that a mesh axis runs over, the one named last changes fastest.
Arguments:
- hidden: bfloat16 [8, 1024, 1024], P('fsdp', 'seq'), may hold values from -6 to 6
- lengths: int32 [8], P('fsdp'), may hold values from 1 to 1024, 5120 in all
- expert_ids: int32 [8, 1024, 1], P('fsdp', 'seq'), may hold values from 0 to 15; in each aligned block of 256 rows (0 to 255, 256 to 511, ..., all dimensions but the last counted through in order) at most 32 rows name the same one
- attn_gain: bfloat16 [1024], P(('seq', 'fsdp')), may hold values from 0.5 to 1.5
- qkv_weight: bfloat16 [1024, 3072], P(('seq', 'fsdp')), may hold values from -0.1875 to 0.1875
- out_weight: bfloat16 [1024, 1024], P(('seq', 'fsdp')), may hold values from -2 to 2
- moe_gain: bfloat16 [1024], P(('seq', 'fsdp')), may hold values from 0.5 to 1.5
- router_weight: bfloat16 [1024, 16], P(('seq', 'fsdp')), may hold values from -0.09375 to 0.09375
- expert_in: bfloat16 [16, 1024, 4096], P('fsdp', None, 'seq'), may hold values from -0.1875 to 0.1875
- expert_out: bfloat16 [16, 4096, 1024], P('fsdp', 'seq'), may hold values from -12 to 12
- out_grad: bfloat16 [8, 1024, 1024], P('fsdp', 'seq'), may hold values from -6 to 6
Outputs:
- output: bfloat16 [8, 1024, 1024], P('fsdp', 'seq')
- input_grad: float32 [8, 1024, 1024], P('fsdp', 'seq')
- attn_gain_grad: float32 [1024], P(('seq', 'fsdp'))
- qkv_grad: float32 [1024, 3072], P(('seq', 'fsdp'))
- out_weight_grad: float32 [1024, 1024], P(('seq', 'fsdp'))
- moe_gain_grad: float32 [1024], P(('seq', 'fsdp'))
- router_grad: float32 [1024, 16], P(('seq', 'fsdp'))
- expert_in_grad: float32 [16, 1024, 4096], P('fsdp', None, 'seq')
- expert_out_grad: float32 [16, 4096, 1024], P('fsdp', 'seq')
Inputs may be any that keep to these rules, and one draw needn't show every extreme that they name: `lengths`: the longest slot holds exactly 1024 valid positions. `expert_ids`: in each aligned block of 256 tokens (the tokens of one device, slots first, then positions), no expert is named more than 32 times, and in some block one expert is named exactly 32 times.
All inputs are finite; a program needn't handle non-finite values. No bound on the sum of `lengths` on one device may be relied on, other than what follows from the above.
Results may differ from a plain program's by a relative error of at most 0.017.
Values may be sent and summed in bfloat16 or wider, within the bound.
A program may use at most 192 MiB of HBM per device.

v0:
```python
import functools

import jax
import jax.numpy as jnp
from jax import lax
from jax.experimental import pallas as pl
from jax.experimental.pallas import tpu as pltpu
from jax.sharding import PartitionSpec as P

HEAD_DIM = 64
EPS = 1e-05
MASKED = -1e30
ROOT = 0.7978845608028654
TILE = 256
GRAD = 256
MESH = pl.DeviceIdType.MESH
ANY = pl.BlockSpec(memory_space=pl.ANY)


def scaled_norm(value, gain):
    return value * lax.rsqrt(jnp.mean(value * value, axis=-1, keepdims=True) + EPS) * gain


def gelu_tanh(value):
    return jax.nn.gelu(value, approximate=True)


def times(left, right):
    return jnp.dot(left, right, preferred_element_type=jnp.float32)


def times_transposed(left, right):
    return lax.dot_general(
        left, right, (((1,), (1,)), ((), ())), preferred_element_type=jnp.float32
    )


def transposed_times(left, right):
    return lax.dot_general(
        left, right, (((0,), (0,)), ((), ())), preferred_element_type=jnp.float32
    )


def greet(axis, peers):
    barrier = pltpu.get_barrier_semaphore()
    for peer in peers:
        pl.semaphore_signal(barrier, inc=1, device_id={axis: peer}, device_id_type=MESH)
    pl.semaphore_wait(barrier, len(peers))


def remote(axis, peer, source, target, send, receive):
    copy = pltpu.make_async_remote_copy(
        source, target, send, receive, device_id={axis: peer}, device_id_type=MESH
    )
    copy.start()
    return copy


def call(kernel, inputs, outputs, scratch, number):
    return pl.pallas_call(
        kernel,
        out_shape=outputs,
        in_specs=[ANY] * len(inputs),
        out_specs=jax.tree.map(lambda _: ANY, outputs),
        scratch_shapes=scratch,
        compiler_params=pltpu.CompilerParams(
            collective_id=number, has_side_effects=True, vmem_limit_bytes=48 * 2**20
        ),
    )(*inputs)


def exchange_kernel(axis, count, views, *refs):
    arrays = len(views)
    sources, targets = refs[:arrays], refs[arrays : 2 * arrays]
    send, receive, local = refs[2 * arrays :]
    me = lax.axis_index(axis)
    peers = [lax.rem(me + step, count) for step in range(1, count)]
    greet(axis, peers)
    copies = []
    for step, peer in enumerate(peers):
        for a, (out_of, into) in enumerate(views):
            copies.append(
                remote(
                    axis,
                    peer,
                    out_of(sources[a], peer),
                    into(targets[a], me),
                    send.at[a, step],
                    receive.at[a, step],
                )
            )
    for a, (out_of, into) in enumerate(views):
        copy = pltpu.make_async_copy(out_of(sources[a], me), into(targets[a], me), local.at[a])
        copy.start()
        copies.append(copy)
    for copy in copies:
        copy.wait()


def exchange(axis, count, inputs, outputs, views, number):
    arrays = len(views)
    return call(
        functools.partial(exchange_kernel, axis, count, views),
        inputs,
        outputs,
        [
            pltpu.SemaphoreType.DMA((arrays, count - 1)),
            pltpu.SemaphoreType.DMA((arrays, count - 1)),
            pltpu.SemaphoreType.DMA((arrays,)),
        ],
        number,
    )


def lead(ref, place):
    return ref.at[place]


def second(ref, place):
    return ref.at[:, place]


def whole(ref, place):
    return ref


def spread_kernel(source, target, send, receive, local):
    me = lax.axis_index("seq")
    one, two, both = me ^ 1, me ^ 2, me ^ 3
    half = source.shape[1] // 2
    greet("seq", [one, two])
    parts = (pl.ds(0, half), pl.ds(half, half))
    own = pltpu.make_async_copy(source, target.at[:, me], local)
    own.start()
    copies = {}
    for side, peer in enumerate((one, two)):
        for order in range(2):
            part = (order + side) % 2
            copies[side, part] = remote(
                "seq",
                peer,
                source.at[:, parts[part]],
                target.at[:, me, parts[part]],
                send.at[side, part],
                receive.at[side, part],
            )
    relayed = []
    for side, (origin, peer) in enumerate(((one, two), (two, one))):
        copies[side, side].wait_recv()
        block = target.at[:, origin, parts[side]]
        relayed.append(remote("seq", peer, block, block, send.at[2, side], receive.at[2, side]))
    for side in range(2):
        copies[side, 1 - side].wait_recv()
        for part in range(2):
            copies[side, part].wait_send()
    for copy in relayed:
        copy.wait()
    own.wait()


def spread(source, number):
    return call(
        spread_kernel,
        (source,),
        jax.ShapeDtypeStruct((source.shape[0], 4, *source.shape[1:]), source.dtype),
        [
            pltpu.SemaphoreType.DMA((3, 2)),
            pltpu.SemaphoreType.DMA((3, 2)),
            pltpu.SemaphoreType.DMA,
        ],
        number,
    )


def collect_kernel(source, target, mine, first, second_in, outgoing, load, send, receive, store):
    me = lax.axis_index("seq")
    one, two, both = me ^ 1, me ^ 2, me ^ 3
    width = source.shape[3] // 2
    greet("seq", [one, two])
    copies = []
    for side, (near, rest) in enumerate(((one, two), (two, one))):
        lanes = pl.ds(side * width, width)
        for order, block in enumerate((both, near)):
            copies.append(
                remote(
                    "seq",
                    near,
                    source.at[:, block, :, lanes],
                    first.at[side, order],
                    send.at[side, order],
                    receive.at[side, order],
                )
            )
        for order, block in enumerate((rest, me)):
            pltpu.make_async_copy(
                source.at[:, block, :, lanes], mine.at[side, order], load.at[side, order]
            ).start()
    passed = []
    for side, rest in enumerate((two, one)):
        copies[side * 2].wait_recv()
        pltpu.make_async_copy(mine.at[side, 0], mine.at[side, 0], load.at[side, 0]).wait()
        outgoing[side] = (
            mine[side, 0].astype(jnp.float32) + first[side, 0].astype(jnp.float32)
        ).astype(outgoing.dtype)
        passed.append(
            remote("seq", rest, outgoing.at[side], second_in.at[side], send.at[2, side], receive.at[2, side])
        )
    for side in range(2):
        copies[side * 2 + 1].wait_recv()
        pltpu.make_async_copy(mine.at[side, 1], mine.at[side, 1], load.at[side, 1]).wait()
        passed[side].wait_recv()
        mine[side, 1] = (
            mine[side, 1].astype(jnp.float32)
            + first[side, 1].astype(jnp.float32)
            + second_in[side].astype(jnp.float32)
        ).astype(mine.dtype)
        out = pltpu.make_async_copy(
            mine.at[side, 1], target.at[:, :, pl.ds(side * width, width)], store.at[side]
        )
        out.start()
    for side in range(2):
        pltpu.make_async_copy(
            mine.at[side, 1], target.at[:, :, pl.ds(side * width, width)], store.at[side]
        ).wait()
    for copy in copies + passed:
        copy.wait_send()


def collect(source, number):
    a, _, rows, width = source.shape
    dma = pltpu.SemaphoreType.DMA
    block = (a, rows, width // 2)
    return call(
        collect_kernel,
        (source,),
        jax.ShapeDtypeStruct((a, rows, width), source.dtype),
        [
            pltpu.VMEM((2, 2, *block), source.dtype),
            pltpu.VMEM((2, 2, *block), source.dtype),
            pltpu.VMEM((2, *block), source.dtype),
            pltpu.VMEM((2, *block), source.dtype),
            dma((2, 2)),
            dma((3, 2)),
            dma((3, 2)),
            dma((2,)),
        ],
        number,
    )


def moe_kernel(
    chips, cap, experts_all, send_rows, up_rows, route, w_in, w_out,
    ret, dw_in, dw_out,
    R, U, G, A, I, PB, first, second, W1, W2, RT, stage,
    load, own, z_send, z_recv, s_send, s_recv, y_send, y_recv,
    c_send, c_recv, d_send, d_recv, r_send, r_recv, store,
):
    me, place = lax.axis_index("seq"), lax.axis_index("fsdp")
    one, two, both = me ^ 1, me ^ 2, me ^ 3
    chip, core = place // 2, lax.rem(place, 2)
    sibling = place ^ 1
    count = chips * 2
    part = 2 * cap
    chunk = 4 * part
    barrier = pltpu.get_barrier_semaphore()
    for peer in (one, two):
        pl.semaphore_signal(barrier, inc=1, device_id={"seq": peer}, device_id_type=MESH)
    for step in range(1, count):
        pl.semaphore_signal(
            barrier, inc=1, device_id={"fsdp": lax.rem(place + step, count)}, device_id_type=MESH
        )
    pl.semaphore_wait(barrier, 2 + count - 1)

    def rows_of(k, s):
        return pl.ds(k * chunk + s * part, part)

    loads = []

    def local(source, target, sem):
        copy = pltpu.make_async_copy(source, target, sem)
        copy.start()
        return copy

    dispatched = []
    own_rows = None
    for k in range(chips):
        to = lax.rem(chip - k + chips, chips)
        for c in range(2):
            target = R.at[:, pl.ds(k * chunk + me * part + core * cap, cap)]
            if k == 0:
                if c == 0:
                    own_rows = local(send_rows.at[place], target, own.at[0])
                    dispatched.append(
                        remote("fsdp", sibling, send_rows.at[sibling], target, z_send.at[0, 0], z_recv.at[0, 0])
                    )
                continue
            peer = to * 2 + (core ^ c)
            dispatched.append(
                remote("fsdp", peer, send_rows.at[peer], target, z_send.at[k, c], z_recv.at[k, c])
            )

    def z_arrived(k):
        if k == 0:
            own_rows.wait()
            dispatched[0].wait_recv()
        else:
            dispatched[2 * k - 1].wait_recv()
            dispatched[2 * k].wait_recv()

    sent = {}

    def spread_out(k):
        for side, peer in enumerate((one, two)):
            for order in range(2):
                j = (order + side) % 2
                block = R.at[j, rows_of(k, me)]
                sent[k, side, j] = remote("seq", peer, block, block, s_send.at[k, side, j], s_recv.at[k, side, j])

    def relay(k):
        for side, (origin, peer) in enumerate(((one, two), (two, one))):
            sent[k, side, side].wait_recv()
            block = R.at[side, rows_of(k, origin)]
            sent[k, 2, side] = remote("seq", peer, block, block, y_send.at[k, side], y_recv.at[k, side])

    def all_arrived(k):
        for side in range(2):
            sent[k, side, 1 - side].wait_recv()
            sent[k, 2, side].wait_recv()

    def experts(k, j):
        rows = pl.ds(k * chunk, chunk)
        logits = times(R[j, rows, :], RT[...])
        lane = lax.broadcasted_iota(jnp.int32, logits.shape, 1)
        logits = jnp.where(lane < experts_all, logits, MASKED)
        powers = jnp.exp(logits - jnp.max(logits, axis=1, keepdims=True))
        picked = jnp.sum(jnp.where(lane == place * 2 + j, powers, 0.0), axis=1, keepdims=True)
        gate = picked / jnp.sum(powers, axis=1, keepdims=True)
        G[j, rows, :] = (U[j, rows, :].astype(jnp.float32) * gate).astype(G.dtype)

        @pl.loop(0, W1.shape[2] // TILE)
        def _(t):
            cols = pl.ds(pl.multiple_of(t * TILE, TILE), TILE)
            v = times(R[j, rows, :], W1[j, :, cols])
            grad = times_transposed(G[j, rows, :], W2[j, cols, :])
            square = v * v
            t = jnp.tanh(ROOT * v * (1.0 + 0.044715 * square))
            half = 0.5 * (1.0 + t)
            A[j, rows, cols] = (v * half).astype(A.dtype)
            slope = half + 0.5 * v * (1.0 - t * t) * (ROOT * (1.0 + 0.134145 * square))
            I[j, rows, cols] = (grad * slope).astype(I.dtype)

        @pl.loop(0, W1.shape[1] // TILE)
        def _(t):
            cols = pl.ds(pl.multiple_of(t * TILE, TILE), TILE)
            PB[0, j, rows, cols] = times(A[j, rows, :], W2[j, :, cols]).astype(PB.dtype)
            PB[1, j, rows, cols] = times_transposed(I[j, rows, :], W1[j, cols, :]).astype(PB.dtype)

    summed = {}

    def near_of(j):
        return (one, two) if j == 0 else (two, one)

    def collect_one(k, j):
        near, rest = near_of(j)
        for a in range(2):
            for order, block in enumerate((both, near)):
                summed[a, k, j, order] = remote(
                    "seq", near, PB.at[a, j, rows_of(k, block)], first.at[a, j, k, order],
                    c_send.at[a, j, k, order], c_recv.at[a, j, k, order],
                )

    def collect_two(k, j):
        near, rest = near_of(j)
        for a in range(2):
            summed[a, k, j, 0].wait_recv()
            first[a, j, k, 0] = (
                first[a, j, k, 0].astype(jnp.float32) + PB[a, j, rows_of(k, rest), :].astype(jnp.float32)
            ).astype(first.dtype)
            summed[a, k, j, 2] = remote(
                "seq", rest, first.at[a, j, k, 0], second.at[a, j, k], d_send.at[a, j, k], d_recv.at[a, j, k]
            )

    returns = {}

    def collect_three(k, j):
        for a in range(2):
            summed[a, k, j, 1].wait_recv()
            summed[a, k, j, 2].wait_recv()
            first[a, j, k, 1] = (
                first[a, j, k, 1].astype(jnp.float32)
                + PB[a, j, rows_of(k, me), :].astype(jnp.float32)
                + second[a, j, k].astype(jnp.float32)
            ).astype(first.dtype)
            to = lax.rem(chip + k, chips)
            target = ret.at[a, place, j]
            for c in range(2):
                if k == 0:
                    if c == 0:
                        returns[a, k, j, 0] = local(
                            first.at[a, j, k, 1, pl.ds(core * cap, cap)], target, own.at[1 + a * 2 + j]
                        )
                        returns[a, k, j, 1] = remote(
                            "fsdp", sibling, first.at[a, j, k, 1, pl.ds((core ^ 1) * cap, cap)], target,
                            r_send.at[a, j, k, 1], r_recv.at[a, j, k, 1],
                        )
                    continue
                returns[a, k, j, c] = remote(
                    "fsdp", to * 2 + (core ^ c), first.at[a, j, k, 1, pl.ds((core ^ c) * cap, cap)], target,
                    r_send.at[a, j, k, c], r_recv.at[a, j, k, c],
                )

    staged = {}

    def weight_grads(j, which):
        left, right, out = ((R, I, dw_in), (A, G, dw_out))[which]
        for m in range(left.shape[2] // GRAD):
            slot = m % 2
            lanes = slice(m * GRAD, (m + 1) * GRAD)
            if slot in staged:
                staged.pop(slot).wait()

            @pl.loop(0, right.shape[2] // TILE)
            def _(t):
                cols = pl.ds(pl.multiple_of(t * TILE, TILE), TILE)
                stage[slot, :, cols] = transposed_times(left[j, :, lanes], right[j, :, cols])

            staged[slot] = local(stage.at[slot], out.at[j, lanes], store.at[slot])

    for j in range(2):
        loads.append(local(w_in.at[j], W1.at[j], load.at[j]))
        loads.append(local(w_out.at[j], W2.at[j], load.at[2 + j]))
    loads.append(local(route, RT, load.at[4]))
    loads.append(local(up_rows, U, load.at[5]))
    z_arrived(0)
    spread_out(0)
    for copy in loads:
        copy.wait()
    for k in range(chips):
        relay(k)
        if k + 1 < chips:
            z_arrived(k + 1)
            spread_out(k + 1)
        all_arrived(k)
        experts(k, 0)
        collect_one(k, 0)
        if k:
            collect_two(k - 1, 0)
            collect_two(k - 1, 1)
        experts(k, 1)
        collect_one(k, 1)
        if k:
            collect_three(k - 1, 0)
            collect_three(k - 1, 1)
    last = chips - 1
    weight_grads(0, 0)
    collect_two(last, 0)
    collect_two(last, 1)
    weight_grads(0, 1)
    weight_grads(1, 0)
    collect_three(last, 0)
    collect_three(last, 1)
    weight_grads(1, 1)
    for copy in staged.values():
        copy.wait()
    for copy in dispatched:
        copy.wait_send()
    for copy in sent.values():
        copy.wait_send()
    for copy in summed.values():
        copy.wait_send()
    for (a, k, j, c), copy in returns.items():
        copy.wait()


def moe(send_rows, up_rows, route, w_in, w_out, experts_all, number):
    S, low, dma = jax.ShapeDtypeStruct, jnp.bfloat16, pltpu.SemaphoreType.DMA
    owners, _, cap, width = send_rows.shape
    chips = owners // 2
    hidden_units = w_in.shape[2]
    count = owners * cap * 4
    part = 2 * cap

    def vmem(*shape, dtype=low):
        return pltpu.VMEM(shape, dtype)

    return pl.pallas_call(
        functools.partial(moe_kernel, chips, cap, experts_all),
        out_shape=(
            S((2, owners, 2, cap, width), low),
            S(w_in.shape, jnp.float32),
            S(w_out.shape, jnp.float32),
        ),
        in_specs=[ANY] * 5,
        out_specs=(ANY,) * 3,
        scratch_shapes=[
            vmem(2, count, width),
            vmem(2, count, width),
            vmem(2, count, width),
            vmem(2, count, hidden_units),
            vmem(2, count, hidden_units),
            vmem(2, 2, count, width),
            vmem(2, 2, chips, 2, part, width),
            vmem(2, 2, chips, part, width),
            vmem(*w_in.shape),
            vmem(*w_out.shape),
            vmem(*route.shape),
            vmem(2, GRAD, max(width, hidden_units), dtype=jnp.float32),
            dma((6,)),
            dma((5,)),
            dma((chips, 2)),
            dma((chips, 2)),
            dma((chips, 2, 2)),
            dma((chips, 2, 2)),
            dma((chips, 2)),
            dma((chips, 2)),
            dma((2, 2, chips, 2)),
            dma((2, 2, chips, 2)),
            dma((2, 2, chips)),
            dma((2, 2, chips)),
            dma((2, 2, chips, 2)),
            dma((2, 2, chips, 2)),
            dma((2,)),
        ],
        compiler_params=pltpu.CompilerParams(
            collective_id=number, has_side_effects=True, vmem_limit_bytes=58 * 2**20
        ),
        cost_estimate=pl.CostEstimate(
            flops=12 * 2 * count * width * hidden_units, bytes_accessed=2**25, transcendentals=0
        ),
    )(send_rows, up_rows, route, w_in, w_out)


def front_kernel(
    count, cap, experts_all, hidden, heads, mix, small, rows, length,
    normed_out, heads_out, mix_all, small_out, up, projected_out, attended_out, sums_out, mixed,
    staged, hid, heads_all, small_all, normed, proj, attended, sums, acc, stat,
    h_send, h_recv, q_send, q_recv, f_send, f_recv, n_send, n_recv, u_send, u_recv, m_send, m_recv,
    s_send, s_recv, x_send, x_recv, local,
):
    me, place = lax.axis_index("seq"), lax.axis_index("fsdp")
    one, two, both = me ^ 1, me ^ 2, me ^ 3
    others = (one, two, both)
    chips = count // 2
    chip, core = place // 2, lax.rem(place, 2)
    sibling = place ^ 1
    share = mix.shape[0]
    tokens = hidden.shape[0]
    group = attended.shape[1]
    part, chunk = 2 * cap, 8 * cap
    barrier = pltpu.get_barrier_semaphore()
    for peer in others:
        pl.semaphore_signal(barrier, inc=1, device_id={"seq": peer}, device_id_type=MESH)
    for step in range(1, count):
        pl.semaphore_signal(
            barrier, inc=1, device_id={"fsdp": lax.rem(place + step, count)}, device_id_type=MESH
        )
    pl.semaphore_wait(barrier, 3 + count - 1)
    finish = []

    def keep(source, target, number):
        copy = pltpu.make_async_copy(source, target, local.at[number])
        copy.start()
        return copy

    def far(k, sign):
        return lax.rem(chip + sign * k + chips, chips) * 2 + core

    def at_rows(ref, s, owner):
        return ref.at[pl.ds((s * count + owner) * share, share)]

    gathered = ((mix, mix_all), (small, small_all))
    away, near = {}, {}

    def block(a, owner):
        return heads_all.at[:, owner] if a == 2 else at_rows(gathered[a][1], me, owner)

    def send_own(a):
        source = staged if a == 2 else gathered[a][0]
        for k in range(1, chips):
            away[a, k] = remote(
                "fsdp", far(k, -1), source, block(a, place), f_send.at[a, k], f_recv.at[a, k]
            )
        near[a, 0] = remote("fsdp", sibling, source, block(a, place), n_send.at[a, 0], n_recv.at[a, 0])

    def pass_on(a):
        for k in range(1, chips):
            away[a, k].wait_recv()
            arrived = block(a, far(k, 1))
            near[a, k] = remote("fsdp", sibling, arrived, arrived, n_send.at[a, k], n_recv.at[a, k])

    direct = {}

    def both_ways(name, views, sources, send, receive):
        for side, peer in enumerate((one, two)):
            for order in range(2):
                p = (order + side) % 2
                direct[name, side, p] = remote(
                    "seq", peer, sources[p], views[p](me), send.at[side, p], receive.at[side, p]
                )

    def relay(name, views, send, receive):
        for side, (origin, peer) in enumerate(((one, two), (two, one))):
            direct[name, side, side].wait_recv()
            source = views[side](origin)
            direct[name, 2, side] = remote("seq", peer, source, source, send.at[2, side], receive.at[2, side])

    def arrived(name):
        for side in range(2):
            direct[name, side, 1 - side].wait_recv()
            direct[name, 2, side].wait_recv()

    send_own(1)
    exchanged = [
        remote("seq", peer, heads.at[peer], staged.at[me], q_send.at[i], q_recv.at[i])
        for i, peer in enumerate(others)
    ]
    own_heads = keep(heads.at[me], staged.at[me], 0)
    own_hidden = keep(hidden, hid.at[pl.ds(me * tokens, tokens)], 1)
    own_mix = keep(mix, block(0, place), 2)
    own_small = keep(small, block(1, place), 3)
    own_rows = keep(rows.at[place], up.at[:, pl.ds(me * part + core * cap, cap)], 4)
    half = tokens // 2
    hidden_views = [
        lambda origin, p=p: hid.at[pl.ds(origin * tokens + p * half, half)] for p in range(2)
    ]
    both_ways("hidden", hidden_views, [hidden.at[pl.ds(p * half, half)] for p in range(2)], h_send, h_recv)
    send_own(0)
    pass_on(1)
    own_heads.wait()
    for copy in exchanged:
        copy.wait_recv()
    own_block = keep(staged, heads_all.at[:, place], 5)
    send_own(2)
    own_small.wait()
    for k in range(chips):
        near[1, k].wait_recv()
    mine = small_all.at[pl.ds(me * count * share, count * share)]
    smalls = [remote("seq", peer, mine, mine, q_send.at[3 + i], q_recv.at[3 + i]) for i, peer in enumerate(others)]
    moved = {}
    for k in range(chips):
        for c in range(2):
            if k == 0 and c == 0:
                continue
            peer = lax.rem(chip - k + chips, chips) * 2 + (core ^ c)
            moved[k, c] = remote(
                "fsdp", peer, rows.at[peer], up.at[:, pl.ds(k * chunk + me * part + core * cap, cap)],
                u_send.at[k, c], u_recv.at[k, c],
            )

    def up_views(k):
        return [lambda origin, j=j: up.at[j, pl.ds(k * chunk + origin * part, part)] for j in range(2)]

    def up_out(k):
        if k == 0:
            own_rows.wait()
        for c in range(2):
            if (k, c) in moved:
                moved[k, c].wait_recv()
        views = up_views(k)
        both_ways(("up", k), views, [views[0](me), views[1](me)], s_send.at[k], s_recv.at[k])

    def up_relay(k):
        relay(("up", k), up_views(k), s_send.at[k], s_recv.at[k])

    relay("hidden", hidden_views, h_send, h_recv)
    pass_on(0)
    for copy in smalls:
        copy.wait_recv()
    small_kept = keep(small_all, small_out, 6)
    own_hidden.wait()
    arrived("hidden")
    up_out(0)
    own_mix.wait()
    for k in range(chips):
        near[0, k].wait_recv()
    length_rows = count // 2 * share
    mix_views = [
        lambda origin, p=p: mix_all.at[pl.ds(origin * count * share + p * length_rows, length_rows)] for p in range(2)
    ]
    both_ways("mix", mix_views, [mix_views[p](me) for p in range(2)], m_send, m_recv)
    gain = jnp.transpose(small_all[...].astype(jnp.float32))[experts_all : experts_all + 1]

    @pl.loop(0, hid.shape[0] // 128)
    def _(t):
        place_rows = pl.ds(pl.multiple_of(t * 128, 128), 128)
        value = hid[place_rows, :].astype(jnp.float32)
        scale = lax.rsqrt(jnp.mean(value * value, axis=-1, keepdims=True) + EPS)
        normed[place_rows, :] = (value * scale * gain).astype(normed.dtype)

    normed_kept = keep(normed, normed_out, 7)
    pass_on(2)
    own_block.wait()
    for k in range(chips):
        near[2, k].wait_recv()
    heads_kept = keep(heads_all, heads_out, 8)
    width = hid.shape[1]

    for p in range(3):

        @pl.loop(0, hid.shape[0] // TILE)
        def _(t):
            place_rows = pl.ds(pl.multiple_of(t * TILE, TILE), TILE)
            weights = heads_all[:, :, :, p * group : (p + 1) * group].reshape(width, group)
            proj[place_rows, p * group : (p + 1) * group] = times(normed[place_rows, :], weights).astype(proj.dtype)

    projected_kept = keep(proj, projected_out, 9)
    head_of = lax.broadcasted_iota(jnp.int32, (tokens, group), 1) // HEAD_DIM
    sent = []
    for i in range(4):
        own = slice(i * tokens, (i + 1) * tokens)
        reach = (i + 1) * tokens

        @pl.loop(0, group // HEAD_DIM)
        def _(h):
            query = jnp.where(head_of == h, proj[own, :group] * (HEAD_DIM**-0.5), 0).astype(proj.dtype)
            scores = times_transposed(query, proj[:reach, group : 2 * group])
            column = lax.broadcasted_iota(jnp.int32, scores.shape, 1)
            row = lax.broadcasted_iota(jnp.int32, scores.shape, 0) + i * tokens
            scores = jnp.where((column <= row) & (column < length[0]), scores, MASKED)
            top = jnp.max(scores, axis=1, keepdims=True)
            powers = jnp.exp(scores - top)
            total = jnp.sum(powers, axis=1, keepdims=True)
            probs = (powers * (1.0 / total)).astype(proj.dtype)
            out = times(probs, proj[:reach, 2 * group :])
            acc[...] = jnp.where(head_of == h, out, acc[...])
            lane = lax.broadcasted_iota(jnp.int32, stat.shape, 1)
            stat[...] = jnp.where(lane == h, top + jnp.log(total), stat[...])

        attended[own, :] = acc[...].astype(attended.dtype)
        sums[:, own] = jnp.transpose(stat[...])[:8]
        target = mixed.at[:, pl.ds(pl.multiple_of(me * group, group), group)]

        @pl.when(me != i)
        def _():
            remote("seq", i, attended.at[own], target, x_send.at[i], x_recv.at[me])

        @pl.when(me == i)
        def _():
            pltpu.make_async_copy(attended.at[own], target, local.at[10]).start()

        if i == 0:
            up_relay(0)
            relay("mix", mix_views, m_send, m_recv)
        elif i < chips:
            up_relay(i)
        if i + 1 < chips:
            up_out(i + 1)
    for k in range(4, chips):
        up_relay(k)
        if k + 1 < chips:
            up_out(k + 1)
    attended_kept = keep(attended, attended_out, 11)
    sums_kept = keep(sums, sums_out, 12)
    arrived("mix")
    for k in range(chips):
        arrived(("up", k))
    for i in range(4):
        target = mixed.at[:, pl.ds(i * group, group)]

        @pl.when(me != i)
        def _():
            copy = pltpu.make_async_remote_copy(
                attended.at[pl.ds(i * tokens, tokens)], target, x_send.at[i], x_recv.at[i],
                device_id={"seq": i}, device_id_type=MESH,
            )
            copy.wait()

        @pl.when(me == i)
        def _():
            pltpu.make_async_copy(attended.at[pl.ds(i * tokens, tokens)], target, local.at[10]).wait()

    for copy in (*direct.values(), *exchanged, *smalls, *away.values(), *near.values(), *moved.values()):
        copy.wait_send()
    for copy in (small_kept, normed_kept, heads_kept, projected_kept, attended_kept, sums_kept):
        copy.wait()


def front(hidden, heads, mix, small, rows, lengths, experts_all, number):
    S, dma, low = jax.ShapeDtypeStruct, pltpu.SemaphoreType.DMA, jnp.bfloat16
    count, _, cap, width = rows.shape
    chips = count // 2
    tokens = hidden.shape[0]
    group = heads.shape[2] // 3
    full = 4 * tokens
    all_heads = (4, count, *heads.shape[1:])
    return pl.pallas_call(
        functools.partial(front_kernel, count, cap, experts_all),
        out_shape=(
            S((full, width), low),
            S(all_heads, low),
            S((width, mix.shape[1]), low),
            S((width, small.shape[1]), low),
            S((2, 4 * count * cap, width), low),
            S((full, 3 * group), low),
            S((full, group), low),
            S((8, full), jnp.float32),
            S((tokens, width), low),
        ),
        in_specs=[ANY] * 5 + [pl.BlockSpec(memory_space=pltpu.SMEM)],
        out_specs=(ANY,) * 9,
        scratch_shapes=[
            pltpu.VMEM(heads.shape, low),
            pltpu.VMEM((full, width), low),
            pltpu.VMEM(all_heads, low),
            pltpu.VMEM((width, small.shape[1]), low),
            pltpu.VMEM((full, width), low),
            pltpu.VMEM((full, 3 * group), low),
            pltpu.VMEM((full, group), low),
            pltpu.VMEM((8, full), jnp.float32),
            pltpu.VMEM((tokens, group), jnp.float32),
            pltpu.VMEM((tokens, 128), jnp.float32),
            dma((3, 2)), dma((3, 2)), dma((6,)), dma((6,)),
            dma((3, chips)), dma((3, chips)), dma((3, chips)), dma((3, chips)),
            dma((chips, 2)), dma((chips, 2)), dma((3, 2)), dma((3, 2)),
            dma((chips, 3, 2)), dma((chips, 3, 2)), dma((4,)), dma((4,)), dma((13,)),
        ],
        compiler_params=pltpu.CompilerParams(
            collective_id=number, has_side_effects=True, vmem_limit_bytes=48 * 2**20
        ),
    )(hidden, heads, mix, small, rows, lengths)


def back_kernel(
    count, gain_row, grad_in, proj_in, attended_in, sums_in, normed_in, heads_in, mix_in, small_in, length,
    normed_out, heads_out, mix_out, small_out,
    grads, proj, attended, sums, normed, heads, mix, small, grad_heads, delta, masked_grad, masked_query,
    masked_key, masked_value, probs, slopes, grad_query, grad_key, grad_value, grad_proj, part, weights, weights_mix, gain_sum,
    sib_a, sib_b, sib_c, own_a, own_b, own_c, got_a, got_b, got_c, total_a, total_b, total_c, first, second,
    g_send, g_recv, b_send, b_recv, bb_send, bb_recv, z_send, z_recv, x_send, x_recv, c_send, c_recv, load, keep,
):
    me, place = lax.axis_index("seq"), lax.axis_index("fsdp")
    one, two, both = me ^ 1, me ^ 2, me ^ 3
    others = (one, two, both)
    chips = count // 2
    chip, core = place // 2, lax.rem(place, 2)
    sibling = place ^ 1
    tokens, width = grad_in.shape
    group = attended.shape[1]
    share = weights.shape[0] // (4 * count)
    heads_local = group // HEAD_DIM
    low = grads.dtype
    barrier = pltpu.get_barrier_semaphore()
    for peer in others:
        pl.semaphore_signal(barrier, inc=1, device_id={"seq": peer}, device_id_type=MESH)
    for k in range(1, chips):
        pl.semaphore_signal(
            barrier, inc=1, device_id={"fsdp": (chip ^ k) * 2 + core}, device_id_type=MESH
        )
    pl.semaphore_signal(barrier, inc=1, device_id={"fsdp": sibling}, device_id_type=MESH)
    pl.semaphore_wait(barrier, 3 + chips)

    def local(source, to, sem):
        copy = pltpu.make_async_copy(source, to, sem)
        copy.start()
        return copy

    own_grad = local(grad_in, grads.at[pl.ds(me * tokens, tokens)], load.at[0])
    half = tokens // 2
    direct = {}
    for side, peer in enumerate((one, two)):
        for order in range(2):
            p = (order + side) % 2
            direct[side, p] = remote(
                "seq", peer, grad_in.at[pl.ds(p * half, half)], grads.at[pl.ds(me * tokens + p * half, half)],
                g_send.at[side, p], g_recv.at[side, p],
            )
    loads = [
        local(source, to, load.at[1 + i])
        for i, (source, to) in enumerate(
            (
                (proj_in, proj),
                (attended_in, attended),
                (sums_in, sums),
                (mix_in, mix),
                (heads_in, heads),
                (normed_in, normed),
                (small_in, small),
            )
        )
    ]
    for side, (origin, peer) in enumerate(((one, two), (two, one))):
        direct[side, side].wait_recv()
        block = grads.at[pl.ds(origin * tokens + side * half, half)]
        direct[2, side] = remote("seq", peer, block, block, g_send.at[2, side], g_recv.at[2, side])
    for copy in loads:
        copy.wait()
    head_of = lax.broadcasted_iota(jnp.int32, (tokens, group), 1) // HEAD_DIM
    for i in range(4):
        rows = slice(i * tokens, (i + 1) * tokens)
        for h in range(heads_local):
            masked_query[i, h * tokens : (h + 1) * tokens, :] = jnp.where(head_of == h, proj[rows, :group], 0).astype(low)
    own_grad.wait()
    for side in range(2):
        direct[side, 1 - side].wait_recv()
        direct[2, side].wait_recv()

    for n in range(width // TILE):
        lanes = slice(n * TILE, (n + 1) * TILE)
        weights_mix[:, lanes] = transposed_times(attended[...], grads[:, lanes]).astype(low)
    order_of = [*range(1, chips), 0]
    to_sibling, away = {}, {}

    def rows_at(s, owner):
        return pl.ds(pl.multiple_of((s * count + owner) * share, share), share)

    def start_sibling(a, k, core_of):
        owner = (chip ^ k) * 2 + core_of
        if a == 1:
            return [
                remote(
                    "fsdp", sibling, weights_mix.at[pl.ds(pl.multiple_of(owner * share, share), share)], sib_b.at[k],
                    b_send.at[0, k], b_recv.at[0, k],
                )
            ]
        if a == 2:
            return [
                remote(
                    "fsdp", sibling, small.at[:, owner * share // 128], sib_c.at[k], b_send.at[1, k], b_recv.at[1, k]
                )
            ]
        return [
            remote(
                "fsdp", sibling, weights.at[rows_at(s, owner)], sib_a.at[k, pl.ds(s * share, share)],
                bb_send.at[s, k], bb_recv.at[s, k],
            )
            for s in range(4)
        ]

    sib, own, got = (sib_a, sib_b, sib_c), (own_a, own_b, own_c), (got_a, got_b, got_c)
    totals = (total_a, total_b, total_c)

    def pair_sum(a, k):
        owner = (chip ^ k) * 2 + core
        for copy in to_sibling[a, k]:
            copy.wait_recv()
        if a == 0:
            for s in range(4):
                rows = slice(s * share, (s + 1) * share)
                own_a[k, rows, :] = (
                    weights[rows_at(s, owner), :].astype(jnp.float32) + sib_a[k, rows, :].astype(jnp.float32)
                ).astype(low)
        elif a == 1:
            mine = weights_mix[pl.ds(pl.multiple_of(owner * share, share), share), :]
            own_b[k] = (mine.astype(jnp.float32) + sib_b[k].astype(jnp.float32)).astype(low)
        else:
            for s in range(4):
                own_c[k, s] = small[s, owner * share // 128] + sib_c[k, s]
        if k:
            away[a, k] = remote(
                "fsdp", (chip ^ k) * 2 + core, own[a].at[k], got[a].at[k], z_send.at[a, k], z_recv.at[a, k]
            )

    for k in order_of:
        to_sibling[1, k] = start_sibling(1, k, core ^ 1)
    for i in range(4):
        rows = slice(i * tokens, (i + 1) * tokens)
        out = times_transposed(grads[rows, :], mix[...])
        grad_heads[rows, :] = out.astype(low)
        out = grad_heads[rows, :].astype(jnp.float32)
        turned = jnp.transpose(out * attended[rows, :].astype(jnp.float32))
        for h in range(heads_local):
            delta[h : h + 1, rows] = jnp.sum(turned[h * HEAD_DIM : (h + 1) * HEAD_DIM], axis=0, keepdims=True)
            masked_grad[i, h * tokens : (h + 1) * tokens, :] = jnp.where(head_of == h, out, 0).astype(low)
    for k in order_of:
        pair_sum(1, k)

    grad_query[...] = jnp.zeros_like(grad_query)
    gain_sum[...] = jnp.zeros_like(gain_sum)
    for j in range(4):
        own_rows = slice(j * tokens, (j + 1) * tokens)
        for h in range(heads_local):
            key = proj[own_rows, group : 2 * group]
            masked_key[h] = jnp.where(head_of == h, key * (HEAD_DIM**-0.5), 0).astype(low)
            masked_value[h] = jnp.where(head_of == h, proj[own_rows, 2 * group :], 0).astype(low)
        grad_key[...] = jnp.zeros_like(grad_key)
        grad_value[...] = jnp.zeros_like(grad_value)
        key_at = lax.broadcasted_iota(jnp.int32, (tokens, tokens), 0)
        outside = j * tokens + key_at >= length[0]

        def block(i, masked):
            rows = pl.ds(pl.multiple_of(i * tokens, tokens), tokens)
            hidden = outside
            if masked:
                hidden = hidden | (key_at > lax.broadcasted_iota(jnp.int32, (tokens, tokens), 1))
            total = None
            for h in range(heads_local):
                lanes = slice(h * tokens, (h + 1) * tokens)
                scores = times_transposed(masked_key[h], proj[rows, :group])
                scores = jnp.where(hidden, MASKED, scores)
                p = jnp.exp(scores - sums[h : h + 1, rows])
                probs[:, lanes] = p.astype(low)
                grad = times_transposed(masked_value[h], grad_heads[rows, :])
                slopes[:, lanes] = (p * (grad - delta[h : h + 1, rows])).astype(low)
                term = transposed_times(slopes[:, lanes], masked_key[h])
                total = term if total is None else total + term
            grad_query[rows, :] += total
            grad_value[...] += times(probs[...], masked_grad[i])
            grad_key[...] += times(slopes[...], masked_query[i])

        block(j, True)
        if j < 3:

            @pl.loop(j + 1, 4)
            def _(i):
                block(i, False)

        grad_proj[own_rows, :group] = grad_query[own_rows, :].astype(low)
        grad_proj[own_rows, group : 2 * group] = (grad_key[...] * (HEAD_DIM**-0.5)).astype(low)
        grad_proj[own_rows, 2 * group :] = grad_value[...].astype(low)
        for n in range(width // TILE):
            lanes = slice(n * TILE, (n + 1) * TILE)
            back = times_transposed(grad_proj[own_rows, :], heads[lanes, :])
            gain_sum[:, lanes] += jnp.sum(back * normed[own_rows, lanes].astype(jnp.float32), axis=0, keepdims=True)
            part[j, :, lanes] = back.astype(low)
    summed = {}
    for side, (near, rest) in enumerate(((one, two), (two, one))):
        rows = pl.ds(side * half, half)
        for order, to in enumerate((both, near)):
            summed[side, order] = remote(
                "seq", near, part.at[to, rows], first.at[side, order], c_send.at[side, order], c_recv.at[side, order]
            )
    for b in range(width // 128):
        small[b // 2, b % 2, gain_row : gain_row + 1, :] = gain_sum[:, b * 128 : (b + 1) * 128]
    for s in range(4):
        lanes = slice(s * group, (s + 1) * group)
        weights[lanes, :] = transposed_times(normed[:, lanes], grad_proj[...]).astype(low)
    for k in order_of:
        to_sibling[0, k] = start_sibling(0, k, core ^ 1)
        to_sibling[2, k] = start_sibling(2, k, core ^ 1)
    for k in order_of:
        pair_sum(0, k)
        pair_sum(2, k)
    for side, rest in enumerate((two, one)):
        rows = slice(side * half, (side + 1) * half)
        summed[side, 0].wait_recv()
        first[side, 0] = (first[side, 0].astype(jnp.float32) + part[rest, rows, :].astype(jnp.float32)).astype(low)
        summed[side, 2] = remote("seq", rest, first.at[side, 0], second.at[side], c_send.at[2, side], c_recv.at[2, side])
    stored = []
    for side in range(2):
        rows = slice(side * half, (side + 1) * half)
        summed[side, 1].wait_recv()
        summed[side, 2].wait_recv()
        first[side, 1] = (
            part[me, rows, :].astype(jnp.float32)
            + first[side, 1].astype(jnp.float32)
            + second[side].astype(jnp.float32)
        ).astype(low)
        stored.append(local(first.at[side, 1], normed_out.at[pl.ds(side * half, half)], keep.at[side]))
    for a in (1, 0, 2):
        total = own[a][0].astype(jnp.float32)
        for k in range(1, chips):
            away[a, k].wait_recv()
            total = total + got[a][k].astype(jnp.float32)
        if a == 0:
            for s in range(4):
                total_a[s] = total[s * share : (s + 1) * share].astype(low)
        else:
            totals[a][...] = total
    crossed = []
    for a, out in ((0, heads_out), (2, small_out)):
        for i, peer in enumerate(others):
            crossed.append(remote("seq", peer, totals[a].at[peer], out.at[me], x_send.at[a, i], x_recv.at[a, i]))
        stored.append(local(totals[a].at[me], out.at[me], keep.at[3 + a // 2]))
    stored.append(local(total_b, mix_out, keep.at[2]))
    for copy in (*stored, *crossed):
        copy.wait()
    for copy in (*summed.values(), *away.values(), *direct.values()):
        copy.wait_send()
    for copies in to_sibling.values():
        for copy in copies:
            copy.wait_send()


def back(grad, proj, attended, sums, normed, heads, mix, small, lengths, count, gain_row, number):
    S, dma, f32, low = jax.ShapeDtypeStruct, pltpu.SemaphoreType.DMA, jnp.float32, jnp.bfloat16
    tokens, width = grad.shape
    group = attended.shape[1]
    chips = count // 2
    full = 4 * tokens
    share = width // (4 * count)
    local_heads = group // HEAD_DIM
    kinds = small.shape[2]

    def vmem(*shape, dtype=low):
        return pltpu.VMEM(shape, dtype)

    sets = [
        vmem(chips, 4 * share, 3 * group),
        vmem(chips, share, width),
        vmem(chips, 4, kinds, 128, dtype=f32),
    ]
    return pl.pallas_call(
        functools.partial(back_kernel, count, gain_row),
        out_shape=(
            S((tokens, width), low),
            S((4, share, 3 * group), low),
            S((share, width), f32),
            S((4, kinds, 128), f32),
        ),
        in_specs=[ANY] * 8 + [pl.BlockSpec(memory_space=pltpu.SMEM)],
        out_specs=(ANY,) * 4,
        scratch_shapes=[
            vmem(full, width),
            vmem(*proj.shape),
            vmem(*attended.shape),
            vmem(*sums.shape, dtype=f32),
            vmem(*normed.shape),
            vmem(*heads.shape),
            vmem(*mix.shape),
            vmem(*small.shape, dtype=f32),
            vmem(full, group),
            vmem(8, full, dtype=f32),
            vmem(4, local_heads * tokens, group),
            vmem(4, local_heads * tokens, group),
            vmem(local_heads, tokens, group),
            vmem(local_heads, tokens, group),
            vmem(tokens, local_heads * tokens),
            vmem(tokens, local_heads * tokens),
            vmem(full, group, dtype=f32),
            vmem(tokens, group, dtype=f32),
            vmem(tokens, group, dtype=f32),
            vmem(full, 3 * group),
            vmem(4, tokens, width),
            vmem(width, 3 * group),
            vmem(group, width),
            vmem(1, width, dtype=f32),
            *sets,
            *sets,
            *sets,
            vmem(4, share, 3 * group),
            vmem(share, width, dtype=f32),
            vmem(4, kinds, 128, dtype=f32),
            vmem(2, 2, tokens // 2, width),
            vmem(2, tokens // 2, width),
            dma((3, 2)), dma((3, 2)),
            dma((2, chips)), dma((2, chips)), dma((4, chips)), dma((4, chips)),
            dma((3, chips)), dma((3, chips)),
            dma((3, 3)), dma((3, 3)), dma((3, 2)), dma((3, 2)), dma((8,)), dma((5,)),
        ],
        compiler_params=pltpu.CompilerParams(
            collective_id=number, has_side_effects=True, vmem_limit_bytes=56 * 2**20
        ),
    )(grad, proj, attended, sums, normed, heads, mix, small, lengths)


def shards(
    hidden,
    lengths,
    expert_ids,
    attn_gain,
    qkv_weight,
    out_weight,
    moe_gain,
    router_weight,
    expert_in,
    expert_out,
    out_grad,
):
    S = jax.ShapeDtypeStruct
    low = jnp.bfloat16
    owners = lax.axis_size("fsdp")
    seq_place = lax.axis_index("seq")
    seq_count = lax.axis_size("seq")
    tokens, width = hidden.shape[1], hidden.shape[2]
    full_len = tokens * seq_count
    group_width = width // seq_count
    rows_own = qkv_weight.shape[0]
    length = lengths[0]
    experts_all = router_weight.shape[1]
    small = jnp.concatenate([router_weight, attn_gain[:, None], moe_gain[:, None]], axis=1)
    small = jnp.pad(small, ((0, 0), (0, -small.shape[1] % 128)))
    expert_local = expert_in.shape[0]
    capacity = -(-max(2, 2 * tokens // experts_all) // 16) * 16
    slots = experts_all * capacity

    position = seq_place * tokens + jnp.arange(tokens, dtype=jnp.int32)
    valid = (position < length).astype(jnp.float32)[:, None]
    chosen = expert_ids[0, :, 0]
    choose = chosen[:, None] == jnp.arange(experts_all, dtype=jnp.int32)[None, :]
    order = jnp.arange(tokens, dtype=jnp.int32)
    earlier = (order[None, :] < order[:, None]) & (chosen[None, :] == chosen[:, None])
    ranks = jnp.sum(earlier.astype(jnp.int32), axis=1)
    slot = chosen * capacity + ranks
    hit = jnp.arange(slots, dtype=jnp.int32)[:, None] == slot[None, :]
    dispatch = hit.astype(low)

    def to_owners(rows, number):
        return exchange(
            "fsdp",
            owners,
            (rows.reshape(owners, expert_local, capacity, width),),
            (S((expert_local, owners, capacity, width), low),),
            ((lead, second),),
            number,
        )[0].reshape(expert_local, owners * capacity, width)

    def to_sources(rows, number):
        return exchange(
            "fsdp",
            owners,
            (rows.reshape(expert_local, owners, capacity, width),),
            (S((owners, expert_local, capacity, width), low),),
            ((second, lead),),
            number,
        )[0].reshape(slots, width)

    upstream_low = jnp.where(valid > 0, out_grad[0], 0).astype(low)
    upstream = upstream_low.astype(jnp.float32)
    up_rows = times(dispatch, upstream_low).astype(low)
    normed, weight_qkv, weight_mix, small, up_all, projected, attended, totals, mixed = front(
        hidden[0],
        qkv_weight.reshape(rows_own, 3, seq_count, group_width)
        .transpose(2, 0, 1, 3)
        .reshape(seq_count, rows_own, 3 * group_width),
        out_weight,
        small,
        up_rows.reshape(owners, expert_local, capacity, width),
        lengths,
        experts_all,
        0,
    )
    weight_qkv = weight_qkv.reshape(width, 3 * group_width)
    weight_route = small[:, :experts_all]
    gain_one = small[:, experts_all].astype(jnp.float32)
    gain_two = small[:, experts_all + 1].astype(jnp.float32)
    mix_rows = lax.dynamic_slice_in_dim(weight_mix, seq_place * group_width, group_width, 0)
    fused = 4 * owners * capacity <= 1024
    if not fused:
        up_all = up_all.reshape(expert_local, owners // 2, seq_count, 2 * capacity, width)
        up_all = jnp.roll(up_all, lax.axis_index("fsdp") // 2, axis=1)
        up_all = up_all.transpose(0, 2, 1, 3, 4)
    inputs = hidden[0].astype(jnp.float32)
    middle = inputs + times(mixed, weight_mix)
    normed_two, norm_two_back = jax.vjp(scaled_norm, middle, gain_two)
    normed_two = normed_two.astype(low)
    logits = times(normed_two, weight_route)

    def gate_of(logit_rows):
        return jnp.sum(jnp.where(choose, jax.nn.softmax(logit_rows, axis=-1), 0.0), axis=-1)

    gate, gate_back = jax.vjp(gate_of, logits)
    sent = times(dispatch, normed_two).astype(low)
    if fused:
        (returned, grad_back), expert_in_grad, expert_out_grad = moe(
            sent.reshape(owners, expert_local, capacity, width),
            up_all,
            small,
            expert_in,
            expert_out,
            experts_all,
            5,
        )
        returned, grad_back = returned.reshape(slots, width), grad_back.reshape(slots, width)
    else:
        gate_rows = jnp.sum(jnp.where(hit, gate[None, :], 0.0), axis=1)
        gates = lax.all_to_all(
            gate_rows.reshape(owners, expert_local, capacity), "fsdp", split_axis=0, concat_axis=0, tiled=True
        )
        gates = lax.all_gather(gates, "seq", axis=0)
        gates = gates.transpose(2, 0, 1, 3).reshape(expert_local, seq_count * owners * capacity, 1)

        rows_all = spread(to_owners(sent, 5), 6)
        count = seq_count * owners * capacity
        rows_all = rows_all.reshape(expert_local, count, width)
        up_all = up_all.reshape(expert_local, count, width)
        grad_rows = (up_all.astype(jnp.float32) * gates).astype(low)

        def per_expert(form, left, right):
            return jnp.einsum(form, left, right, preferred_element_type=jnp.float32)

        inner = per_expert("jrd,jdf->jrf", rows_all, expert_in)
        active, active_back = jax.vjp(gelu_tanh, inner)
        active = active.astype(low)
        partial_out = per_expert("jrf,jfd->jrd", active, expert_out).astype(low)
        grad_active = per_expert("jrd,jfd->jrf", grad_rows, expert_out)
        grad_inner = active_back(grad_active)[0].astype(low)
        partial_back = per_expert("jrf,jdf->jrd", grad_inner, expert_in).astype(low)
        expert_out_grad = per_expert("jrf,jrd->jfd", active, grad_rows)
        expert_in_grad = per_expert("jrd,jrf->jdf", rows_all, grad_inner)

        shape = (expert_local, seq_count, owners * capacity, width)
        returned = to_sources(collect(partial_out.reshape(shape), 7), 8)
        grad_back = to_sources(collect(partial_back.reshape(shape), 9), 10)

    back_rows = transposed_times(dispatch, returned)
    output = valid * (middle + gate[:, None] * back_rows)
    grad_gate = jnp.sum(upstream * back_rows, axis=1)
    grad_logits = gate_back(grad_gate)[0].astype(low)
    grad_normed_two = times_transposed(grad_logits, weight_route) + transposed_times(dispatch, grad_back)
    grad_middle, grad_gain_two = norm_two_back(grad_normed_two)
    grad_middle = grad_middle + upstream
    grad_attn = grad_middle.astype(low)

    small_grad = jnp.concatenate([transposed_times(grad_logits, normed_two), jnp.zeros((1, width)), grad_gain_two[None]])
    small_grad = jnp.pad(small_grad, ((0, -small_grad.shape[0] % 8), (0, 0)))
    kinds = small_grad.shape[0]
    small_grad = small_grad.reshape(kinds, seq_count, group_width // 128, 128).transpose(1, 2, 0, 3)
    grad_normed, qkv_sum, mix_grad, small_sum = back(
        grad_attn,
        projected,
        attended,
        totals,
        normed,
        weight_qkv,
        mix_rows,
        small_grad,
        lengths,
        owners,
        experts_all,
        12,
    )
    qkv_weight_grad = (
        qkv_sum.astype(jnp.float32)
        .reshape(seq_count, rows_own, 3, group_width)
        .transpose(1, 2, 0, 3)
        .reshape(rows_own, 3 * width)
    )
    start = lax.axis_index("fsdp") * rows_own % 128
    small_sum = lax.dynamic_slice_in_dim(jnp.sum(small_sum, axis=0), start, rows_own, 1)
    _, norm_back = jax.vjp(scaled_norm, inputs, gain_one)
    grad_inputs = norm_back(grad_normed.astype(jnp.float32))[0] + grad_middle
    return (
        output.astype(low)[None],
        grad_inputs[None],
        small_sum[experts_all] / attn_gain.astype(jnp.float32),
        qkv_weight_grad,
        mix_grad,
        small_sum[experts_all + 1],
        small_sum[:experts_all].T,
        expert_in_grad,
        expert_out_grad,
    )


def solution(mesh):
    placed = (
        P("fsdp", "seq", None),
        P("fsdp"),
        P("fsdp", "seq", None),
        P(("seq", "fsdp")),
        P(("seq", "fsdp"), None),
        P(("seq", "fsdp"), None),
        P(("seq", "fsdp")),
        P(("seq", "fsdp"), None),
        P("fsdp", None, "seq"),
        P("fsdp", "seq", None),
        P("fsdp", "seq", None),
    )
    return jax.shard_map(
        shards,
        mesh=mesh,
        in_specs=placed,
        out_specs=(
            P("fsdp", "seq", None),
            P("fsdp", "seq", None),
            P(("seq", "fsdp")),
            P(("seq", "fsdp"), None),
            P(("seq", "fsdp"), None),
            P(("seq", "fsdp")),
            P(("seq", "fsdp"), None),
            P("fsdp", None, "seq"),
            P("fsdp", "seq", None),
        ),
        check_vma=False,
    )
```

profile of v0, /device:TPU:0, one launch (start us, length us, event | category | flops | bytes accessed | tf_op | source)
XLA Modules:
  0.0 364.5 jit_solution(15982954103689207995)
XLA Ops:
  0.6 0.0 copy-start
  0.7 0.0 copy-start.5
  1.4 0.1 pad.11.clone
  1.5 0.9 convert_reduce_fusion.2
  2.4 0.7 multiply_add_fusion.2
  3.1 0.7 copy.39
  3.8 0.8 copy.37
  4.6 0.8 copy.38
  5.4 0.1 fusion.26.small
  5.4 1.1 reshape.130
  6.5 0.1 copy.44
  6.6 0.2 reshape.131.heads
  6.8 1.6 convolution_convert_fusion.1
  8.4 0.0 copy-done
  8.4 0.0 copy-done.5
  8.4 90.8 %shard_map.178 = (bf16[1024,1024]{1,0:T(8,128)(2,1)}, bf16[4,8,32,768]{3,2,1,0:T(8,128)(2,1)S(1)}, bf16[1024,1024]{1,0:T(8,128)(2,1)}, bf16[1024,128]{1,0:T(8,12...) custom-call(bf16[256,1024]{1,0:T(8,128)(2,1)S(1)} %bitcast.51, ...), custom_call_target="tpu_custom_call" | custom-call | tf_op jit(solution)/shard_map/pallas_call | solution.py:786
  99.3 0.0 copy-start.3
  99.3 0.0 copy-start.4
  99.3 0.0 copy-start.6
  99.3 0.0 copy-start.1
  99.3 0.4 convert_reduce_fusion
  99.7 2.3 constant_dynamic-slice_fusion.mix_in
  102.0 2.4 multiply_reduce_fusion.2
  104.3 0.0 copy-done.3
  104.4 0.0 copy-done.4
  104.4 0.0 copy-done.6
  104.4 0.2 multiply_convert_fusion.1
  104.6 0.0 copy-done.1
  104.6 0.3 fusion.35
  104.9 1.4 convolution_convert_fusion
  106.3 161.9 %shard_map.179 = (bf16[2,8,2,32,1024]{4,3,2,1,0:T(8,128)(2,1)}, f32[2,1024,1024]{2,1,0:T(8,128)}, f32[2,1024,1024]{2,1,0:T(8,128)}) custom-call(bf16[8,2,32,1024]{3,2,1,0:T(8,128)(2,1)} %bitcast.58, bf16[2,1024,1024]{2,1,0:T(8,128)(2,1)} %get-tuple-element.28.up_rows, bf16[1024,128]{1,0:T(8,128)(2,1)} %copy-done.1, bf16[2,1024,1024]{2,1,0:T(8,128)(2,1)} %w_in.1, ...), custom_call_target="tpu_custom_call" | custom-call | flops 25769803776 | bytes 33554432 | tf_op jit(solution)/shard_map/pallas_call | solution.py:486
  268.2 0.0 copy-start.7
  268.2 1.8 fusion.34
  270.0 0.0 copy-start.10
  270.0 0.0 copy-start.2
  270.0 0.0 copy-done.7
  270.0 0.6 fusion
  270.6 0.1 copy-done.10
  270.7 0.2 fusion.30
  270.9 0.1 copy-done.2
  270.9 0.3 fusion.12
  271.3 0.7 multiply_reduce_fusion
  272.0 1.5 fusion.33
  273.5 0.1 pad_maximum_fusion
  273.6 0.1 reshape.136
  273.6 0.7 copy.45
  274.3 0.0 copy-start.11
  274.3 64.6 %shard_map.180 = (bf16[256,1024]{1,0:T(8,128)(2,1)}, bf16[4,32,768]{2,1,0:T(8,128)(2,1)}, f32[32,1024]{1,0:T(8,128)}, f32[4,24,128]{2,1,0:T(8,128)}) custom-call(bf16[256,1024]{1,0:T(8,128)(2,1)} %get-tuple-element.49.grad_in, bf16[1024,768]{1,0:T(8,128)(2,1)} %get-tuple-element.30.proj_in, bf16[1024,256]{1,0:T(8,128)(2,1)} %copy-done.4, ...), custom_call_target="tpu_custom_call" | custom-call | tf_op jit(solution)/shard_map/pallas_call | solution.py:1092
  338.9 0.8 reduce_sum.125
  339.8 0.6 dynamic-slice_bitcast_fusion.1
  340.3 0.0 copy-done.11
  340.3 0.6 fusion.29
  340.9 0.7 dynamic-slice_bitcast_fusion
  341.6 1.4 fusion.3
  343.0 0.0 copy-start.9
  343.0 2.4 fusion.2
  345.4 0.0 copy-done.8
  345.4 0.2 reshape.146
  345.6 0.3 copy.41
  345.9 0.9 reshape.143
  346.8 0.0 copy-done.9
  346.8 0.7 copy.50
  347.5 8.4 %copy.51 = f32[2,1024,1024]{2,1,0:T(8,128)} copy(f32[2,1024,1024]{2,1,0:T(8,128)} %get-tuple-element.81) | data formatting | bytes 16777216
  355.9 8.4 %copy.52 = f32[2,1024,1024]{2,1,0:T(8,128)} copy(f32[2,1024,1024]{2,1,0:T(8,128)} %get-tuple-element.82) | data formatting | bytes 16777216
  (10 shorter events, 0.1 us)
Async XLA Ops:
  0.6 7.8 %copy-start = (bf16[1,256,1024]{2,1,0:T(8,128)(2,1)S(1)}, bf16[1,256,1024]{2,1,0:T(8,128)(2,1)}, u32[]{:S(2)}) copy-start(bf16[1,256,1024]{2,1,0:T(8,128)(2,1)} %param.11) | copy-start | bytes 1572868
  0.7 7.8 %copy-start.5 = (bf16[32,1024]{1,0:T(8,128)(2,1)S(1)}, bf16[32,1024]{1,0:T(8,128)(2,1)}, u32[]{:S(2)}) copy-start(bf16[32,1024]{1,0:T(8,128)(2,1)} %mix.1) | copy-start | bytes 196612
  99.3 5.1 %copy-start.3 = (bf16[4,8,32,768]{3,2,1,0:T(8,128)(2,1)}, bf16[4,8,32,768]{3,2,1,0:T(8,128)(2,1)S(1)}, u32[]{:S(2)}) copy-start(bf16[4,8,32,768]{3,2,1,0:T(8,128)(2,1)S(1)} %get-tuple-element.34) | copy-start | bytes 4718596
  99.3 5.1 %copy-start.4 = (bf16[1024,256]{1,0:T(8,128)(2,1)}, bf16[1024,256]{1,0:T(8,128)(2,1)S(1)}, u32[]{:S(2)}) copy-start(bf16[1024,256]{1,0:T(8,128)(2,1)S(1)} %get-tuple-element.31.attended_in) | copy-start | bytes 1572868
  99.3 5.1 %copy-start.6 = (f32[8,1024]{1,0:T(8,128)}, f32[8,1024]{1,0:T(8,128)S(1)}, u32[]{:S(2)}) copy-start(f32[8,1024]{1,0:T(8,128)S(1)} %get-tuple-element.32.sums_in) | copy-start | bytes 98308
  99.3 5.2 %copy-start.1 = (bf16[1024,128]{1,0:T(8,128)(2,1)}, bf16[1024,128]{1,0:T(8,128)(2,1)S(1)}, u32[]{:S(2)}) copy-start(bf16[1024,128]{1,0:T(8,128)(2,1)S(1)} %get-tuple-element.27.route) | copy-start | bytes 786436
  268.2 1.8 copy-start.7
  270.0 0.7 copy-start.10
  270.0 1.0 copy-start.2
  274.3 66.0 %copy-start.11 = (bf16[32]{0:T(256)(128)(2,1)S(1)}, bf16[32]{0:T(256)(128)(2,1)}, u32[]{:S(2)}) copy-start(bf16[32]{0:T(256)(128)(2,1)} %param.14) | copy-start | bytes 196
  341.6 3.8 %copy-start.8 = (bf16[4,32,768]{2,1,0:T(8,128)(2,1)S(1)}, bf16[4,32,768]{2,1,0:T(8,128)(2,1)}, u32[]{:S(2)}) copy-start(bf16[4,32,768]{2,1,0:T(8,128)(2,1)} %get-tuple-element.37) | copy-start | bytes 589828
  343.0 3.8 %copy-start.9 = (f32[32,1024]{1,0:T(8,128)S(1)}, f32[32,1024]{1,0:T(8,128)}, u32[]{:S(2)}) copy-start(f32[32,1024]{1,0:T(8,128)} %get-tuple-element.78) | copy-start | bytes 393220
where the time goes:
time: 371 us; the launch traced here: 365 us
  Pallas kernels  317 us (85%)
  local copies, waits for them, and re-layouts  28.9 us (8%)
  other arithmetic  9.03 us (2%)
  matrix products  7.45 us (2%)
    pallas_call x1, Pallas kernels, moe(): pl.pallas_call(functools.partial(moe_kernel, chips, cap, experts_all), ou...  162 us
    pallas_call x1, Pallas kernels, front(): pl.pallas_call(functools.partial(front_kernel, count, cap, experts_all),...  90.8 us
    pallas_call x1, Pallas kernels, back(): pl.pallas_call(functools.partial(back_kernel, count, gain_row), out_shape...  64.6 us
    unnamed x28, local copies, waits for them, and re-layouts  18.5 us

commit v1 on v0

--- a/solution.py
+++ b/solution.py
@@ -12,6 +12,7 @@
 MASKED = -1e30
 ROOT = 0.7978845608028654
 TILE = 256
+SPREAD_FIRST = 3
 GRAD = 256
 MESH = pl.DeviceIdType.MESH
 ANY = pl.BlockSpec(memory_space=pl.ANY)
@@ -249,7 +250,7 @@
 
 
 def moe_kernel(
-    chips, cap, experts_all, send_rows, up_rows, route, w_in, w_out,
+    chips, cap, experts_all, spread_first, send_rows, up_rows, route, w_in, w_out,
     ret, dw_in, dw_out,
     R, U, G, A, I, PB, first, second, W1, W2, RT, stage,
     load, own, z_send, z_recv, s_send, s_recv, y_send, y_recv,
@@ -281,51 +282,49 @@
         copy.start()
         return copy
 
-    dispatched = []
-    own_rows = None
-    for k in range(chips):
-        to = lax.rem(chip - k + chips, chips)
+    dispatched = {}
+    own_rows = []
+
+    def dispatch(k):
+        target = R.at[:, pl.ds(k * chunk + me * part + core * cap, cap)]
+        if k == 0:
+            own_rows.append(local(send_rows.at[place], target, own.at[0]))
         for c in range(2):
-            target = R.at[:, pl.ds(k * chunk + me * part + core * cap, cap)]
-            if k == 0:
-                if c == 0:
-                    own_rows = local(send_rows.at[place], target, own.at[0])
-                    dispatched.append(
-                        remote("fsdp", sibling, send_rows.at[sibling], target, z_send.at[0, 0], z_recv.at[0, 0])
-                    )
-                continue
-            peer = to * 2 + (core ^ c)
-            dispatched.append(
-                remote("fsdp", peer, send_rows.at[peer], target, z_send.at[k, c], z_recv.at[k, c])
-            )
+            if k or c:
+                peer = (chip ^ k) * 2 + (core ^ c)
+                dispatched[k, c] = remote(
+                    "fsdp", peer, send_rows.at[peer], target, z_send.at[k, c], z_recv.at[k, c]
+                )
 
     def z_arrived(k):
         if k == 0:
-            own_rows.wait()
-            dispatched[0].wait_recv()
-        else:
-            dispatched[2 * k - 1].wait_recv()
-            dispatched[2 * k].wait_recv()
+            own_rows[0].wait()
+        for c in range(2):
+            if k or c:
+                dispatched[k, c].wait_recv()
 
     sent = {}
 
-    def spread_out(k):
+    def spread_out(a, k):
         for side, peer in enumerate((one, two)):
             for order in range(2):
                 j = (order + side) % 2
-                block = R.at[j, rows_of(k, me)]
-                sent[k, side, j] = remote("seq", peer, block, block, s_send.at[k, side, j], s_recv.at[k, side, j])
-
-    def relay(k):
+                target = (U, R)[a].at[j, rows_of(k, me)]
+                source = target if a else up_rows.at[j, rows_of(k, me)]
+                sent[a, k, side, j] = remote(
+                    "seq", peer, source, target, s_send.at[a, k, side, j], s_recv.at[a, k, side, j]
+                )
+
+    def relay(a, k):
         for side, (origin, peer) in enumerate(((one, two), (two, one))):
-            sent[k, side, side].wait_recv()
-            block = R.at[side, rows_of(k, origin)]
-            sent[k, 2, side] = remote("seq", peer, block, block, y_send.at[k, side], y_recv.at[k, side])
-
-    def all_arrived(k):
+            sent[a, k, side, side].wait_recv()
+            block = (U, R)[a].at[side, rows_of(k, origin)]
+            sent[a, k, 2, side] = remote("seq", peer, block, block, y_send.at[a, k, side], y_recv.at[a, k, side])
+
+    def all_arrived(a, k):
         for side in range(2):
-            sent[k, side, 1 - side].wait_recv()
-            sent[k, 2, side].wait_recv()
+            sent[a, k, side, 1 - side].wait_recv()
+            sent[a, k, 2, side].wait_recv()
 
     def experts(k, j):
         rows = pl.ds(k * chunk, chunk)
@@ -391,7 +390,7 @@
                 + PB[a, j, rows_of(k, me), :].astype(jnp.float32)
                 + second[a, j, k].astype(jnp.float32)
             ).astype(first.dtype)
-            to = lax.rem(chip + k, chips)
+            to = chip ^ k
             target = ret.at[a, place, j]
             for c in range(2):
                 if k == 0:
@@ -411,9 +410,9 @@
 
     staged = {}
 
-    def weight_grads(j, which):
+    def weight_grads(j, which, tiles):
         left, right, out = ((R, I, dw_in), (A, G, dw_out))[which]
-        for m in range(left.shape[2] // GRAD):
+        for m in tiles:
             slot = m % 2
             lanes = slice(m * GRAD, (m + 1) * GRAD)
             if slot in staged:
@@ -422,47 +421,79 @@
             @pl.loop(0, right.shape[2] // TILE)
             def _(t):
                 cols = pl.ds(pl.multiple_of(t * TILE, TILE), TILE)
-                stage[slot, :, cols] = transposed_times(left[j, :, lanes], right[j, :, cols])
+                stage[slot, :, cols] = transposed_times(left[j, :, lanes], right[j, :, cols]).astype(stage.dtype)
 
             staged[slot] = local(stage.at[slot], out.at[j, lanes], store.at[slot])
 
+    later = range(spread_first, chips)
+    dispatch(0)
+    dispatch(1)
+    dispatch(2)
     for j in range(2):
         loads.append(local(w_in.at[j], W1.at[j], load.at[j]))
         loads.append(local(w_out.at[j], W2.at[j], load.at[2 + j]))
     loads.append(local(route, RT, load.at[4]))
-    loads.append(local(up_rows, U, load.at[5]))
+    early = spread_first * chunk
+    for j in range(2):
+        loads.append(local(up_rows.at[j, pl.ds(0, early)], U.at[j, pl.ds(0, early)], load.at[5 + j]))
+    for n, k in enumerate(later):
+        for j in range(2):
+            block = rows_of(k, me)
+            loads.append(local(up_rows.at[j, block], U.at[j, block], load.at[7 + 2 * n + j]))
     z_arrived(0)
-    spread_out(0)
+    spread_out(1, 0)
+    for k in later:
+        spread_out(0, k)
+    z_arrived(1)
+    spread_out(1, 1)
+    dispatch(3)
+    relay(1, 0)
     for copy in loads:
         copy.wait()
-    for k in range(chips):
-        relay(k)
-        if k + 1 < chips:
-            z_arrived(k + 1)
-            spread_out(k + 1)
-        all_arrived(k)
+    for k in later:
+        relay(0, k)
+    z_arrived(2)
+    spread_out(1, 2)
+    all_arrived(1, 0)
+    experts(0, 0)
+    collect_one(0, 0)
+    relay(1, 1)
+    z_arrived(3)
+    spread_out(1, 3)
+    experts(0, 1)
+    collect_one(0, 1)
+    relay(1, 2)
+    for k in range(1, chips):
+        all_arrived(1, k)
+        if k >= spread_first:
+            all_arrived(0, k)
         experts(k, 0)
         collect_one(k, 0)
-        if k:
-            collect_two(k - 1, 0)
-            collect_two(k - 1, 1)
+        if k == 1:
+            relay(1, 3)
+        collect_two(k - 1, 0)
+        if k > 1:
+            collect_three(k - 2, 0)
         experts(k, 1)
         collect_one(k, 1)
-        if k:
-            collect_three(k - 1, 0)
-            collect_three(k - 1, 1)
+        collect_two(k - 1, 1)
+        if k > 1:
+            collect_three(k - 2, 1)
     last = chips - 1
-    weight_grads(0, 0)
+    weight_grads(0, 0, range(4))
     collect_two(last, 0)
+    collect_three(last - 1, 0)
     collect_two(last, 1)
-    weight_grads(0, 1)
-    weight_grads(1, 0)
+    collect_three(last - 1, 1)
+    weight_grads(0, 1, range(4))
+    weight_grads(1, 0, range(2))
     collect_three(last, 0)
+    weight_grads(1, 0, range(2, 4))
     collect_three(last, 1)
-    weight_grads(1, 1)
+    weight_grads(1, 1, range(4))
     for copy in staged.values():
         copy.wait()
-    for copy in dispatched:
+    for copy in dispatched.values():
         copy.wait_send()
     for copy in sent.values():
         copy.wait_send()
@@ -484,11 +515,11 @@
         return pltpu.VMEM(shape, dtype)
 
     return pl.pallas_call(
-        functools.partial(moe_kernel, chips, cap, experts_all),
+        functools.partial(moe_kernel, chips, cap, experts_all, SPREAD_FIRST),
         out_shape=(
             S((2, owners, 2, cap, width), low),
-            S(w_in.shape, jnp.float32),
-            S(w_out.shape, jnp.float32),
+            S(w_in.shape, low),
+            S(w_out.shape, low),
         ),
         in_specs=[ANY] * 5,
         out_specs=(ANY,) * 3,
@@ -504,15 +535,15 @@
             vmem(*w_in.shape),
             vmem(*w_out.shape),
             vmem(*route.shape),
-            vmem(2, GRAD, max(width, hidden_units), dtype=jnp.float32),
-            dma((6,)),
+            vmem(2, GRAD, max(width, hidden_units)),
+            dma((7 + 2 * (chips - SPREAD_FIRST),)),
             dma((5,)),
             dma((chips, 2)),
             dma((chips, 2)),
-            dma((chips, 2, 2)),
-            dma((chips, 2, 2)),
-            dma((chips, 2)),
-            dma((chips, 2)),
+            dma((2, chips, 2, 2)),
+            dma((2, chips, 2, 2)),
+            dma((2, chips, 2)),
+            dma((2, chips, 2)),
             dma((2, 2, chips, 2)),
             dma((2, 2, chips, 2)),
             dma((2, 2, chips)),
@@ -531,11 +562,11 @@
 
 
 def front_kernel(
-    count, cap, experts_all, hidden, heads, mix, small, rows, length,
+    count, cap, experts_all, spread_here, hidden, heads, mix, small, rows, length,
     normed_out, heads_out, mix_all, small_out, up, projected_out, attended_out, sums_out, mixed,
     staged, hid, heads_all, small_all, normed, proj, attended, sums, acc, stat,
     h_send, h_recv, q_send, q_recv, f_send, f_recv, n_send, n_recv, u_send, u_recv, m_send, m_recv,
-    s_send, s_recv, x_send, x_recv, local,
+    s_send, s_recv, x_send, x_recv, y_send, y_recv, local,
 ):
     me, place = lax.axis_index("seq"), lax.axis_index("fsdp")
     one, two, both = me ^ 1, me ^ 2, me ^ 3
@@ -555,37 +586,37 @@
             barrier, inc=1, device_id={"fsdp": lax.rem(place + step, count)}, device_id_type=MESH
         )
     pl.semaphore_wait(barrier, 3 + count - 1)
-    finish = []
 
     def keep(source, target, number):
         copy = pltpu.make_async_copy(source, target, local.at[number])
         copy.start()
         return copy
 
-    def far(k, sign):
-        return lax.rem(chip + sign * k + chips, chips) * 2 + core
-
-    def at_rows(ref, s, owner):
-        return ref.at[pl.ds((s * count + owner) * share, share)]
-
-    gathered = ((mix, mix_all), (small, small_all))
+    def far(k):
+        return (chip ^ k) * 2 + core
+
     away, near = {}, {}
 
     def block(a, owner):
-        return heads_all.at[:, owner] if a == 2 else at_rows(gathered[a][1], me, owner)
-
-    def send_own(a):
-        source = staged if a == 2 else gathered[a][0]
+        if a == 0:
+            return mix_all.at[me, owner // 2, core]
+        if a == 1:
+            return small_all.at[pl.ds(pl.multiple_of((me * count + owner) * share, share), share)]
+        return heads_all.at[:, owner]
+
+    own_of = (mix, small, staged)
+
+    def send_far(a):
         for k in range(1, chips):
-            away[a, k] = remote(
-                "fsdp", far(k, -1), source, block(a, place), f_send.at[a, k], f_recv.at[a, k]
-            )
-        near[a, 0] = remote("fsdp", sibling, source, block(a, place), n_send.at[a, 0], n_recv.at[a, 0])
+            away[a, k] = remote("fsdp", far(k), own_of[a], block(a, place), f_send.at[a, k], f_recv.at[a, k])
+
+    def send_near(a):
+        near[a, 0] = remote("fsdp", sibling, own_of[a], block(a, place), n_send.at[a, 0], n_recv.at[a, 0])
 
     def pass_on(a):
         for k in range(1, chips):
             away[a, k].wait_recv()
-            arrived = block(a, far(k, 1))
+            arrived = block(a, far(k))
             near[a, k] = remote("fsdp", sibling, arrived, arrived, n_send.at[a, k], n_recv.at[a, k])
 
     direct = {}
@@ -609,7 +640,20 @@
             direct[name, side, 1 - side].wait_recv()
             direct[name, 2, side].wait_recv()
 
-    send_own(1)
+    moved = {}
+
+    def send_rows(k):
+        for c in range(2):
+            if k == 0 and c == 0:
+                continue
+            peer = (chip ^ k) * 2 + (core ^ c)
+            moved[k, c] = remote(
+                "fsdp", peer, rows.at[peer], up.at[:, pl.ds(k * chunk + me * part + core * cap, cap)],
+                u_send.at[k, c], u_recv.at[k, c],
+            )
+
+    send_far(1)
+    send_near(1)
     exchanged = [
         remote("seq", peer, heads.at[peer], staged.at[me], q_send.at[i], q_recv.at[i])
         for i, peer in enumerate(others)
@@ -624,28 +668,20 @@
         lambda origin, p=p: hid.at[pl.ds(origin * tokens + p * half, half)] for p in range(2)
     ]
     both_ways("hidden", hidden_views, [hidden.at[pl.ds(p * half, half)] for p in range(2)], h_send, h_recv)
-    send_own(0)
+    send_far(0)
+    send_rows(0)
     pass_on(1)
     own_heads.wait()
     for copy in exchanged:
         copy.wait_recv()
     own_block = keep(staged, heads_all.at[:, place], 5)
-    send_own(2)
+    send_far(2)
+    send_near(2)
     own_small.wait()
     for k in range(chips):
         near[1, k].wait_recv()
-    mine = small_all.at[pl.ds(me * count * share, count * share)]
+    mine = small_all.at[pl.ds(pl.multiple_of(me * count * share, share), count * share)]
     smalls = [remote("seq", peer, mine, mine, q_send.at[3 + i], q_recv.at[3 + i]) for i, peer in enumerate(others)]
-    moved = {}
-    for k in range(chips):
-        for c in range(2):
-            if k == 0 and c == 0:
-                continue
-            peer = lax.rem(chip - k + chips, chips) * 2 + (core ^ c)
-            moved[k, c] = remote(
-                "fsdp", peer, rows.at[peer], up.at[:, pl.ds(k * chunk + me * part + core * cap, cap)],
-                u_send.at[k, c], u_recv.at[k, c],
-            )
 
     def up_views(k):
         return [lambda origin, j=j: up.at[j, pl.ds(k * chunk + origin * part, part)] for j in range(2)]
@@ -656,28 +692,28 @@
         for c in range(2):
             if (k, c) in moved:
                 moved[k, c].wait_recv()
-        views = up_views(k)
-        both_ways(("up", k), views, [views[0](me), views[1](me)], s_send.at[k], s_recv.at[k])
+        if k < spread_here:
+            views = up_views(k)
+            both_ways(("up", k), views, [views[0](me), views[1](me)], s_send.at[k], s_recv.at[k])
 
     def up_relay(k):
-        relay(("up", k), up_views(k), s_send.at[k], s_recv.at[k])
-
+        if k < spread_here:
+            relay(("up", k), up_views(k), s_send.at[k], s_recv.at[k])
+
+    up_out(0)
     relay("hidden", hidden_views, h_send, h_recv)
-    pass_on(0)
+    own_mix.wait()
+    for k in range(1, chips):
+        away[0, k].wait_recv()
+    mix_views = [
+        lambda origin, p=p: mix_all.at[origin, pl.ds(p * (chips // 2), chips // 2), core] for p in range(2)
+    ]
+    both_ways("mix", mix_views, [mix_views[p](me) for p in range(2)], m_send, m_recv)
     for copy in smalls:
         copy.wait_recv()
     small_kept = keep(small_all, small_out, 6)
     own_hidden.wait()
     arrived("hidden")
-    up_out(0)
-    own_mix.wait()
-    for k in range(chips):
-        near[0, k].wait_recv()
-    length_rows = count // 2 * share
-    mix_views = [
-        lambda origin, p=p: mix_all.at[pl.ds(origin * count * share + p * length_rows, length_rows)] for p in range(2)
-    ]
-    both_ways("mix", mix_views, [mix_views[p](me) for p in range(2)], m_send, m_recv)
     gain = jnp.transpose(small_all[...].astype(jnp.float32))[experts_all : experts_all + 1]
 
     @pl.loop(0, hid.shape[0] // 128)
@@ -689,6 +725,10 @@
 
     normed_kept = keep(normed, normed_out, 7)
     pass_on(2)
+    for k in range(1, chips):
+        send_rows(k)
+    up_relay(0)
+    relay("mix", mix_views, m_send, m_recv)
     own_block.wait()
     for k in range(chips):
         near[2, k].wait_recv()
@@ -738,22 +778,28 @@
         def _():
             pltpu.make_async_copy(attended.at[own], target, local.at[10]).start()
 
-        if i == 0:
-            up_relay(0)
-            relay("mix", mix_views, m_send, m_recv)
-        elif i < chips:
-            up_relay(i)
         if i + 1 < chips:
             up_out(i + 1)
+        if i:
+            up_relay(i)
+        if i == 0:
+            arrived("mix")
+            both_cores = [
+                remote(
+                    "fsdp", sibling, mix_all.at[s, :, core], mix_all.at[s, :, core], y_send.at[s], y_recv.at[s]
+                )
+                for s in range(4)
+            ]
     for k in range(4, chips):
         up_relay(k)
         if k + 1 < chips:
             up_out(k + 1)
     attended_kept = keep(attended, attended_out, 11)
     sums_kept = keep(sums, sums_out, 12)
-    arrived("mix")
-    for k in range(chips):
+    for k in range(spread_here):
         arrived(("up", k))
+    for copy in both_cores:
+        copy.wait()
     for i in range(4):
         target = mixed.at[:, pl.ds(i * group, group)]
 
@@ -775,7 +821,7 @@
         copy.wait()
 
 
-def front(hidden, heads, mix, small, rows, lengths, experts_all, number):
+def front(hidden, heads, mix, small, rows, lengths, experts_all, spread_here, number):
     S, dma, low = jax.ShapeDtypeStruct, pltpu.SemaphoreType.DMA, jnp.bfloat16
     count, _, cap, width = rows.shape
     chips = count // 2
@@ -784,11 +830,11 @@
     full = 4 * tokens
     all_heads = (4, count, *heads.shape[1:])
     return pl.pallas_call(
-        functools.partial(front_kernel, count, cap, experts_all),
+        functools.partial(front_kernel, count, cap, experts_all, spread_here),
         out_shape=(
             S((full, width), low),
             S(all_heads, low),
-            S((width, mix.shape[1]), low),
+            S((4, chips, 2, *mix.shape), low),
             S((width, small.shape[1]), low),
             S((2, 4 * count * cap, width), low),
             S((full, 3 * group), low),
@@ -812,7 +858,7 @@
             dma((3, 2)), dma((3, 2)), dma((6,)), dma((6,)),
             dma((3, chips)), dma((3, chips)), dma((3, chips)), dma((3, chips)),
             dma((chips, 2)), dma((chips, 2)), dma((3, 2)), dma((3, 2)),
-            dma((chips, 3, 2)), dma((chips, 3, 2)), dma((4,)), dma((4,)), dma((13,)),
+            dma((chips, 3, 2)), dma((chips, 3, 2)), dma((4,)), dma((4,)), dma((4,)), dma((4,)), dma((13,)),
         ],
         compiler_params=pltpu.CompilerParams(
             collective_id=number, has_side_effects=True, vmem_limit_bytes=48 * 2**20
@@ -871,29 +917,79 @@
                 (proj_in, proj),
                 (attended_in, attended),
                 (sums_in, sums),
-                (mix_in, mix),
+                (mix_in.at[pl.ds(pl.multiple_of(me * group, group), group)], mix),
                 (heads_in, heads),
                 (normed_in, normed),
                 (small_in, small),
             )
         )
     ]
-    for side, (origin, peer) in enumerate(((one, two), (two, one))):
-        direct[side, side].wait_recv()
-        block = grads.at[pl.ds(origin * tokens + side * half, half)]
-        direct[2, side] = remote("seq", peer, block, block, g_send.at[2, side], g_recv.at[2, side])
     for copy in loads:
         copy.wait()
     head_of = lax.broadcasted_iota(jnp.int32, (tokens, group), 1) // HEAD_DIM
-    for i in range(4):
-        rows = slice(i * tokens, (i + 1) * tokens)
+    key_at = lax.broadcasted_iota(jnp.int32, (tokens, tokens), 0)
+    for j in range(4):
+        rows = slice(j * tokens, (j + 1) * tokens)
         for h in range(heads_local):
-            masked_query[i, h * tokens : (h + 1) * tokens, :] = jnp.where(head_of == h, proj[rows, :group], 0).astype(low)
+            key = proj[rows, group : 2 * group] * (HEAD_DIM**-0.5)
+            masked_key[j * heads_local + h] = jnp.where(head_of == h, key, 0).astype(low)
+            masked_value[j * heads_local + h] = jnp.where(head_of == h, proj[rows, 2 * group :], 0).astype(low)
+    grad_key[...] = jnp.zeros_like(grad_key)
+    grad_value[...] = jnp.zeros_like(grad_value)
+    gain_sum[...] = jnp.zeros_like(gain_sum)
+
+    def block(i, j, masked):
+        rows = pl.ds(pl.multiple_of(i * tokens, tokens), tokens)
+        keys = pl.ds(pl.multiple_of(j * tokens, tokens), tokens)
+        hidden = j * tokens + key_at >= length[0]
+        if masked:
+            hidden = hidden | (key_at > lax.broadcasted_iota(jnp.int32, (tokens, tokens), 1))
+        total = None
+        for h in range(heads_local):
+            lanes = slice(h * tokens, (h + 1) * tokens)
+            key = masked_key[j * heads_local + h]
+            scores = times_transposed(key, proj[rows, :group])
+            scores = jnp.where(hidden, MASKED, scores)
+            p = jnp.exp(scores - sums[h : h + 1, rows])
+            probs[:, lanes] = p.astype(low)
+            grad = times_transposed(masked_value[j * heads_local + h], grad_heads[...])
+            slopes[:, lanes] = (p * (grad - delta[h : h + 1, :])).astype(low)
+            term = transposed_times(slopes[:, lanes], key)
+            total = term if total is None else total + term
+        grad_query[...] += total
+        grad_value[keys, :] += times(probs[...], masked_grad[...])
+        grad_key[keys, :] += times(slopes[...], masked_query[...])
+
+    def queries(i):
+        rows = pl.ds(pl.multiple_of(i * tokens, tokens), tokens)
+        grad_heads[...] = times_transposed(grads[rows, :], mix[...]).astype(low)
+        out = grad_heads[...].astype(jnp.float32)
+        turned = jnp.transpose(out * attended[rows, :].astype(jnp.float32))
+        query = proj[rows, :group]
+        for h in range(heads_local):
+            delta[h : h + 1, :] = jnp.sum(turned[h * HEAD_DIM : (h + 1) * HEAD_DIM], axis=0, keepdims=True)
+            masked_grad[h * tokens : (h + 1) * tokens, :] = jnp.where(head_of == h, out, 0).astype(low)
+            masked_query[h * tokens : (h + 1) * tokens, :] = jnp.where(head_of == h, query, 0).astype(low)
+        grad_query[...] = jnp.zeros_like(grad_query)
+
+        @pl.loop(0, i)
+        def _(j):
+            block(i, j, False)
+
+        block(i, i, True)
+        grad_proj[rows, :group] = grad_query[...].astype(low)
+
     own_grad.wait()
+    queries(me)
+    for side, (origin, peer) in enumerate(((one, two), (two, one))):
+        direct[side, side].wait_recv()
+        source = grads.at[pl.ds(origin * tokens + side * half, half)]
+        direct[2, side] = remote("seq", peer, source, source, g_send.at[2, side], g_recv.at[2, side])
+    for side, origin in enumerate((one, two)):
+        direct[side, 1 - side].wait_recv()
+        queries(origin)
     for side in range(2):
-        direct[side, 1 - side].wait_recv()
         direct[2, side].wait_recv()
-
     for n in range(width // TILE):
         lanes = slice(n * TILE, (n + 1) * TILE)
         weights_mix[:, lanes] = transposed_times(attended[...], grads[:, lanes]).astype(low)
@@ -918,13 +1014,7 @@
                     "fsdp", sibling, small.at[:, owner * share // 128], sib_c.at[k], b_send.at[1, k], b_recv.at[1, k]
                 )
             ]
-        return [
-            remote(
-                "fsdp", sibling, weights.at[rows_at(s, owner)], sib_a.at[k, pl.ds(s * share, share)],
-                bb_send.at[s, k], bb_recv.at[s, k],
-            )
-            for s in range(4)
-        ]
+        raise ValueError(a)
 
     sib, own, got = (sib_a, sib_b, sib_c), (own_a, own_b, own_c), (got_a, got_b, got_c)
     totals = (total_a, total_b, total_c)
@@ -933,13 +1023,7 @@
         owner = (chip ^ k) * 2 + core
         for copy in to_sibling[a, k]:
             copy.wait_recv()
-        if a == 0:
-            for s in range(4):
-                rows = slice(s * share, (s + 1) * share)
-                own_a[k, rows, :] = (
-                    weights[rows_at(s, owner), :].astype(jnp.float32) + sib_a[k, rows, :].astype(jnp.float32)
-                ).astype(low)
-        elif a == 1:
+        if a == 1:
             mine = weights_mix[pl.ds(pl.multiple_of(owner * share, share), share), :]
             own_b[k] = (mine.astype(jnp.float32) + sib_b[k].astype(jnp.float32)).astype(low)
         else:
@@ -952,61 +1036,37 @@
 
     for k in order_of:
         to_sibling[1, k] = start_sibling(1, k, core ^ 1)
-    for i in range(4):
-        rows = slice(i * tokens, (i + 1) * tokens)
-        out = times_transposed(grads[rows, :], mix[...])
-        grad_heads[rows, :] = out.astype(low)
-        out = grad_heads[rows, :].astype(jnp.float32)
-        turned = jnp.transpose(out * attended[rows, :].astype(jnp.float32))
-        for h in range(heads_local):
-            delta[h : h + 1, rows] = jnp.sum(turned[h * HEAD_DIM : (h + 1) * HEAD_DIM], axis=0, keepdims=True)
-            masked_grad[i, h * tokens : (h + 1) * tokens, :] = jnp.where(head_of == h, out, 0).astype(low)
+    queries(both)
     for k in order_of:
         pair_sum(1, k)
-
-    grad_query[...] = jnp.zeros_like(grad_query)
-    gain_sum[...] = jnp.zeros_like(gain_sum)
+    grad_proj[:, group : 2 * group] = (grad_key[...] * (HEAD_DIM**-0.5)).astype(low)
+    grad_proj[:, 2 * group :] = grad_value[...].astype(low)
+    for s in range(4):
+        lanes = slice(s * group, (s + 1) * group)
+        weights[lanes, :] = transposed_times(normed[:, lanes], grad_proj[...]).astype(low)
+        for k in order_of:
+            owner = (chip ^ k) * 2
+            to_sibling[s + 3, k] = [
+                remote(
+                    "fsdp", sibling, weights.at[rows_at(s, owner + (core ^ 1))], sib_a.at[k, pl.ds(s * share, share)],
+                    bb_send.at[s, k], bb_recv.at[s, k],
+                )
+            ]
+    for s in range(4):
+        rows = slice(s * share, (s + 1) * share)
+        for k in order_of:
+            owner = (chip ^ k) * 2 + core
+            to_sibling[s + 3, k][0].wait_recv()
+            own_a[k, rows, :] = (
+                weights[rows_at(s, owner), :].astype(jnp.float32) + sib_a[k, rows, :].astype(jnp.float32)
+            ).astype(low)
+            if k:
+                away[s + 3, k] = remote(
+                    "fsdp", owner, own_a.at[k, pl.ds(s * share, share)], got_a.at[k, pl.ds(s * share, share)],
+                    z_send.at[s + 3, k], z_recv.at[s + 3, k],
+                )
     for j in range(4):
         own_rows = slice(j * tokens, (j + 1) * tokens)
-        for h in range(heads_local):
-            key = proj[own_rows, group : 2 * group]
-            masked_key[h] = jnp.where(head_of == h, key * (HEAD_DIM**-0.5), 0).astype(low)
-            masked_value[h] = jnp.where(head_of == h, proj[own_rows, 2 * group :], 0).astype(low)
-        grad_key[...] = jnp.zeros_like(grad_key)
-        grad_value[...] = jnp.zeros_like(grad_value)
-        key_at = lax.broadcasted_iota(jnp.int32, (tokens, tokens), 0)
-        outside = j * tokens + key_at >= length[0]
-
-        def block(i, masked):
-            rows = pl.ds(pl.multiple_of(i * tokens, tokens), tokens)
-            hidden = outside
-            if masked:
-                hidden = hidden | (key_at > lax.broadcasted_iota(jnp.int32, (tokens, tokens), 1))
-            total = None
-            for h in range(heads_local):
-                lanes = slice(h * tokens, (h + 1) * tokens)
-                scores = times_transposed(masked_key[h], proj[rows, :group])
-                scores = jnp.where(hidden, MASKED, scores)
-                p = jnp.exp(scores - sums[h : h + 1, rows])
-                probs[:, lanes] = p.astype(low)
-                grad = times_transposed(masked_value[h], grad_heads[rows, :])
-                slopes[:, lanes] = (p * (grad - delta[h : h + 1, rows])).astype(low)
-                term = transposed_times(slopes[:, lanes], masked_key[h])
-                total = term if total is None else total + term
-            grad_query[rows, :] += total
-            grad_value[...] += times(probs[...], masked_grad[i])
-            grad_key[...] += times(slopes[...], masked_query[i])
-
-        block(j, True)
-        if j < 3:
-
-            @pl.loop(j + 1, 4)
-            def _(i):
-                block(i, False)
-
-        grad_proj[own_rows, :group] = grad_query[own_rows, :].astype(low)
-        grad_proj[own_rows, group : 2 * group] = (grad_key[...] * (HEAD_DIM**-0.5)).astype(low)
-        grad_proj[own_rows, 2 * group :] = grad_value[...].astype(low)
         for n in range(width // TILE):
             lanes = slice(n * TILE, (n + 1) * TILE)
             back = times_transposed(grad_proj[own_rows, :], heads[lanes, :])
@@ -1021,14 +1081,9 @@
             )
     for b in range(width // 128):
         small[b // 2, b % 2, gain_row : gain_row + 1, :] = gain_sum[:, b * 128 : (b + 1) * 128]
-    for s in range(4):
-        lanes = slice(s * group, (s + 1) * group)
-        weights[lanes, :] = transposed_times(normed[:, lanes], grad_proj[...]).astype(low)
     for k in order_of:
-        to_sibling[0, k] = start_sibling(0, k, core ^ 1)
         to_sibling[2, k] = start_sibling(2, k, core ^ 1)
     for k in order_of:
-        pair_sum(0, k)
         pair_sum(2, k)
     for side, rest in enumerate((two, one)):
         rows = slice(side * half, (side + 1) * half)
@@ -1047,14 +1102,19 @@
         ).astype(low)
         stored.append(local(first.at[side, 1], normed_out.at[pl.ds(side * half, half)], keep.at[side]))
     for a in (1, 0, 2):
-        total = own[a][0].astype(jnp.float32)
-        for k in range(1, chips):
-            away[a, k].wait_recv()
-            total = total + got[a][k].astype(jnp.float32)
         if a == 0:
             for s in range(4):
-                total_a[s] = total[s * share : (s + 1) * share].astype(low)
+                rows = slice(s * share, (s + 1) * share)
+                total = own_a[0, rows, :].astype(jnp.float32)
+                for k in range(1, chips):
+                    away[s + 3, k].wait_recv()
+                    total = total + got_a[k, rows, :].astype(jnp.float32)
+                total_a[s] = total.astype(low)
         else:
+            total = own[a][0].astype(jnp.float32)
+            for k in range(1, chips):
+                away[a, k].wait_recv()
+                total = total + got[a][k].astype(jnp.float32)
             totals[a][...] = total
     crossed = []
     for a, out in ((0, heads_out), (2, small_out)):
@@ -1106,19 +1166,19 @@
             vmem(*sums.shape, dtype=f32),
             vmem(*normed.shape),
             vmem(*heads.shape),
-            vmem(*mix.shape),
+            vmem(group, width),
             vmem(*small.shape, dtype=f32),
-            vmem(full, group),
-            vmem(8, full, dtype=f32),
-            vmem(4, local_heads * tokens, group),
-            vmem(4, local_heads * tokens, group),
-            vmem(local_heads, tokens, group),
-            vmem(local_heads, tokens, group),
+            vmem(tokens, group),
+            vmem(8, tokens, dtype=f32),
+            vmem(local_heads * tokens, group),
+            vmem(local_heads * tokens, group),
+            vmem(4 * local_heads, tokens, group),
+            vmem(4 * local_heads, tokens, group),
             vmem(tokens, local_heads * tokens),
             vmem(tokens, local_heads * tokens),
+            vmem(tokens, group, dtype=f32),
             vmem(full, group, dtype=f32),
-            vmem(tokens, group, dtype=f32),
-            vmem(tokens, group, dtype=f32),
+            vmem(full, group, dtype=f32),
             vmem(full, 3 * group),
             vmem(4, tokens, width),
             vmem(width, 3 * group),
@@ -1134,7 +1194,7 @@
             vmem(2, tokens // 2, width),
             dma((3, 2)), dma((3, 2)),
             dma((2, chips)), dma((2, chips)), dma((4, chips)), dma((4, chips)),
-            dma((3, chips)), dma((3, chips)),
+            dma((7, chips)), dma((7, chips)),
             dma((3, 3)), dma((3, 3)), dma((3, 2)), dma((3, 2)), dma((8,)), dma((5,)),
         ],
         compiler_params=pltpu.CompilerParams(
@@ -1207,6 +1267,8 @@
     upstream_low = jnp.where(valid > 0, out_grad[0], 0).astype(low)
     upstream = upstream_low.astype(jnp.float32)
     up_rows = times(dispatch, upstream_low).astype(low)
+    chips = owners // 2
+    fused = 4 * owners * capacity <= 1024
     normed, weight_qkv, weight_mix, small, up_all, projected, attended, totals, mixed = front(
         hidden[0],
         qkv_weight.reshape(rows_own, 3, seq_count, group_width)
@@ -1217,17 +1279,22 @@
         up_rows.reshape(owners, expert_local, capacity, width),
         lengths,
         experts_all,
+        SPREAD_FIRST if fused else chips,
         0,
     )
     weight_qkv = weight_qkv.reshape(width, 3 * group_width)
+    weight_mix = weight_mix.reshape(width, width)
     weight_route = small[:, :experts_all]
     gain_one = small[:, experts_all].astype(jnp.float32)
     gain_two = small[:, experts_all + 1].astype(jnp.float32)
-    mix_rows = lax.dynamic_slice_in_dim(weight_mix, seq_place * group_width, group_width, 0)
-    fused = 4 * owners * capacity <= 1024
     if not fused:
-        up_all = up_all.reshape(expert_local, owners // 2, seq_count, 2 * capacity, width)
-        up_all = jnp.roll(up_all, lax.axis_index("fsdp") // 2, axis=1)
+        up_all = up_all.reshape(expert_local, chips, seq_count, 2 * capacity, width)
+        chip, bit = lax.axis_index("fsdp") // 2, 1
+        while bit < chips:
+            pairs = up_all.reshape(expert_local, chips // (2 * bit), 2, bit, seq_count, 2 * capacity, width)
+            up_all = jnp.where((chip // bit) % 2 == 1, pairs[:, :, ::-1], pairs)
+            bit *= 2
+        up_all = up_all.reshape(expert_local, chips, seq_count, 2 * capacity, width)
         up_all = up_all.transpose(0, 2, 1, 3, 4)
     inputs = hidden[0].astype(jnp.float32)
     middle = inputs + times(mixed, weight_mix)
@@ -1302,7 +1369,7 @@
         totals,
         normed,
         weight_qkv,
-        mix_rows,
+        weight_mix,
         small_grad,
         lengths,
         owners,
@@ -1327,8 +1394,8 @@
         mix_grad,
         small_sum[experts_all + 1],
         small_sum[:experts_all].T,
-        expert_in_grad,
-        expert_out_grad,
+        expert_in_grad.astype(jnp.float32),
+        expert_out_grad.astype(jnp.float32),
     )
 
 

time: 371 us -> 333 us (0.90)
  Pallas kernels: 317 us -> 290 us
  local copies, waits for them, and re-layouts: 28.9 us -> 9.1 us
  other arithmetic: 9.03 us -> 18.9 us
    pallas_call x2, Pallas kernels: 253 us -> 217 us  [the longest x1 142 us: moe(): pl.pallas_call(functools.partial(moe_kernel, chips, cap, experts_all, SPR...]
    unnamed x28 -> x36, local copies, waits for them, and re-layouts: 18.5 us -> 1.17 us
    convert_element_type x0 -> x2, other arithmetic: none -> 11.2 us  [the longest x1 6.79 us: shards(): expert_in_grad.astype(jnp.float32)]
    pallas_call x1, Pallas kernels: 64.6 us -> 73 us  [back(): pl.pallas_call(functools.partial(back_kernel, count, gain_row), out_shape...]
where the time goes in v1:
time: 333 us; the launch traced here: 329 us
  Pallas kernels  290 us (87%)
  other arithmetic  18.9 us (6%)
  matrix products  9.18 us (3%)
  local copies, waits for them, and re-layouts  9.1 us (3%)
    pallas_call x1, Pallas kernels, moe(): pl.pallas_call(functools.partial(moe_kernel, chips, cap, experts_all, SPR...  142 us
    pallas_call x1, Pallas kernels, front(): pl.pallas_call(functools.partial(front_kernel, count, cap, experts_all, s...  75.1 us
    pallas_call x1, Pallas kernels, back(): pl.pallas_call(functools.partial(back_kernel, count, gain_row), out_shape...  73 us
    convert_element_type x1, other arithmetic, shards(): expert_in_grad.astype(jnp.float32)  6.79 us

profile of v1, /device:TPU:0, one launch (start us, length us, event | category | flops | bytes accessed | tf_op | source)
XLA Modules:
  0.0 328.9 jit_solution(6986710109943510055)
XLA Ops:
  0.6 0.0 copy-start.14
  0.7 0.0 copy-start.15
  0.7 0.0 copy-start.16
  0.7 0.0 copy-start
  0.7 0.0 copy-start.5
  0.7 0.9 convert_reduce_fusion.2
  1.6 0.7 multiply_add_fusion.2
  3.0 1.6 convolution_convert_fusion.1
  4.6 1.1 reshape.133
  5.6 0.1 copy.44
  5.7 0.2 reshape.134.heads
  6.0 0.0 copy-done.14
  6.0 0.1 copy.37
  6.1 0.0 copy-done.15
  6.1 0.1 copy.38
  6.2 0.0 copy-done.16
  6.2 0.1 copy.39
  6.3 0.1 fusion.26.small
  6.4 0.0 copy-done
  6.4 0.0 copy-done.5
  6.4 75.1 %shard_map.178 = (bf16[1024,1024]{1,0:T(8,128)(2,1)}, bf16[4,8,32,768]{3,2,1,0:T(8,128)(2,1)S(1)}, bf16[4,4,2,32,1024]{4,3,2,1,0:T(8,128)(2,1)}, bf16[1024,128]{...) custom-call(bf16[256,1024]{1,0:T(8,128)(2,1)S(1)} %bitcast.52, ...), custom_call_target="tpu_custom_call" | custom-call | tf_op jit(solution)/shard_map/pallas_call | solution.py:832
  81.4 0.0 copy-start.3
  81.5 0.0 copy-start.4
  81.5 0.0 copy-start.1
  81.5 3.2 multiply_reduce_fusion.2
  84.7 0.0 copy-done.4
  84.7 0.0 copy-done.6
  84.8 0.4 convert_reduce_fusion
  85.1 0.2 multiply_convert_fusion.1
  85.3 1.4 convolution_convert_fusion
  86.7 141.9 %shard_map.179 = (bf16[2,8,2,32,1024]{4,3,2,1,0:T(8,128)(2,1)}, bf16[2,1024,1024]{2,1,0:T(8,128)(2,1)}, bf16[2,1024,1024]{2,1,0:T(8,128)(2,1)}) custom-call(bf16[8,2,32,1024]{3,2,1,0:T(8,128)(2,1)} %bitcast.61, bf16[2,1024,1024]{2,1,0:T(8,128)(2,1)} %get-tuple-element.28.up_rows, bf16[1024,128]{1,0:T(8,128)(2,1)} %copy-done.1, bf16[2,1024,1024]{2,1,0:T(8,128)(2,1)} %w_in.1, ...), custom_call_target="tpu_custom_call" | custom-call | flops 25769803776 | bytes 33554432 | tf_op jit(solution)/shard_map/pallas_call | solution.py:517
  228.7 0.0 copy-start.9
  228.7 1.8 fusion.34
  230.5 0.0 copy-start.2
  230.5 0.0 copy-start.13
  230.5 0.0 copy-done.9
  230.5 0.6 fusion
  231.1 0.3 copy-done.2
  231.4 0.3 fusion.35
  231.7 0.0 copy-done.13
  231.8 0.2 fusion.30
  232.0 0.3 fusion.12
  232.3 1.6 multiply_reduce_fusion
  233.9 0.1 pad.11.clone
  234.0 0.1 pad_maximum_fusion
  234.1 0.1 reshape.140
  234.2 0.7 copy.45
  234.8 3.0 fusion.33
  237.9 73.0 %shard_map.180 = (bf16[256,1024]{1,0:T(8,128)(2,1)}, bf16[4,32,768]{2,1,0:T(8,128)(2,1)}, f32[32,1024]{1,0:T(8,128)}, f32[4,24,128]{2,1,0:T(8,128)}) custom-call(bf16[256,1024]{1,0:T(8,128)(2,1)} %get-tuple-element.49.grad_in, bf16[1024,768]{1,0:T(8,128)(2,1)} %get-tuple-element.30.proj_in, bf16[1024,256]{1,0:T(8,128)(2,1)} %copy-done.4, ...), custom_call_target="tpu_custom_call" | custom-call | tf_op jit(solution)/shard_map/pallas_call | solution.py:1152
  310.9 0.0 copy-start.10
  310.9 0.0 copy-start.8
  310.9 1.2 reshape.150
  312.1 0.3 copy.41
  312.4 0.9 reshape.147
  313.4 0.0 copy-done.10
  313.4 0.3 fusion.3
  313.7 1.3 fusion.2
  315.0 0.7 dynamic-slice_bitcast_fusion
  315.7 0.6 dynamic-slice_bitcast_fusion.1
  316.3 0.6 fusion.29
  316.9 6.8 %convert_element_type.93 = f32[2,1024,1024]{2,1,0:T(8,128)} convert(bf16[2,1024,1024]{2,1,0:T(8,128)(2,1)} %get-tuple-element.39) | non-fusion elementwise | flops 2097152 | bytes 12582912 | tf_op jit(solution)/shard_map/convert_element_type | solution.py:1397
  323.7 0.0 copy-done.7
  323.7 4.4 %convert_element_type.94 = f32[2,1024,1024]{2,1,0:T(8,128)} convert(bf16[2,1024,1024]{2,1,0:T(8,128)(2,1)S(1)} %copy-done.7) | non-fusion elementwise | flops 2097152 | bytes 12582912 | tf_op jit(solution)/shard_map/convert_element_type | solution.py:1398
  328.1 0.7 copy.48
  (19 shorter events, 0.1 us)
Async XLA Ops:
  0.6 5.3 %copy-start.14 = (bf16[32,16]{0,1:T(8,128)(2,1)S(1)}, bf16[32,16]{0,1:T(8,128)(2,1)}, u32[]{:S(2)}) copy-start(bf16[32,16]{0,1:T(8,128)(2,1)} %param.18) | copy-start | bytes 3076
  0.7 5.4 %copy-start.15 = (bf16[32]{0:T(256)(128)(2,1)S(1)}, bf16[32]{0:T(256)(128)(2,1)}, u32[]{:S(2)}) copy-start(bf16[32]{0:T(256)(128)(2,1)} %param.14) | copy-start | bytes 196
  0.7 5.5 %copy-start.16 = (bf16[32]{0:T(256)(128)(2,1)S(1)}, bf16[32]{0:T(256)(128)(2,1)}, u32[]{:S(2)}) copy-start(bf16[32]{0:T(256)(128)(2,1)} %param.17) | copy-start | bytes 196
  0.7 5.7 %copy-start = (bf16[1,256,1024]{2,1,0:T(8,128)(2,1)S(1)}, bf16[1,256,1024]{2,1,0:T(8,128)(2,1)}, u32[]{:S(2)}) copy-start(bf16[1,256,1024]{2,1,0:T(8,128)(2,1)} %param.11) | copy-start | bytes 1572868
  0.7 5.7 %copy-start.5 = (bf16[32,1024]{1,0:T(8,128)(2,1)S(1)}, bf16[32,1024]{1,0:T(8,128)(2,1)}, u32[]{:S(2)}) copy-start(bf16[32,1024]{1,0:T(8,128)(2,1)} %mix.1) | copy-start | bytes 196612
  81.4 3.3 copy-start.3
  81.5 3.3 copy-start.4
  81.5 3.3 copy-start.6
  81.5 3.3 %copy-start.1 = (bf16[1024,128]{1,0:T(8,128)(2,1)}, bf16[1024,128]{1,0:T(8,128)(2,1)S(1)}, u32[]{:S(2)}) copy-start(bf16[1024,128]{1,0:T(8,128)(2,1)S(1)} %get-tuple-element.27.route) | copy-start | bytes 786436
  228.7 1.8 copy-start.9
  230.5 1.0 copy-start.2
  230.5 1.2 copy-start.13
  310.9 2.5 copy-start.10
  310.9 2.8 copy-start.8
  313.4 1.6 copy-start.12
  316.9 6.8 %copy-start.7 = (bf16[2,1024,1024]{2,1,0:T(8,128)(2,1)S(1)}, bf16[2,1024,1024]{2,1,0:T(8,128)(2,1)}, u32[]{:S(2)}) copy-start(bf16[2,1024,1024]{2,1,0:T(8,128)(2,1)} %get-tuple-element.40) | copy-start | bytes 12582916
  323.7 4.4 %copy-start.11 = (f32[32,1024]{1,0:T(8,128)S(1)}, f32[32,1024]{1,0:T(8,128)}, u32[]{:S(2)}) copy-start(f32[32,1024]{1,0:T(8,128)} %get-tuple-element.78) | copy-start | bytes 393220

commit v2 on v1

--- a/solution.py
+++ b/solution.py
@@ -13,6 +13,7 @@
 ROOT = 0.7978845608028654
 TILE = 256
 SPREAD_FIRST = 3
+TURN = (1, 3, 2, 0)
 GRAD = 256
 MESH = pl.DeviceIdType.MESH
 ANY = pl.BlockSpec(memory_space=pl.ANY)
@@ -65,7 +66,7 @@
         out_specs=jax.tree.map(lambda _: ANY, outputs),
         scratch_shapes=scratch,
         compiler_params=pltpu.CompilerParams(
-            collective_id=number, has_side_effects=True, vmem_limit_bytes=48 * 2**20
+            collective_id=number, has_side_effects=True, vmem_limit_bytes=60 * 2**20
         ),
     )(*inputs)
 
@@ -426,9 +427,11 @@
             staged[slot] = local(stage.at[slot], out.at[j, lanes], store.at[slot])
 
     later = range(spread_first, chips)
+    turn = TURN
+    away = [k for k in turn if k]
     dispatch(0)
-    dispatch(1)
-    dispatch(2)
+    dispatch(away[0])
+    dispatch(away[1])
     for j in range(2):
         loads.append(local(w_in.at[j], W1.at[j], load.at[j]))
         loads.append(local(w_out.at[j], W2.at[j], load.at[2 + j]))
@@ -440,56 +443,58 @@
         for j in range(2):
             block = rows_of(k, me)
             loads.append(local(up_rows.at[j, block], U.at[j, block], load.at[7 + 2 * n + j]))
-    z_arrived(0)
-    spread_out(1, 0)
-    for k in later:
-        spread_out(0, k)
-    z_arrived(1)
-    spread_out(1, 1)
-    dispatch(3)
-    relay(1, 0)
+    if turn[0]:
+        for k in later:
+            spread_out(0, k)
+    z_arrived(turn[0])
+    spread_out(1, turn[0])
+    if not turn[0]:
+        for k in later:
+            spread_out(0, k)
+    z_arrived(turn[1])
+    spread_out(1, turn[1])
+    dispatch(away[2])
+    relay(1, turn[0])
     for copy in loads:
         copy.wait()
     for k in later:
         relay(0, k)
-    z_arrived(2)
-    spread_out(1, 2)
-    all_arrived(1, 0)
-    experts(0, 0)
-    collect_one(0, 0)
-    relay(1, 1)
-    z_arrived(3)
-    spread_out(1, 3)
-    experts(0, 1)
-    collect_one(0, 1)
-    relay(1, 2)
-    for k in range(1, chips):
+    z_arrived(turn[2])
+    spread_out(1, turn[2])
+    for n in range(chips):
+        k = turn[n]
         all_arrived(1, k)
         if k >= spread_first:
             all_arrived(0, k)
         experts(k, 0)
         collect_one(k, 0)
-        if k == 1:
-            relay(1, 3)
-        collect_two(k - 1, 0)
-        if k > 1:
-            collect_three(k - 2, 0)
+        if n < 2:
+            relay(1, turn[n + 1 + (n > 0)])
+        if n == 0:
+            z_arrived(turn[3])
+            spread_out(1, turn[3])
+        else:
+            collect_two(turn[n - 1], 0)
+        if n > 1:
+            collect_three(turn[n - 2], 0)
         experts(k, 1)
         collect_one(k, 1)
-        collect_two(k - 1, 1)
-        if k > 1:
-            collect_three(k - 2, 1)
-    last = chips - 1
+        if n == 0:
+            relay(1, turn[2])
+        else:
+            collect_two(turn[n - 1], 1)
+        if n > 1:
+            collect_three(turn[n - 2], 1)
     weight_grads(0, 0, range(4))
-    collect_two(last, 0)
-    collect_three(last - 1, 0)
-    collect_two(last, 1)
-    collect_three(last - 1, 1)
+    collect_two(turn[3], 0)
+    collect_three(turn[2], 0)
+    collect_two(turn[3], 1)
+    collect_three(turn[2], 1)
     weight_grads(0, 1, range(4))
     weight_grads(1, 0, range(2))
-    collect_three(last, 0)
+    collect_three(turn[3], 0)
     weight_grads(1, 0, range(2, 4))
-    collect_three(last, 1)
+    collect_three(turn[3], 1)
     weight_grads(1, 1, range(4))
     for copy in staged.values():
         copy.wait()
@@ -553,7 +558,7 @@
             dma((2,)),
         ],
         compiler_params=pltpu.CompilerParams(
-            collective_id=number, has_side_effects=True, vmem_limit_bytes=58 * 2**20
+            collective_id=number, has_side_effects=True, vmem_limit_bytes=60 * 2**20
         ),
         cost_estimate=pl.CostEstimate(
             flops=12 * 2 * count * width * hidden_units, bytes_accessed=2**25, transcendentals=0
@@ -562,9 +567,11 @@
 
 
 def front_kernel(
-    count, cap, experts_all, spread_here, hidden, heads, mix, small, rows, length,
-    normed_out, heads_out, mix_all, small_out, up, projected_out, attended_out, sums_out, mixed,
-    staged, hid, heads_all, small_all, normed, proj, attended, sums, acc, stat,
+    count, cap, experts_all, spread_here, hidden, qkv_weight, mix, out_grad, router, gain_a, gain_b, ids, length,
+    normed_out, heads_out, mix_out, small_out, gains_out, up, projected_out, attended_out, sums_out,
+    middle_out, low_out, logits_out, sent_out, hit_out,
+    staged, hid, heads_all, small_own, small_all, gains, normed, proj, attended, sums, acc, stat,
+    mix_all, up_low, rows, hit, mixed, middle, normed_low, logits, sent_rows,
     h_send, h_recv, q_send, q_recv, f_send, f_recv, n_send, n_recv, u_send, u_recv, m_send, m_recv,
     s_send, s_recv, x_send, x_recv, y_send, y_recv, local,
 ):
@@ -604,7 +611,7 @@
             return small_all.at[pl.ds(pl.multiple_of((me * count + owner) * share, share), share)]
         return heads_all.at[:, owner]
 
-    own_of = (mix, small, staged)
+    own_of = (mix, small_own, staged)
 
     def send_far(a):
         for k in range(1, chips):
@@ -652,26 +659,65 @@
                 u_send.at[k, c], u_recv.at[k, c],
             )
 
-    send_far(1)
-    send_near(1)
+    columns = [
+        (pl.ds(p * group, group), lambda to, p=p: pl.ds(pl.multiple_of((p * 4 + to) * group, group), group))
+        for p in range(3)
+    ]
     exchanged = [
-        remote("seq", peer, heads.at[peer], staged.at[me], q_send.at[i], q_recv.at[i])
+        remote(
+            "seq", peer, qkv_weight.at[:, view(peer)], staged.at[me, :, into], q_send.at[i, p], q_recv.at[i, p]
+        )
         for i, peer in enumerate(others)
+        for p, (into, view) in enumerate(columns)
     ]
-    own_heads = keep(heads.at[me], staged.at[me], 0)
-    own_hidden = keep(hidden, hid.at[pl.ds(me * tokens, tokens)], 1)
-    own_mix = keep(mix, block(0, place), 2)
-    own_small = keep(small, block(1, place), 3)
-    own_rows = keep(rows.at[place], up.at[:, pl.ds(me * part + core * cap, cap)], 4)
     half = tokens // 2
     hidden_views = [
         lambda origin, p=p: hid.at[pl.ds(origin * tokens + p * half, half)] for p in range(2)
     ]
     both_ways("hidden", hidden_views, [hidden.at[pl.ds(p * half, half)] for p in range(2)], h_send, h_recv)
     send_far(0)
+    own_heads = [
+        keep(qkv_weight.at[:, view(me)], staged.at[me, :, into], 14 + p) for p, (into, view) in enumerate(columns)
+    ]
+    own_hidden = keep(hidden, hid.at[pl.ds(me * tokens, tokens)], 1)
+    own_mix = keep(mix, block(0, place), 2)
+    own_grad = keep(out_grad, up_low, 13)
+    at_lane = lax.broadcasted_iota(jnp.int32, small_own.shape, 1)
+    square = lax.broadcasted_iota(jnp.int32, (share, share), 0) == lax.broadcasted_iota(jnp.int32, (share, share), 1)
+    stat[:share, :] = jnp.zeros((share, 128), jnp.float32)
+    stat[:share, :experts_all] = router[...].astype(jnp.float32)
+    packed = stat[:share, :]
+    for n, gain in enumerate((gain_a, gain_b)):
+        column = jnp.sum(jnp.where(square, gain[...].astype(jnp.float32), 0.0), axis=1, keepdims=True)
+        packed = jnp.where(at_lane == experts_all + n, column, packed)
+    small_own[...] = packed.astype(small_own.dtype)
+    send_far(1)
+    send_near(1)
+    own_small = keep(small_own, block(1, place), 3)
+    chosen = ids[...].astype(jnp.float32)
+    across = jnp.transpose(jnp.broadcast_to(chosen, (tokens, 128)))[:1]
+    first = lax.broadcasted_iota(jnp.int32, (tokens, tokens), 0)
+    second = lax.broadcasted_iota(jnp.int32, (tokens, tokens), 1)
+    ranks = jnp.sum(jnp.where((chosen == across) & (first < second), 1.0, 0.0), axis=0, keepdims=True)
+    slot = (across * cap + ranks).astype(jnp.int32)
+    hit[...] = jnp.where(lax.broadcasted_iota(jnp.int32, hit.shape, 0) == slot, 1.0, 0.0).astype(hit.dtype)
+    own_grad.wait()
+    position = me * tokens + lax.broadcasted_iota(jnp.int32, (tokens, 1), 0)
+    up_low[...] = jnp.where(position < length[0], up_low[...].astype(jnp.float32), 0.0).astype(up_low.dtype)
+
+    def to_slots(values, target):
+        @pl.loop(0, count)
+        def _(owner):
+            picked = hit[pl.ds(pl.multiple_of(owner * 2 * cap, 2 * cap), 2 * cap), :]
+            target[owner] = times(picked, values[...]).astype(target.dtype).reshape(target.shape[1:])
+
+    to_slots(up_low, rows)
+    own_rows = keep(rows.at[place], up.at[:, pl.ds(me * part + core * cap, cap)], 4)
     send_rows(0)
+    hit_kept = keep(hit, hit_out, 0)
     pass_on(1)
-    own_heads.wait()
+    for copy in own_heads:
+        copy.wait()
     for copy in exchanged:
         copy.wait_recv()
     own_block = keep(staged, heads_all.at[:, place], 5)
@@ -681,7 +727,7 @@
     for k in range(chips):
         near[1, k].wait_recv()
     mine = small_all.at[pl.ds(pl.multiple_of(me * count * share, share), count * share)]
-    smalls = [remote("seq", peer, mine, mine, q_send.at[3 + i], q_recv.at[3 + i]) for i, peer in enumerate(others)]
+    smalls = [remote("seq", peer, mine, mine, q_send.at[3, i], q_recv.at[3, i]) for i, peer in enumerate(others)]
 
     def up_views(k):
         return [lambda origin, j=j: up.at[j, pl.ds(k * chunk + origin * part, part)] for j in range(2)]
@@ -714,7 +760,11 @@
     small_kept = keep(small_all, small_out, 6)
     own_hidden.wait()
     arrived("hidden")
-    gain = jnp.transpose(small_all[...].astype(jnp.float32))[experts_all : experts_all + 1]
+    turned = jnp.transpose(small_all[...].astype(jnp.float32))
+    gains[0:1, :] = turned[experts_all : experts_all + 1]
+    gains[1:2, :] = turned[experts_all + 1 : experts_all + 2]
+    gains_kept = keep(gains, gains_out, 17)
+    gain = gains[0:1, :]
 
     @pl.loop(0, hid.shape[0] // 128)
     def _(t):
@@ -778,11 +828,10 @@
         def _():
             pltpu.make_async_copy(attended.at[own], target, local.at[10]).start()
 
-        if i + 1 < chips:
-            up_out(i + 1)
-        if i:
-            up_relay(i)
+        if i == 1:
+            up_relay(1)
         if i == 0:
+            up_out(1)
             arrived("mix")
             both_cores = [
                 remote(
@@ -790,16 +839,9 @@
                 )
                 for s in range(4)
             ]
-    for k in range(4, chips):
-        up_relay(k)
-        if k + 1 < chips:
-            up_out(k + 1)
+    up_out(2)
     attended_kept = keep(attended, attended_out, 11)
     sums_kept = keep(sums, sums_out, 12)
-    for k in range(spread_here):
-        arrived(("up", k))
-    for copy in both_cores:
-        copy.wait()
     for i in range(4):
         target = mixed.at[:, pl.ds(i * group, group)]
 
@@ -815,55 +857,111 @@
         def _():
             pltpu.make_async_copy(attended.at[pl.ds(i * tokens, tokens)], target, local.at[10]).wait()
 
+    up_relay(2)
+    for copy in both_cores:
+        copy.wait()
+    mix_kept = keep(mix_all.at[me], mix_out, 18)
+    for n in range(width // TILE):
+        lanes = slice(n * TILE, (n + 1) * TILE)
+        total = hid[pl.ds(pl.multiple_of(me * tokens, tokens), tokens), lanes].astype(jnp.float32)
+        for s in range(4):
+            weights = mix_all[s, :, :, :, lanes].reshape(group, TILE)
+            total = total + times(mixed[:, s * group : (s + 1) * group], weights)
+        middle[:, lanes] = total
+    middle_kept = keep(middle, middle_out, 19)
+    for t in range(tokens // 128):
+        span = slice(t * 128, (t + 1) * 128)
+        value = middle[span, :]
+        scale = lax.rsqrt(jnp.mean(value * value, axis=-1, keepdims=True) + EPS)
+        normed_low[span, :] = (value * scale * gains[1:2, :]).astype(normed_low.dtype)
+    logits[...] = times(normed_low[...], small_all[...])
+    to_slots(normed_low, sent_rows)
+    last = [
+        keep(normed_low, low_out, 20),
+        keep(logits, logits_out, 21),
+        keep(sent_rows, sent_out, 22),
+    ]
+    for k in range(3, chips):
+        up_out(k)
+        up_relay(k)
+    for k in range(spread_here):
+        arrived(("up", k))
     for copy in (*direct.values(), *exchanged, *smalls, *away.values(), *near.values(), *moved.values()):
         copy.wait_send()
-    for copy in (small_kept, normed_kept, heads_kept, projected_kept, attended_kept, sums_kept):
+    for copy in (
+        small_kept, normed_kept, heads_kept, projected_kept, attended_kept, sums_kept,
+        hit_kept, gains_kept, mix_kept, middle_kept, *last,
+    ):
         copy.wait()
 
 
-def front(hidden, heads, mix, small, rows, lengths, experts_all, spread_here, number):
-    S, dma, low = jax.ShapeDtypeStruct, pltpu.SemaphoreType.DMA, jnp.bfloat16
-    count, _, cap, width = rows.shape
+def front(hidden, qkv_weight, mix, out_grad, router, gain_a, gain_b, ids, lengths, count, cap, spread_here, number):
+    S, dma, low, f32 = jax.ShapeDtypeStruct, pltpu.SemaphoreType.DMA, jnp.bfloat16, jnp.float32
     chips = count // 2
-    tokens = hidden.shape[0]
-    group = heads.shape[2] // 3
+    tokens, width = hidden.shape
+    experts_all = router.shape[1]
+    group = qkv_weight.shape[1] // 12
+    share = qkv_weight.shape[0]
     full = 4 * tokens
-    all_heads = (4, count, *heads.shape[1:])
+    lanes = -(-(experts_all + 2) // 128) * 128
+    all_heads = (4, count, share, 3 * group)
+    slots = experts_all * cap
+
+    def vmem(*shape, dtype=low):
+        return pltpu.VMEM(shape, dtype)
+
+    near = pl.BlockSpec(memory_space=pltpu.VMEM)
     return pl.pallas_call(
         functools.partial(front_kernel, count, cap, experts_all, spread_here),
         out_shape=(
             S((full, width), low),
             S(all_heads, low),
-            S((4, chips, 2, *mix.shape), low),
-            S((width, small.shape[1]), low),
+            S((chips, 2, share, width), low),
+            S((width, lanes), low),
+            S((8, width), f32),
             S((2, 4 * count * cap, width), low),
             S((full, 3 * group), low),
             S((full, group), low),
-            S((8, full), jnp.float32),
+            S((8, full), f32),
+            S((tokens, width), f32),
             S((tokens, width), low),
+            S((tokens, lanes), f32),
+            S((count, 2, cap, width), low),
+            S((slots, tokens), low),
         ),
-        in_specs=[ANY] * 5 + [pl.BlockSpec(memory_space=pltpu.SMEM)],
-        out_specs=(ANY,) * 9,
+        in_specs=[ANY] * 4 + [near] * 4 + [pl.BlockSpec(memory_space=pltpu.SMEM)],
+        out_specs=(ANY,) * 14,
         scratch_shapes=[
-            pltpu.VMEM(heads.shape, low),
-            pltpu.VMEM((full, width), low),
-            pltpu.VMEM(all_heads, low),
-            pltpu.VMEM((width, small.shape[1]), low),
-            pltpu.VMEM((full, width), low),
-            pltpu.VMEM((full, 3 * group), low),
-            pltpu.VMEM((full, group), low),
-            pltpu.VMEM((8, full), jnp.float32),
-            pltpu.VMEM((tokens, group), jnp.float32),
-            pltpu.VMEM((tokens, 128), jnp.float32),
-            dma((3, 2)), dma((3, 2)), dma((6,)), dma((6,)),
+            vmem(4, share, 3 * group),
+            vmem(full, width),
+            vmem(*all_heads),
+            vmem(share, lanes),
+            vmem(width, lanes),
+            vmem(8, width, dtype=f32),
+            vmem(full, width),
+            vmem(full, 3 * group),
+            vmem(full, group),
+            vmem(8, full, dtype=f32),
+            vmem(tokens, group, dtype=f32),
+            vmem(tokens, 128, dtype=f32),
+            vmem(4, chips, 2, share, width),
+            vmem(tokens, width),
+            vmem(count, 2, cap, width),
+            vmem(slots, tokens),
+            vmem(tokens, width),
+            vmem(tokens, width, dtype=f32),
+            vmem(tokens, width),
+            vmem(tokens, lanes, dtype=f32),
+            vmem(count, 2, cap, width),
+            dma((3, 2)), dma((3, 2)), dma((4, 3)), dma((4, 3)),
             dma((3, chips)), dma((3, chips)), dma((3, chips)), dma((3, chips)),
             dma((chips, 2)), dma((chips, 2)), dma((3, 2)), dma((3, 2)),
-            dma((chips, 3, 2)), dma((chips, 3, 2)), dma((4,)), dma((4,)), dma((4,)), dma((4,)), dma((13,)),
+            dma((chips, 3, 2)), dma((chips, 3, 2)), dma((4,)), dma((4,)), dma((4,)), dma((4,)), dma((23,)),
         ],
         compiler_params=pltpu.CompilerParams(
-            collective_id=number, has_side_effects=True, vmem_limit_bytes=48 * 2**20
+            collective_id=number, has_side_effects=True, vmem_limit_bytes=60 * 2**20
         ),
-    )(hidden, heads, mix, small, rows, lengths)
+    )(hidden, qkv_weight, mix, out_grad, router, gain_a, gain_b, ids, lengths)
 
 
 def back_kernel(
@@ -917,7 +1015,7 @@
                 (proj_in, proj),
                 (attended_in, attended),
                 (sums_in, sums),
-                (mix_in.at[pl.ds(pl.multiple_of(me * group, group), group)], mix),
+                (mix_in, mix),
                 (heads_in, heads),
                 (normed_in, normed),
                 (small_in, small),
@@ -1198,7 +1296,7 @@
             dma((3, 3)), dma((3, 3)), dma((3, 2)), dma((3, 2)), dma((8,)), dma((5,)),
         ],
         compiler_params=pltpu.CompilerParams(
-            collective_id=number, has_side_effects=True, vmem_limit_bytes=56 * 2**20
+            collective_id=number, has_side_effects=True, vmem_limit_bytes=60 * 2**20
         ),
     )(grad, proj, attended, sums, normed, heads, mix, small, lengths)
 
@@ -1227,8 +1325,6 @@
     rows_own = qkv_weight.shape[0]
     length = lengths[0]
     experts_all = router_weight.shape[1]
-    small = jnp.concatenate([router_weight, attn_gain[:, None], moe_gain[:, None]], axis=1)
-    small = jnp.pad(small, ((0, 0), (0, -small.shape[1] % 128)))
     expert_local = expert_in.shape[0]
     capacity = -(-max(2, 2 * tokens // experts_all) // 16) * 16
     slots = experts_all * capacity
@@ -1237,13 +1333,6 @@
     valid = (position < length).astype(jnp.float32)[:, None]
     chosen = expert_ids[0, :, 0]
     choose = chosen[:, None] == jnp.arange(experts_all, dtype=jnp.int32)[None, :]
-    order = jnp.arange(tokens, dtype=jnp.int32)
-    earlier = (order[None, :] < order[:, None]) & (chosen[None, :] == chosen[:, None])
-    ranks = jnp.sum(earlier.astype(jnp.int32), axis=1)
-    slot = chosen * capacity + ranks
-    hit = jnp.arange(slots, dtype=jnp.int32)[:, None] == slot[None, :]
-    dispatch = hit.astype(low)
-
     def to_owners(rows, number):
         return exchange(
             "fsdp",
@@ -1266,27 +1355,42 @@
 
     upstream_low = jnp.where(valid > 0, out_grad[0], 0).astype(low)
     upstream = upstream_low.astype(jnp.float32)
-    up_rows = times(dispatch, upstream_low).astype(low)
     chips = owners // 2
     fused = 4 * owners * capacity <= 1024
-    normed, weight_qkv, weight_mix, small, up_all, projected, attended, totals, mixed = front(
+    (
+        normed,
+        weight_qkv,
+        mix_rows,
+        small,
+        gains,
+        up_all,
+        projected,
+        attended,
+        totals,
+        middle,
+        normed_two,
+        logits,
+        sent,
+        dispatch,
+    ) = front(
         hidden[0],
-        qkv_weight.reshape(rows_own, 3, seq_count, group_width)
-        .transpose(2, 0, 1, 3)
-        .reshape(seq_count, rows_own, 3 * group_width),
+        qkv_weight,
         out_weight,
-        small,
-        up_rows.reshape(owners, expert_local, capacity, width),
+        out_grad[0],
+        router_weight,
+        attn_gain[None],
+        moe_gain[None],
+        expert_ids[0],
         lengths,
-        experts_all,
+        owners,
+        capacity,
         SPREAD_FIRST if fused else chips,
         0,
     )
     weight_qkv = weight_qkv.reshape(width, 3 * group_width)
-    weight_mix = weight_mix.reshape(width, width)
+    mix_rows = mix_rows.reshape(group_width, width)
     weight_route = small[:, :experts_all]
-    gain_one = small[:, experts_all].astype(jnp.float32)
-    gain_two = small[:, experts_all + 1].astype(jnp.float32)
+    gain_one, gain_two = gains[0], gains[1]
     if not fused:
         up_all = up_all.reshape(expert_local, chips, seq_count, 2 * capacity, width)
         chip, bit = lax.axis_index("fsdp") // 2, 1
@@ -1297,19 +1401,16 @@
         up_all = up_all.reshape(expert_local, chips, seq_count, 2 * capacity, width)
         up_all = up_all.transpose(0, 2, 1, 3, 4)
     inputs = hidden[0].astype(jnp.float32)
-    middle = inputs + times(mixed, weight_mix)
-    normed_two, norm_two_back = jax.vjp(scaled_norm, middle, gain_two)
-    normed_two = normed_two.astype(low)
-    logits = times(normed_two, weight_route)
+    _, norm_two_back = jax.vjp(scaled_norm, middle, gain_two)
+    logits = logits[:, :experts_all]
 
     def gate_of(logit_rows):
         return jnp.sum(jnp.where(choose, jax.nn.softmax(logit_rows, axis=-1), 0.0), axis=-1)
 
     gate, gate_back = jax.vjp(gate_of, logits)
-    sent = times(dispatch, normed_two).astype(low)
     if fused:
         (returned, grad_back), expert_in_grad, expert_out_grad = moe(
-            sent.reshape(owners, expert_local, capacity, width),
+            sent,
             up_all,
             small,
             expert_in,
@@ -1319,7 +1420,7 @@
         )
         returned, grad_back = returned.reshape(slots, width), grad_back.reshape(slots, width)
     else:
-        gate_rows = jnp.sum(jnp.where(hit, gate[None, :], 0.0), axis=1)
+        gate_rows = jnp.sum(jnp.where(dispatch > 0, gate[None, :], 0.0), axis=1)
         gates = lax.all_to_all(
             gate_rows.reshape(owners, expert_local, capacity), "fsdp", split_axis=0, concat_axis=0, tiled=True
         )
@@ -1369,7 +1470,7 @@
         totals,
         normed,
         weight_qkv,
-        weight_mix,
+        mix_rows,
         small_grad,
         lengths,
         owners,

time: 333 us -> 317 us (0.952)
  Pallas kernels: 290 us -> 278 us
  matrix products: 9.18 us -> 2.09 us
    pallas_call x1, Pallas kernels: 73 us -> 63 us  [back(): pl.pallas_call(functools.partial(back_kernel, count, gain_row), out_shape...]
    dot_general x4 -> x0, matrix products: 6.49 us -> none  [times(): return jnp.dot(left, right, preferred_element_type=jnp.float32)]
    pallas_call x1, Pallas kernels: 142 us -> 136 us  [moe(): pl.pallas_call(functools.partial(moe_kernel, chips, cap, experts_all, SPR...]
    pallas_call x1, Pallas kernels: 75.1 us -> 79.3 us  [front(): pl.pallas_call(functools.partial(front_kernel, count, cap, experts_all, s...]
where the time goes in v2:
time: 317 us; the launch traced here: 313 us
  Pallas kernels  278 us (88%)
  other arithmetic  21 us (7%)
  local copies, waits for them, and re-layouts  9.76 us (3%)
    pallas_call x1, Pallas kernels, moe(): pl.pallas_call(functools.partial(moe_kernel, chips, cap, experts_all, SPR...  136 us
    pallas_call x1, Pallas kernels, front(): pl.pallas_call(functools.partial(front_kernel, count, cap, experts_all, s...  79.3 us
    pallas_call x1, Pallas kernels, back(): pl.pallas_call(functools.partial(back_kernel, count, gain_row), out_shape...  63 us
    convert_element_type x1, other arithmetic, shards(): expert_in_grad.astype(jnp.float32)  6.79 us

profile of v2, /device:TPU:0, one launch (start us, length us, event | category | flops | bytes accessed | tf_op | source)
XLA Modules:
  0.0 312.9 jit_solution(1017545937329305364)
XLA Ops:
  1.3 1.4 copy.25.router
  2.7 1.5 copy.26.ids
  4.1 79.3 %shard_map.178 = (bf16[1024,1024]{1,0:T(8,128)(2,1)}, bf16[4,8,32,768]{3,2,1,0:T(8,128)(2,1)}, bf16[4,2,32,1024]{3,2,1,0:T(8,128)(2,1)}, bf16[1024,128]{1,0:T(8,...) custom-call(bf16[256,1024]{1,0:T(8,128)(2,1)} %bitcast.44, ...), custom_call_target="tpu_custom_call" | custom-call | tf_op jit(solution)/shard_map/pallas_call | solution.py:914
  83.4 1.4 multiply_reduce_fusion.2
  84.8 0.8 fusion.22
  85.7 1.0 slice_reduce_fusion
  86.7 1.1 fusion.16
  87.8 136.1 %shard_map.179 = (bf16[2,8,2,32,1024]{4,3,2,1,0:T(8,128)(2,1)}, bf16[2,1024,1024]{2,1,0:T(8,128)(2,1)}, bf16[2,1024,1024]{2,1,0:T(8,128)(2,1)}) custom-call(bf16[8,2,32,1024]{3,2,1,0:T(8,128)(2,1)} %get-tuple-element.33.send_rows, bf16[2,1024,1024]{2,1,0:T(8,128)(2,1)} %get-tuple-element.34.up_rows, bf16[1024,128]{1,0:T(8,128)(2,1)} %get-tuple-element.35.route, ...), custom_call_target="tpu_custom_call" | custom-call | flops 25769803776 | bytes 33554432 | tf_op jit(solution)/shard_map/pallas_call | solution.py:522
  223.9 0.0 copy-start.1
  223.9 0.0 copy-start.5
  223.9 0.0 copy-start.4
  224.0 0.0 copy-start.10
  224.0 0.0 copy-start.6
  224.0 0.0 copy-start
  224.0 1.9 fusion.21
  225.8 0.0 copy-done.1
  225.9 0.0 copy-done.5
  225.9 0.5 fusion
  226.4 0.0 copy-done.4
  226.4 0.0 copy-done.10
  226.4 0.4 fusion.11
  226.8 0.0 copy-done.6
  226.8 0.4 fusion.6
  227.2 0.0 copy-done
  227.2 0.0 copy-start.12
  227.2 0.7 multiply_reduce_fusion
  228.0 1.5 fusion.20
  229.4 0.0 copy-done.12
  229.5 0.0 copy-start.2
  229.5 0.4 fusion.17
  229.9 0.1 pad.6.clone
  229.9 0.1 pad_maximum_fusion
  230.1 0.1 reshape.101
  230.1 0.7 copy.30
  230.8 0.0 copy-start.11
  230.8 63.0 %shard_map.180 = (bf16[256,1024]{1,0:T(8,128)(2,1)}, bf16[4,32,768]{2,1,0:T(8,128)(2,1)}, f32[32,1024]{1,0:T(8,128)}, f32[4,24,128]{2,1,0:T(8,128)}) custom-call(bf16[256,1024]{1,0:T(8,128)(2,1)} %get-tuple-element.57.grad_in, bf16[1024,768]{1,0:T(8,128)(2,1)} %get-tuple-element.38.proj_in, bf16[1024,256]{1,0:T(8,128)(2,1)} %get-tuple-element.39.attended_in, ...), custom_call_target="tpu_custom_call" | custom-call | tf_op jit(solution)/shard_map/pallas_call | solution.py:1250
  293.8 0.0 copy-start.9
  293.8 0.0 copy-start.7
  293.8 0.0 copy-done.2
  293.8 1.4 fusion.1
  295.2 2.3 fusion.4
  297.6 0.0 copy-done.9
  297.6 0.0 copy-done.11
  297.6 0.6 fusion.15
  298.2 0.0 copy-done.7
  298.2 0.2 reshape.109
  298.4 0.3 copy.28
  298.7 0.9 reshape.106
  299.6 0.6 dynamic-slice_bitcast_fusion.1
  300.2 0.7 dynamic-slice_bitcast_fusion
  300.9 0.0 copy-start.3
  300.9 6.8 %convert_element_type.50 = f32[2,1024,1024]{2,1,0:T(8,128)} convert(bf16[2,1024,1024]{2,1,0:T(8,128)(2,1)} %get-tuple-element.49) | non-fusion elementwise | flops 2097152 | bytes 12582912 | tf_op jit(solution)/shard_map/convert_element_type | solution.py:1498
  307.7 0.0 copy-done.3
  307.7 0.0 copy-start.8
  307.7 4.4 %convert_element_type.51 = f32[2,1024,1024]{2,1,0:T(8,128)} convert(bf16[2,1024,1024]{2,1,0:T(8,128)(2,1)S(1)} %copy-done.3) | non-fusion elementwise | flops 2097152 | bytes 12582912 | tf_op jit(solution)/shard_map/convert_element_type | solution.py:1499
  312.1 0.0 copy-done.8
  312.1 0.7 copy.33
  (8 shorter events, 0.1 us)
Async XLA Ops:
  223.9 1.9 copy-start.1
  223.9 1.9 copy-start.5
  223.9 2.5 copy-start.4
  224.0 2.5 copy-start.10
  224.0 2.8 copy-start.6
  224.0 3.3 %copy-start = (f32[256,1024]{1,0:T(8,128)S(1)}, f32[256,1024]{1,0:T(8,128)}, u32[]{:S(2)}) copy-start(f32[256,1024]{1,0:T(8,128)} %get-tuple-element.30) | copy-start | bytes 3145732
  227.2 2.2 copy-start.12
  229.5 64.4 %copy-start.2 = (bf16[1,256,1024]{2,1,0:T(8,128)(2,1)S(1)}, bf16[1,256,1024]{2,1,0:T(8,128)(2,1)}, u32[]{:S(2)}) copy-start(bf16[1,256,1024]{2,1,0:T(8,128)(2,1)} %param.11) | copy-start | bytes 1572868
  230.8 66.8 %copy-start.11 = (bf16[32]{0:T(256)(128)(2,1)S(1)}, bf16[32]{0:T(256)(128)(2,1)}, u32[]{:S(2)}) copy-start(bf16[32]{0:T(256)(128)(2,1)} %param.14) | copy-start | bytes 196
  293.8 3.8 %copy-start.9 = (f32[4,24,128]{2,1,0:T(8,128)S(1)}, f32[4,24,128]{2,1,0:T(8,128)}, u32[]{:S(2)}) copy-start(f32[4,24,128]{2,1,0:T(8,128)} %get-tuple-element.46) | copy-start | bytes 147460
  293.8 4.4 %copy-start.7 = (bf16[4,32,768]{2,1,0:T(8,128)(2,1)S(1)}, bf16[4,32,768]{2,1,0:T(8,128)(2,1)}, u32[]{:S(2)}) copy-start(bf16[4,32,768]{2,1,0:T(8,128)(2,1)} %get-tuple-element.47) | copy-start | bytes 589828
  300.9 6.8 %copy-start.3 = (bf16[2,1024,1024]{2,1,0:T(8,128)(2,1)S(1)}, bf16[2,1024,1024]{2,1,0:T(8,128)(2,1)}, u32[]{:S(2)}) copy-start(bf16[2,1024,1024]{2,1,0:T(8,128)(2,1)} %get-tuple-element.50) | copy-start | bytes 12582916
  307.7 4.4 %copy-start.8 = (f32[32,1024]{1,0:T(8,128)S(1)}, f32[32,1024]{1,0:T(8,128)}, u32[]{:S(2)}) copy-start(f32[32,1024]{1,0:T(8,128)} %get-tuple-element.84) | copy-start | bytes 393220

commit v3 on v2

--- a/solution.py
+++ b/solution.py
@@ -12,6 +12,8 @@
 MASKED = -1e30
 ROOT = 0.7978845608028654
 TILE = 256
+WIDEN = 512
+STEP = 128
 SPREAD_FIRST = 3
 TURN = (1, 3, 2, 0)
 GRAD = 256
@@ -571,7 +573,7 @@
     normed_out, heads_out, mix_out, small_out, gains_out, up, projected_out, attended_out, sums_out,
     middle_out, low_out, logits_out, sent_out, hit_out,
     staged, hid, heads_all, small_own, small_all, gains, normed, proj, attended, sums, acc, stat,
-    mix_all, up_low, rows, hit, mixed, middle, normed_low, logits, sent_rows,
+    mix_all, up_low, rows, hit, mixed, middle, normed_low, logits, sent_rows, pile,
     h_send, h_recv, q_send, q_recv, f_send, f_recv, n_send, n_recv, u_send, u_recv, m_send, m_recv,
     s_send, s_recv, x_send, x_recv, y_send, y_recv, local,
 ):
@@ -682,20 +684,16 @@
     own_hidden = keep(hidden, hid.at[pl.ds(me * tokens, tokens)], 1)
     own_mix = keep(mix, block(0, place), 2)
     own_grad = keep(out_grad, up_low, 13)
-    at_lane = lax.broadcasted_iota(jnp.int32, small_own.shape, 1)
-    square = lax.broadcasted_iota(jnp.int32, (share, share), 0) == lax.broadcasted_iota(jnp.int32, (share, share), 1)
-    stat[:share, :] = jnp.zeros((share, 128), jnp.float32)
-    stat[:share, :experts_all] = router[...].astype(jnp.float32)
-    packed = stat[:share, :]
+    pile[...] = jnp.zeros_like(pile)
+    pile[:experts_all, :share] = router[...].astype(jnp.float32)
     for n, gain in enumerate((gain_a, gain_b)):
-        column = jnp.sum(jnp.where(square, gain[...].astype(jnp.float32), 0.0), axis=1, keepdims=True)
-        packed = jnp.where(at_lane == experts_all + n, column, packed)
-    small_own[...] = packed.astype(small_own.dtype)
+        pile[experts_all + n : experts_all + n + 1, :share] = gain[...].astype(jnp.float32)
+    small_own[...] = jnp.transpose(pile[...])[:share].astype(small_own.dtype)
     send_far(1)
     send_near(1)
     own_small = keep(small_own, block(1, place), 3)
-    chosen = ids[...].astype(jnp.float32)
-    across = jnp.transpose(jnp.broadcast_to(chosen, (tokens, 128)))[:1]
+    across = ids[...].astype(jnp.float32)
+    chosen = jnp.transpose(jnp.broadcast_to(across, (128, tokens)))[:, :1]
     first = lax.broadcasted_iota(jnp.int32, (tokens, tokens), 0)
     second = lax.broadcasted_iota(jnp.int32, (tokens, tokens), 1)
     ranks = jnp.sum(jnp.where((chosen == across) & (first < second), 1.0, 0.0), axis=0, keepdims=True)
@@ -899,7 +897,7 @@
     S, dma, low, f32 = jax.ShapeDtypeStruct, pltpu.SemaphoreType.DMA, jnp.bfloat16, jnp.float32
     chips = count // 2
     tokens, width = hidden.shape
-    experts_all = router.shape[1]
+    experts_all = router.shape[0]
     group = qkv_weight.shape[1] // 12
     share = qkv_weight.shape[0]
     full = 4 * tokens
@@ -953,6 +951,7 @@
             vmem(tokens, width),
             vmem(tokens, lanes, dtype=f32),
             vmem(count, 2, cap, width),
+            vmem(lanes, 128, dtype=f32),
             dma((3, 2)), dma((3, 2)), dma((4, 3)), dma((4, 3)),
             dma((3, chips)), dma((3, chips)), dma((3, chips)), dma((3, chips)),
             dma((chips, 2)), dma((chips, 2)), dma((3, 2)), dma((3, 2)),
@@ -964,9 +963,29 @@
     )(hidden, qkv_weight, mix, out_grad, router, gain_a, gain_b, ids, lengths)
 
 
+def widen_kernel(one, two, one_out, two_out):
+    one_out[...] = one[...].astype(one_out.dtype)
+    two_out[...] = two[...].astype(two_out.dtype)
+
+
+def widen(one, two):
+    steps = one.shape[1] // WIDEN
+    blocks = [pl.BlockSpec((1, WIDEN, x.shape[2]), lambda a, b: (a, b, 0)) for x in (one, two)]
+    return pl.pallas_call(
+        widen_kernel,
+        out_shape=tuple(jax.ShapeDtypeStruct(x.shape, jnp.float32) for x in (one, two)),
+        grid=(one.shape[0], steps),
+        in_specs=blocks,
+        out_specs=blocks,
+        compiler_params=pltpu.CompilerParams(vmem_limit_bytes=48 * 2**20),
+    )(one, two)
+
+
 def back_kernel(
-    count, gain_row, grad_in, proj_in, attended_in, sums_in, normed_in, heads_in, mix_in, small_in, length,
-    normed_out, heads_out, mix_out, small_out,
+    count, experts_all, ret_in, hit_in, middle_in, logits_in, low_in, out_grad, small_all, gains_in, hidden_in,
+    proj_in, attended_in, sums_in, normed_in, heads_in, mix_in, ids, length,
+    output_out, input_out, heads_out, mix_out, small_out,
+    ret, hit, middle, logits, normed_two, up_low, route, gains, hid, output, grad_middle, grad_in, grad_logits, grad_two,
     grads, proj, attended, sums, normed, heads, mix, small, grad_heads, delta, masked_grad, masked_query,
     masked_key, masked_value, probs, slopes, grad_query, grad_key, grad_value, grad_proj, part, weights, weights_mix, gain_sum,
     sib_a, sib_b, sib_c, own_a, own_b, own_c, got_a, got_b, got_c, total_a, total_b, total_c, first, second,
@@ -979,6 +998,7 @@
     chip, core = place // 2, lax.rem(place, 2)
     sibling = place ^ 1
     tokens, width = grad_in.shape
+    gain_row = experts_all
     group = attended.shape[1]
     share = weights.shape[0] // (4 * count)
     heads_local = group // HEAD_DIM
@@ -998,6 +1018,66 @@
         copy.start()
         return copy
 
+    heads_of = [
+        local(source, to, load.at[9 + i])
+        for i, (source, to) in enumerate(
+            (
+                (hit_in, hit),
+                (ret_in, ret),
+                (middle_in, middle),
+                (logits_in, logits),
+                (low_in, normed_two),
+                (out_grad, up_low),
+                (small_all, route),
+                (gains_in, gains),
+                (hidden_in, hid),
+            )
+        )
+    ]
+    loads = [
+        local(source, to, load.at[1 + i])
+        for i, (source, to) in enumerate(
+            (
+                (proj_in, proj),
+                (attended_in, attended),
+                (sums_in, sums),
+                (mix_in, mix),
+                (heads_in, heads),
+                (normed_in, normed),
+            )
+        )
+    ]
+    for copy in heads_of:
+        copy.wait()
+    small[...] = jnp.zeros_like(small)
+    grad_two[...] = jnp.zeros_like(grad_two)
+    lane = lax.broadcasted_iota(jnp.int32, (STEP, route.shape[1]), 1)
+    chosen = jnp.transpose(jnp.broadcast_to(ids[...].astype(jnp.float32), (128, tokens)))[:, :1].astype(jnp.int32)
+    for t in range(tokens // STEP):
+        span = slice(t * STEP, (t + 1) * STEP)
+        position = me * tokens + t * STEP + lax.broadcasted_iota(jnp.int32, (STEP, 1), 0)
+        valid = jnp.where(position < length[0], 1.0, 0.0)
+        scores = jnp.where(lane < experts_all, logits[span, :], MASKED)
+        powers = jnp.exp(scores - jnp.max(scores, axis=1, keepdims=True))
+        share_of = powers / jnp.sum(powers, axis=1, keepdims=True)
+        choose = lane == chosen[span]
+        gate = jnp.sum(jnp.where(choose, share_of, 0.0), axis=1, keepdims=True)
+        back_rows = transposed_times(hit[:, span], ret[0])
+        value = middle[span, :]
+        output[span, :] = (valid * (value + gate * back_rows)).astype(low)
+        upstream = valid * up_low[span, :].astype(jnp.float32)
+        grad_gate = jnp.sum(upstream * back_rows, axis=1, keepdims=True)
+        slope = grad_gate * gate * (jnp.where(choose, 1.0, 0.0) - share_of)
+        grad_logits[span, :] = slope.astype(low)
+        incoming = times_transposed(grad_logits[span, :], route[...]) + transposed_times(hit[:, span], ret[1])
+        scale = lax.rsqrt(jnp.mean(value * value, axis=-1, keepdims=True) + EPS)
+        shrunk = value * scale
+        grad_two[...] += jnp.sum(incoming * shrunk, axis=0, keepdims=True)
+        scaled = incoming * gains[1:2, :]
+        total = upstream + scale * (scaled - shrunk * jnp.mean(scaled * shrunk, axis=-1, keepdims=True))
+        grad_middle[span, :] = total
+        grad_in[span, :] = total.astype(low)
+    output_kept = local(output, output_out, load.at[8])
     own_grad = local(grad_in, grads.at[pl.ds(me * tokens, tokens)], load.at[0])
     half = tokens // 2
     direct = {}
@@ -1008,20 +1088,11 @@
                 "seq", peer, grad_in.at[pl.ds(p * half, half)], grads.at[pl.ds(me * tokens + p * half, half)],
                 g_send.at[side, p], g_recv.at[side, p],
             )
-    loads = [
-        local(source, to, load.at[1 + i])
-        for i, (source, to) in enumerate(
-            (
-                (proj_in, proj),
-                (attended_in, attended),
-                (sums_in, sums),
-                (mix_in, mix),
-                (heads_in, heads),
-                (normed_in, normed),
-                (small_in, small),
-            )
-        )
-    ]
+    for n in range(width // 128):
+        lanes = slice(n * 128, (n + 1) * 128)
+        kinds = transposed_times(grad_logits[...], normed_two[:, lanes])
+        small[n // 2, n % 2, :experts_all, :] = kinds[:experts_all]
+        small[n // 2, n % 2, gain_row + 1 : gain_row + 2, :] = grad_two[:, lanes]
     for copy in loads:
         copy.wait()
     head_of = lax.broadcasted_iota(jnp.int32, (tokens, group), 1) // HEAD_DIM
@@ -1193,12 +1264,19 @@
         rows = slice(side * half, (side + 1) * half)
         summed[side, 1].wait_recv()
         summed[side, 2].wait_recv()
-        first[side, 1] = (
+        incoming = (
             part[me, rows, :].astype(jnp.float32)
             + first[side, 1].astype(jnp.float32)
             + second[side].astype(jnp.float32)
-        ).astype(low)
-        stored.append(local(first.at[side, 1], normed_out.at[pl.ds(side * half, half)], keep.at[side]))
+        )
+        value = hid[rows, :].astype(jnp.float32)
+        scale = lax.rsqrt(jnp.mean(value * value, axis=-1, keepdims=True) + EPS)
+        shrunk = value * scale
+        scaled = incoming * gains[0:1, :]
+        grad_middle[rows, :] += scale * (scaled - shrunk * jnp.mean(scaled * shrunk, axis=-1, keepdims=True))
+        stored.append(
+            local(grad_middle.at[pl.ds(side * half, half)], input_out.at[pl.ds(side * half, half)], keep.at[side])
+        )
     for a in (1, 0, 2):
         if a == 0:
             for s in range(4):
@@ -1220,7 +1298,7 @@
             crossed.append(remote("seq", peer, totals[a].at[peer], out.at[me], x_send.at[a, i], x_recv.at[a, i]))
         stored.append(local(totals[a].at[me], out.at[me], keep.at[3 + a // 2]))
     stored.append(local(total_b, mix_out, keep.at[2]))
-    for copy in (*stored, *crossed):
+    for copy in (*stored, *crossed, output_kept):
         copy.wait()
     for copy in (*summed.values(), *away.values(), *direct.values()):
         copy.wait_send()
@@ -1229,15 +1307,18 @@
             copy.wait_send()
 
 
-def back(grad, proj, attended, sums, normed, heads, mix, small, lengths, count, gain_row, number):
+def back(
+    ret, hit, middle, logits, normed_two, out_grad, route, gains, hidden,
+    proj, attended, sums, normed, heads, mix, ids, lengths, count, experts_all, number,
+):
     S, dma, f32, low = jax.ShapeDtypeStruct, pltpu.SemaphoreType.DMA, jnp.float32, jnp.bfloat16
-    tokens, width = grad.shape
+    tokens, width = out_grad.shape
     group = attended.shape[1]
     chips = count // 2
     full = 4 * tokens
     share = width // (4 * count)
     local_heads = group // HEAD_DIM
-    kinds = small.shape[2]
+    kinds = -(-(experts_all + 2) // 8) * 8
 
     def vmem(*shape, dtype=low):
         return pltpu.VMEM(shape, dtype)
@@ -1248,16 +1329,31 @@
         vmem(chips, 4, kinds, 128, dtype=f32),
     ]
     return pl.pallas_call(
-        functools.partial(back_kernel, count, gain_row),
+        functools.partial(back_kernel, count, experts_all),
         out_shape=(
             S((tokens, width), low),
+            S((tokens, width), f32),
             S((4, share, 3 * group), low),
             S((share, width), f32),
             S((4, kinds, 128), f32),
         ),
-        in_specs=[ANY] * 8 + [pl.BlockSpec(memory_space=pltpu.SMEM)],
-        out_specs=(ANY,) * 4,
+        in_specs=[ANY] * 15 + [pl.BlockSpec(memory_space=pltpu.VMEM), pl.BlockSpec(memory_space=pltpu.SMEM)],
+        out_specs=(ANY,) * 5,
         scratch_shapes=[
+            vmem(*ret.shape),
+            vmem(*hit.shape),
+            vmem(tokens, width, dtype=f32),
+            vmem(*logits.shape, dtype=f32),
+            vmem(tokens, width),
+            vmem(tokens, width),
+            vmem(*route.shape),
+            vmem(*gains.shape, dtype=f32),
+            vmem(tokens, width),
+            vmem(tokens, width),
+            vmem(tokens, width, dtype=f32),
+            vmem(tokens, width),
+            vmem(*logits.shape),
+            vmem(1, width, dtype=f32),
             vmem(full, width),
             vmem(*proj.shape),
             vmem(*attended.shape),
@@ -1265,7 +1361,7 @@
             vmem(*normed.shape),
             vmem(*heads.shape),
             vmem(group, width),
-            vmem(*small.shape, dtype=f32),
+            vmem(4, group // 128, kinds, 128, dtype=f32),
             vmem(tokens, group),
             vmem(8, tokens, dtype=f32),
             vmem(local_heads * tokens, group),
@@ -1293,12 +1389,15 @@
             dma((3, 2)), dma((3, 2)),
             dma((2, chips)), dma((2, chips)), dma((4, chips)), dma((4, chips)),
             dma((7, chips)), dma((7, chips)),
-            dma((3, 3)), dma((3, 3)), dma((3, 2)), dma((3, 2)), dma((8,)), dma((5,)),
+            dma((3, 3)), dma((3, 3)), dma((3, 2)), dma((3, 2)), dma((18,)), dma((5,)),
         ],
         compiler_params=pltpu.CompilerParams(
             collective_id=number, has_side_effects=True, vmem_limit_bytes=60 * 2**20
         ),
-    )(grad, proj, attended, sums, normed, heads, mix, small, lengths)
+    )(
+        ret, hit, middle, logits, normed_two, out_grad, route, gains, hidden,
+        proj, attended, sums, normed, heads, mix, ids, lengths,
+    )
 
 
 def shards(
@@ -1317,22 +1416,18 @@
     S = jax.ShapeDtypeStruct
     low = jnp.bfloat16
     owners = lax.axis_size("fsdp")
-    seq_place = lax.axis_index("seq")
     seq_count = lax.axis_size("seq")
     tokens, width = hidden.shape[1], hidden.shape[2]
     full_len = tokens * seq_count
     group_width = width // seq_count
     rows_own = qkv_weight.shape[0]
-    length = lengths[0]
     experts_all = router_weight.shape[1]
     expert_local = expert_in.shape[0]
     capacity = -(-max(2, 2 * tokens // experts_all) // 16) * 16
     slots = experts_all * capacity
 
-    position = seq_place * tokens + jnp.arange(tokens, dtype=jnp.int32)
-    valid = (position < length).astype(jnp.float32)[:, None]
     chosen = expert_ids[0, :, 0]
-    choose = chosen[:, None] == jnp.arange(experts_all, dtype=jnp.int32)[None, :]
+
     def to_owners(rows, number):
         return exchange(
             "fsdp",
@@ -1353,8 +1448,6 @@
             number,
         )[0].reshape(slots, width)
 
-    upstream_low = jnp.where(valid > 0, out_grad[0], 0).astype(low)
-    upstream = upstream_low.astype(jnp.float32)
     chips = owners // 2
     fused = 4 * owners * capacity <= 1024
     (
@@ -1377,10 +1470,10 @@
         qkv_weight,
         out_weight,
         out_grad[0],
-        router_weight,
+        router_weight.T,
         attn_gain[None],
         moe_gain[None],
-        expert_ids[0],
+        expert_ids[0].T,
         lengths,
         owners,
         capacity,
@@ -1389,8 +1482,6 @@
     )
     weight_qkv = weight_qkv.reshape(width, 3 * group_width)
     mix_rows = mix_rows.reshape(group_width, width)
-    weight_route = small[:, :experts_all]
-    gain_one, gain_two = gains[0], gains[1]
     if not fused:
         up_all = up_all.reshape(expert_local, chips, seq_count, 2 * capacity, width)
         chip, bit = lax.axis_index("fsdp") // 2, 1
@@ -1400,16 +1491,8 @@
             bit *= 2
         up_all = up_all.reshape(expert_local, chips, seq_count, 2 * capacity, width)
         up_all = up_all.transpose(0, 2, 1, 3, 4)
-    inputs = hidden[0].astype(jnp.float32)
-    _, norm_two_back = jax.vjp(scaled_norm, middle, gain_two)
-    logits = logits[:, :experts_all]
-
-    def gate_of(logit_rows):
-        return jnp.sum(jnp.where(choose, jax.nn.softmax(logit_rows, axis=-1), 0.0), axis=-1)
-
-    gate, gate_back = jax.vjp(gate_of, logits)
     if fused:
-        (returned, grad_back), expert_in_grad, expert_out_grad = moe(
+        returned, *expert_grads = moe(
             sent,
             up_all,
             small,
@@ -1418,8 +1501,12 @@
             experts_all,
             5,
         )
-        returned, grad_back = returned.reshape(slots, width), grad_back.reshape(slots, width)
+        expert_in_grad, expert_out_grad = widen(*expert_grads)
+        returned = returned.reshape(2, slots, width)
     else:
+        choose = chosen[:, None] == jnp.arange(experts_all, dtype=jnp.int32)[None, :]
+        weights = jax.nn.softmax(logits[:, :experts_all], axis=-1)
+        gate = jnp.sum(jnp.where(choose, weights, 0.0), axis=-1)
         gate_rows = jnp.sum(jnp.where(dispatch > 0, gate[None, :], 0.0), axis=1)
         gates = lax.all_to_all(
             gate_rows.reshape(owners, expert_local, capacity), "fsdp", split_axis=0, concat_axis=0, tiled=True
@@ -1449,29 +1536,24 @@
         shape = (expert_local, seq_count, owners * capacity, width)
         returned = to_sources(collect(partial_out.reshape(shape), 7), 8)
         grad_back = to_sources(collect(partial_back.reshape(shape), 9), 10)
-
-    back_rows = transposed_times(dispatch, returned)
-    output = valid * (middle + gate[:, None] * back_rows)
-    grad_gate = jnp.sum(upstream * back_rows, axis=1)
-    grad_logits = gate_back(grad_gate)[0].astype(low)
-    grad_normed_two = times_transposed(grad_logits, weight_route) + transposed_times(dispatch, grad_back)
-    grad_middle, grad_gain_two = norm_two_back(grad_normed_two)
-    grad_middle = grad_middle + upstream
-    grad_attn = grad_middle.astype(low)
-
-    small_grad = jnp.concatenate([transposed_times(grad_logits, normed_two), jnp.zeros((1, width)), grad_gain_two[None]])
-    small_grad = jnp.pad(small_grad, ((0, -small_grad.shape[0] % 8), (0, 0)))
-    kinds = small_grad.shape[0]
-    small_grad = small_grad.reshape(kinds, seq_count, group_width // 128, 128).transpose(1, 2, 0, 3)
-    grad_normed, qkv_sum, mix_grad, small_sum = back(
-        grad_attn,
+        returned = jnp.stack([returned, grad_back])
+    output, grad_inputs, qkv_sum, mix_grad, small_sum = back(
+        returned,
+        dispatch,
+        middle,
+        logits,
+        normed_two,
+        out_grad[0],
+        small,
+        gains,
+        hidden[0],
         projected,
         attended,
         totals,
         normed,
         weight_qkv,
         mix_rows,
-        small_grad,
+        expert_ids[0].T,
         lengths,
         owners,
         experts_all,
@@ -1485,18 +1567,16 @@
     )
     start = lax.axis_index("fsdp") * rows_own % 128
     small_sum = lax.dynamic_slice_in_dim(jnp.sum(small_sum, axis=0), start, rows_own, 1)
-    _, norm_back = jax.vjp(scaled_norm, inputs, gain_one)
-    grad_inputs = norm_back(grad_normed.astype(jnp.float32))[0] + grad_middle
     return (
-        output.astype(low)[None],
+        output[None],
         grad_inputs[None],
         small_sum[experts_all] / attn_gain.astype(jnp.float32),
         qkv_weight_grad,
         mix_grad,
         small_sum[experts_all + 1],
         small_sum[:experts_all].T,
-        expert_in_grad.astype(jnp.float32),
-        expert_out_grad.astype(jnp.float32),
+        expert_in_grad,
+        expert_out_grad,
     )
 
 

time: 317 us -> 306 us (0.965)
  other arithmetic: 21 us -> 1.39 us
  Pallas kernels: 278 us -> 291 us
    convert_element_type x4 -> x0, other arithmetic: 12.7 us -> none  [the longest x1 6.79 us: shards(): expert_in_grad.astype(jnp.float32)]
    pallas_call x1 -> x2, Pallas kernels: 63 us -> 75.5 us  [the longest x1 67.8 us: back(): pl.pallas_call(functools.partial(back_kernel, count, experts_all), out_sh...]
    reduce_sum x4 -> x0, other arithmetic: 4.22 us -> none  [the longest x2 2.77 us: scaled_norm(): jnp.mean(value * value, axis=-1, keepdims=True) + EPS]
where the time goes in v3:
time: 306 us; the launch traced here: 302 us
  Pallas kernels  291 us (95%)
  local copies, waits for them, and re-layouts  8.21 us (3%)
    pallas_call x1, Pallas kernels, moe(): pl.pallas_call(functools.partial(moe_kernel, chips, cap, experts_all, SPR...  136 us
    pallas_call x1, Pallas kernels, front(): pl.pallas_call(functools.partial(front_kernel, count, cap, experts_all, s...  79.1 us
    pallas_call x1, Pallas kernels, back(): pl.pallas_call(functools.partial(back_kernel, count, experts_all), out_sh...  67.8 us
    pallas_call x1, Pallas kernels, widen(): pl.pallas_call(widen_kernel, out_shape=tuple((jax.ShapeDtypeStruct(x.shap...  7.67 us

profile of v3, /device:TPU:0, one launch (start us, length us, event | category | flops | bytes accessed | tf_op | source)
XLA Modules:
  0.0 301.8 jit_solution(7262613304173866366)
XLA Ops:
  1.3 79.1 %shard_map.178 = (bf16[1024,1024]{1,0:T(8,128)(2,1)}, bf16[4,8,32,768]{3,2,1,0:T(8,128)(2,1)}, bf16[4,2,32,1024]{3,2,1,0:T(8,128)(2,1)}, bf16[1024,128]{1,0:T(8,...) custom-call(bf16[256,1024]{1,0:T(8,128)(2,1)} %bitcast.20, ...), custom_call_target="tpu_custom_call" | custom-call | tf_op jit(solution)/shard_map/pallas_call | solution.py:912
  80.4 136.1 %shard_map.179 = (bf16[2,8,2,32,1024]{4,3,2,1,0:T(8,128)(2,1)}, bf16[2,1024,1024]{2,1,0:T(8,128)(2,1)}, bf16[2,1024,1024]{2,1,0:T(8,128)(2,1)}) custom-call(bf16[8,2,32,1024]{3,2,1,0:T(8,128)(2,1)} %get-tuple-element.33.send_rows, bf16[2,1024,1024]{2,1,0:T(8,128)(2,1)} %get-tuple-element.34.up_rows, bf16[1024,128]{1,0:T(8,128)(2,1)} %get-tuple-element.35.route.small_all, ...), custom_call_target="tpu_custom_call" | custom-call | flops 25769803776 | bytes 33554432 | tf_op jit(solution)/shard_map/pallas_call | solution.py:524
  216.5 0.0 copy-start.4
  216.5 67.8 %shard_map.180 = (bf16[256,1024]{1,0:T(8,128)(2,1)}, f32[256,1024]{1,0:T(8,128)}, bf16[4,32,768]{2,1,0:T(8,128)(2,1)}, f32[32,1024]{1,0:T(8,128)}, f32[4,24,128]{2,1,0:T(8,128)}) custom-call(bf16[2,512,1024]{2,1,0:T(8,128)(2,1)} %bitcast.25, bf16[512,256]{1,0:T(8,128)(2,1)} %get-tuple-element.37.hit_in, f32[256,1024]{1,0:T(8,128)} %get-tuple-element.38.middle_in, ...), custom_call_target="tpu_custom_call" | custom-call | tf_op jit(solution)/shard_map/pallas_call | solution.py:1331
  284.4 0.8 reduce_sum.9
  285.2 0.6 dynamic-slice_bitcast_fusion.1
  285.8 0.0 copy-done.4
  285.8 0.6 fusion
  286.3 0.7 dynamic-slice_bitcast_fusion
  287.0 1.1 reshape.47
  288.1 0.3 copy.21
  288.4 0.9 reshape.44
  289.4 0.0 copy-start
  289.4 2.2 copy-done
  291.5 0.0 copy-start.2
  291.6 0.0 copy-start.1
  291.6 0.0 copy-start.3
  291.6 7.7 %shard_map.181 = (f32[2,1024,1024]{2,1,0:T(8,128)}, f32[2,1024,1024]{2,1,0:T(8,128)}) custom-call(bf16[2,1024,1024]{2,1,0:T(8,128)(2,1)S(1)} %copy-done, bf16[2,1024,1024]{2,1,0:T(8,128)(2,1)} %get-tuple-element.54.two), custom_call_target="tpu_custom_call" | custom-call | tf_op jit(solution)/shard_map/pallas_call | solution.py:974
  299.2 0.0 copy-done.2
  299.2 0.8 copy.26
  300.0 0.0 copy-done.1
  300.0 1.0 copy.27
  301.0 0.0 copy-done.3
  301.0 0.7 copy.28
Async XLA Ops:
  216.5 69.2 %copy-start.4 = (bf16[32]{0:T(256)(128)(2,1)S(1)}, bf16[32]{0:T(256)(128)(2,1)}, u32[]{:S(2)}) copy-start(bf16[32]{0:T(256)(128)(2,1)} %param.14) | copy-start | bytes 196
  289.4 2.2 copy-start
  291.5 7.7 %copy-start.2 = (bf16[256,1024]{1,0:T(8,128)(2,1)S(1)}, bf16[256,1024]{1,0:T(8,128)(2,1)}, u32[]{:S(2)}) copy-start(bf16[256,1024]{1,0:T(8,128)(2,1)} %get-tuple-element.48) | copy-start | bytes 1572868
  291.6 8.5 %copy-start.1 = (f32[256,1024]{1,0:T(8,128)S(1)}, f32[256,1024]{1,0:T(8,128)}, u32[]{:S(2)}) copy-start(f32[256,1024]{1,0:T(8,128)} %get-tuple-element.49) | copy-start | bytes 3145732
  291.6 9.4 %copy-start.3 = (f32[32,1024]{1,0:T(8,128)S(1)}, f32[32,1024]{1,0:T(8,128)}, u32[]{:S(2)}) copy-start(f32[32,1024]{1,0:T(8,128)} %get-tuple-element.70) | copy-start | bytes 393220

commit v4 on v3

--- a/solution.py
+++ b/solution.py
@@ -12,7 +12,6 @@
 MASKED = -1e30
 ROOT = 0.7978845608028654
 TILE = 256
-WIDEN = 512
 STEP = 128
 SPREAD_FIRST = 3
 TURN = (1, 3, 2, 0)
@@ -963,22 +962,69 @@
     )(hidden, qkv_weight, mix, out_grad, router, gain_a, gain_b, ids, lengths)
 
 
-def widen_kernel(one, two, one_out, two_out):
-    one_out[...] = one[...].astype(one_out.dtype)
-    two_out[...] = two[...].astype(two_out.dtype)
-
-
-def widen(one, two):
-    steps = one.shape[1] // WIDEN
-    blocks = [pl.BlockSpec((1, WIDEN, x.shape[2]), lambda a, b: (a, b, 0)) for x in (one, two)]
+def finish_kernel(
+    experts_all, experts, output, input_grad, heads, mix, small, gain, *refs
+):
+    wide, refs = refs[:experts], refs[experts:]
+    output_out, input_out, heads_out, mix_out, route_out, gain_a, gain_b = refs[:7]
+    wide_out, kinds = refs[7 : 7 + experts], refs[7 + experts]
+    for source, target in zip(wide, wide_out):
+        target[...] = source[...].astype(target.dtype)
+    output_out[...] = output[...]
+    input_out[...] = input_grad[...]
+    heads_out[...] = heads[...].astype(heads_out.dtype)
+    mix_out[...] = mix[...]
+
+    @pl.when(pl.program_id(0) == 0)
+    def _():
+        share = route_out.shape[1]
+        start = lax.rem(lax.axis_index("fsdp") * share, 128)
+        total = small[0] + small[1] + small[2] + small[3]
+        own = jnp.zeros((total.shape[0], share), jnp.float32)
+        for place in range(0, 128, share):
+            own = own + jnp.where(start == place, total[:, place : place + share], 0.0)
+        kinds[...] = own
+        route_out[...] = kinds[:experts_all]
+        gain_a[...] = kinds[experts_all : experts_all + 1] / gain[...].astype(jnp.float32)
+        gain_b[...] = kinds[experts_all + 1 : experts_all + 2]
+
+
+def finish(output, input_grad, heads, mix, small, gain, experts_all, wide):
+    S, f32 = jax.ShapeDtypeStruct, jnp.float32
+    steps = 8
+    share = heads.shape[0]
+
+    def part(x, dim):
+        shape = tuple(size // steps if d == dim else size for d, size in enumerate(x.shape))
+        return pl.BlockSpec(shape, lambda n: tuple(n if d == dim else 0 for d in range(len(shape))))
+
+    def same(*shape):
+        return pl.BlockSpec(shape, lambda n: (0,) * len(shape))
+
+    halves = [pl.BlockSpec((1, x.shape[1] * 2 // steps, x.shape[2]), lambda n: (n // (steps // 2), n % (steps // 2), 0)) for x in wide]
     return pl.pallas_call(
-        widen_kernel,
-        out_shape=tuple(jax.ShapeDtypeStruct(x.shape, jnp.float32) for x in (one, two)),
-        grid=(one.shape[0], steps),
-        in_specs=blocks,
-        out_specs=blocks,
-        compiler_params=pltpu.CompilerParams(vmem_limit_bytes=48 * 2**20),
-    )(one, two)
+        functools.partial(finish_kernel, experts_all, len(wide)),
+        grid=(steps,),
+        out_shape=(
+            S(output.shape, output.dtype),
+            S(input_grad.shape, f32),
+            S(heads.shape, f32),
+            S(mix.shape, f32),
+            S((experts_all, share), f32),
+            S((1, share), f32),
+            S((1, share), f32),
+            *(S(x.shape, f32) for x in wide),
+        ),
+        in_specs=[
+            part(output, 0), part(input_grad, 0), part(heads, 1), part(mix, 1), same(*small.shape), same(1, share), *halves
+        ],
+        out_specs=(
+            part(output, 0), part(input_grad, 0), part(heads, 1), part(mix, 1),
+            same(experts_all, share), same(1, share), same(1, share), *halves,
+        ),
+        scratch_shapes=[pltpu.VMEM((small.shape[1], share), f32)],
+        compiler_params=pltpu.CompilerParams(vmem_limit_bytes=60 * 2**20),
+    )(output, input_grad, heads, mix, small, gain, *wide)
 
 
 def back_kernel(
@@ -989,7 +1035,7 @@
     grads, proj, attended, sums, normed, heads, mix, small, grad_heads, delta, masked_grad, masked_query,
     masked_key, masked_value, probs, slopes, grad_query, grad_key, grad_value, grad_proj, part, weights, weights_mix, gain_sum,
     sib_a, sib_b, sib_c, own_a, own_b, own_c, got_a, got_b, got_c, total_a, total_b, total_c, first, second,
-    g_send, g_recv, b_send, b_recv, bb_send, bb_recv, z_send, z_recv, x_send, x_recv, c_send, c_recv, load, keep,
+    g_send, g_recv, b_send, b_recv, bb_send, bb_recv, z_send, z_recv, x_send, x_recv, w_send, w_recv, c_send, c_recv, load, keep,
 ):
     me, place = lax.axis_index("seq"), lax.axis_index("fsdp")
     one, two, both = me ^ 1, me ^ 2, me ^ 3
@@ -1293,10 +1339,17 @@
                 total = total + got[a][k].astype(jnp.float32)
             totals[a][...] = total
     crossed = []
-    for a, out in ((0, heads_out), (2, small_out)):
+    for p in range(3):
+        lanes = pl.ds(p * group, group)
+        target = heads_out.at[:, pl.ds(pl.multiple_of((p * 4 + me) * group, group), group)]
         for i, peer in enumerate(others):
-            crossed.append(remote("seq", peer, totals[a].at[peer], out.at[me], x_send.at[a, i], x_recv.at[a, i]))
-        stored.append(local(totals[a].at[me], out.at[me], keep.at[3 + a // 2]))
+            crossed.append(
+                remote("seq", peer, total_a.at[peer, :, lanes], target, w_send.at[p, i], w_recv.at[p, i])
+            )
+        stored.append(local(total_a.at[me, :, lanes], target, load.at[18 + p]))
+    for i, peer in enumerate(others):
+        crossed.append(remote("seq", peer, total_c.at[peer], small_out.at[me], x_send.at[i], x_recv.at[i]))
+    stored.append(local(total_c.at[me], small_out.at[me], keep.at[3]))
     stored.append(local(total_b, mix_out, keep.at[2]))
     for copy in (*stored, *crossed, output_kept):
         copy.wait()
@@ -1333,7 +1386,7 @@
         out_shape=(
             S((tokens, width), low),
             S((tokens, width), f32),
-            S((4, share, 3 * group), low),
+            S((share, 12 * group), low),
             S((share, width), f32),
             S((4, kinds, 128), f32),
         ),
@@ -1389,7 +1442,7 @@
             dma((3, 2)), dma((3, 2)),
             dma((2, chips)), dma((2, chips)), dma((4, chips)), dma((4, chips)),
             dma((7, chips)), dma((7, chips)),
-            dma((3, 3)), dma((3, 3)), dma((3, 2)), dma((3, 2)), dma((18,)), dma((5,)),
+            dma((3,)), dma((3,)), dma((3, 3)), dma((3, 3)), dma((3, 2)), dma((3, 2)), dma((21,)), dma((5,)),
         ],
         compiler_params=pltpu.CompilerParams(
             collective_id=number, has_side_effects=True, vmem_limit_bytes=60 * 2**20
@@ -1420,7 +1473,6 @@
     tokens, width = hidden.shape[1], hidden.shape[2]
     full_len = tokens * seq_count
     group_width = width // seq_count
-    rows_own = qkv_weight.shape[0]
     experts_all = router_weight.shape[1]
     expert_local = expert_in.shape[0]
     capacity = -(-max(2, 2 * tokens // experts_all) // 16) * 16
@@ -1501,7 +1553,6 @@
             experts_all,
             5,
         )
-        expert_in_grad, expert_out_grad = widen(*expert_grads)
         returned = returned.reshape(2, slots, width)
     else:
         choose = chosen[:, None] == jnp.arange(experts_all, dtype=jnp.int32)[None, :]
@@ -1536,7 +1587,7 @@
         shape = (expert_local, seq_count, owners * capacity, width)
         returned = to_sources(collect(partial_out.reshape(shape), 7), 8)
         grad_back = to_sources(collect(partial_back.reshape(shape), 9), 10)
-        returned = jnp.stack([returned, grad_back])
+        returned, expert_grads = jnp.stack([returned, grad_back]), ()
     output, grad_inputs, qkv_sum, mix_grad, small_sum = back(
         returned,
         dispatch,
@@ -1559,22 +1610,19 @@
         experts_all,
         12,
     )
-    qkv_weight_grad = (
-        qkv_sum.astype(jnp.float32)
-        .reshape(seq_count, rows_own, 3, group_width)
-        .transpose(1, 2, 0, 3)
-        .reshape(rows_own, 3 * width)
+    output, grad_inputs, qkv_grad, mix_grad, route_grad, gain_one_grad, gain_two_grad, *wide = finish(
+        output, grad_inputs, qkv_sum, mix_grad, small_sum, attn_gain[None], experts_all, expert_grads
     )
-    start = lax.axis_index("fsdp") * rows_own % 128
-    small_sum = lax.dynamic_slice_in_dim(jnp.sum(small_sum, axis=0), start, rows_own, 1)
+    if fused:
+        expert_in_grad, expert_out_grad = wide
     return (
         output[None],
         grad_inputs[None],
-        small_sum[experts_all] / attn_gain.astype(jnp.float32),
-        qkv_weight_grad,
+        gain_one_grad[0],
+        qkv_grad,
         mix_grad,
-        small_sum[experts_all + 1],
-        small_sum[:experts_all].T,
+        gain_two_grad[0],
+        route_grad.T,
         expert_in_grad,
         expert_out_grad,
     )

time: 306 us -> 301 us (0.984)
  local copies, waits for them, and re-layouts: 8.21 us -> 0 us
  Pallas kernels: 291 us -> 295 us
    unnamed x13 -> x0, local copies, waits for them, and re-layouts: 4.62 us -> none
    pallas_call x1, Pallas kernels: 7.67 us -> 11.8 us  [finish(): pl.pallas_call(functools.partial(finish_kernel, experts_all, len(wide)),...]
where the time goes in v4:
time: 301 us; the launch traced here: 297 us
  Pallas kernels  295 us (98%)
    pallas_call x1, Pallas kernels, moe(): pl.pallas_call(functools.partial(moe_kernel, chips, cap, experts_all, SPR...  136 us
    pallas_call x1, Pallas kernels, front(): pl.pallas_call(functools.partial(front_kernel, count, cap, experts_all, s...  79.1 us
    pallas_call x1, Pallas kernels, back(): pl.pallas_call(functools.partial(back_kernel, count, experts_all), out_sh...  67.9 us
    pallas_call x1, Pallas kernels, finish(): pl.pallas_call(functools.partial(finish_kernel, experts_all, len(wide)),...  11.8 us

profile of v4, /device:TPU:0, one launch (start us, length us, event | category | flops | bytes accessed | tf_op | source)
XLA Modules:
  0.0 296.6 jit_solution(10021418777107700964)
XLA Ops:
  1.3 79.1 %shard_map.178 = (bf16[1024,1024]{1,0:T(8,128)(2,1)}, bf16[4,8,32,768]{3,2,1,0:T(8,128)(2,1)}, bf16[4,2,32,1024]{3,2,1,0:T(8,128)(2,1)}, bf16[1024,128]{1,0:T(8,...) custom-call(bf16[256,1024]{1,0:T(8,128)(2,1)} %bitcast.14, ...), custom_call_target="tpu_custom_call" | custom-call | tf_op jit(solution)/shard_map/pallas_call | solution.py:911
  80.4 136.1 %shard_map.179 = (bf16[2,8,2,32,1024]{4,3,2,1,0:T(8,128)(2,1)}, bf16[2,1024,1024]{2,1,0:T(8,128)(2,1)}, bf16[2,1024,1024]{2,1,0:T(8,128)(2,1)}) custom-call(bf16[8,2,32,1024]{3,2,1,0:T(8,128)(2,1)} %get-tuple-element.40.send_rows, bf16[2,1024,1024]{2,1,0:T(8,128)(2,1)} %get-tuple-element.41.up_rows, bf16[1024,128]{1,0:T(8,128)(2,1)} %get-tuple-element.42.route.small_all, ...), custom_call_target="tpu_custom_call" | custom-call | flops 25769803776 | bytes 33554432 | tf_op jit(solution)/shard_map/pallas_call | solution.py:523
  216.5 67.9 %shard_map.180 = (bf16[256,1024]{1,0:T(8,128)(2,1)}, f32[256,1024]{1,0:T(8,128)}, bf16[32,3072]{1,0:T(8,128)(2,1)}, f32[32,1024]{1,0:T(8,128)}, f32[4,24,128]{2,1,0:T(8,128)}) custom-call(bf16[2,512,1024]{2,1,0:T(8,128)(2,1)} %bitcast.18, bf16[512,256]{1,0:T(8,128)(2,1)} %get-tuple-element.44.hit_in, f32[256,1024]{1,0:T(8,128)} %get-tuple-element.45.middle_in, ...), custom_call_target="tpu_custom_call" | custom-call | tf_op jit(solution)/shard_map/pallas_call | solution.py:1384
  284.4 11.8 %shard_map.181 = (bf16[256,1024]{1,0:T(8,128)(2,1)}, f32[256,1024]{1,0:T(8,128)}, f32[32,3072]{1,0:T(8,128)}, f32[32,1024]{1,0:T(8,128)}, f32[16,32]{1,0:T(8,128...) custom-call(bf16[256,1024]{1,0:T(8,128)(2,1)} %get-tuple-element.55.output, ...), custom_call_target="tpu_custom_call" | custom-call | tf_op jit(solution)/shard_map/pallas_call | solution.py:1005

commit v5 on v4

--- a/solution.py
+++ b/solution.py
@@ -12,7 +12,6 @@
 MASKED = -1e30
 ROOT = 0.7978845608028654
 TILE = 256
-STEP = 128
 SPREAD_FIRST = 3
 TURN = (1, 3, 2, 0)
 GRAD = 256
@@ -1057,7 +1056,6 @@
             barrier, inc=1, device_id={"fsdp": (chip ^ k) * 2 + core}, device_id_type=MESH
         )
     pl.semaphore_signal(barrier, inc=1, device_id={"fsdp": sibling}, device_id_type=MESH)
-    pl.semaphore_wait(barrier, 3 + chips)
 
     def local(source, to, sem):
         copy = pltpu.make_async_copy(source, to, sem)
@@ -1097,11 +1095,13 @@
         copy.wait()
     small[...] = jnp.zeros_like(small)
     grad_two[...] = jnp.zeros_like(grad_two)
-    lane = lax.broadcasted_iota(jnp.int32, (STEP, route.shape[1]), 1)
+    lane = lax.broadcasted_iota(jnp.int32, (tokens // 2, route.shape[1]), 1)
     chosen = jnp.transpose(jnp.broadcast_to(ids[...].astype(jnp.float32), (128, tokens)))[:, :1].astype(jnp.int32)
-    for t in range(tokens // STEP):
-        span = slice(t * STEP, (t + 1) * STEP)
-        position = me * tokens + t * STEP + lax.broadcasted_iota(jnp.int32, (STEP, 1), 0)
+    half = tokens // 2
+    direct = {}
+    for t in range(2):
+        span = slice(t * half, (t + 1) * half)
+        position = me * tokens + t * half + lax.broadcasted_iota(jnp.int32, (half, 1), 0)
         valid = jnp.where(position < length[0], 1.0, 0.0)
         scores = jnp.where(lane < experts_all, logits[span, :], MASKED)
         powers = jnp.exp(scores - jnp.max(scores, axis=1, keepdims=True))
@@ -1123,17 +1123,15 @@
         total = upstream + scale * (scaled - shrunk * jnp.mean(scaled * shrunk, axis=-1, keepdims=True))
         grad_middle[span, :] = total
         grad_in[span, :] = total.astype(low)
+        if t == 0:
+            pl.semaphore_wait(barrier, 3 + chips)
+        for side, peer in enumerate((one, two)):
+            direct[side, t] = remote(
+                "seq", peer, grad_in.at[pl.ds(t * half, half)], grads.at[pl.ds(me * tokens + t * half, half)],
+                g_send.at[side, t], g_recv.at[side, t],
+            )
     output_kept = local(output, output_out, load.at[8])
     own_grad = local(grad_in, grads.at[pl.ds(me * tokens, tokens)], load.at[0])
-    half = tokens // 2
-    direct = {}
-    for side, peer in enumerate((one, two)):
-        for order in range(2):
-            p = (order + side) % 2
-            direct[side, p] = remote(
-                "seq", peer, grad_in.at[pl.ds(p * half, half)], grads.at[pl.ds(me * tokens + p * half, half)],
-                g_send.at[side, p], g_recv.at[side, p],
-            )
     for n in range(width // 128):
         lanes = slice(n * 128, (n + 1) * 128)
         kinds = transposed_times(grad_logits[...], normed_two[:, lanes])
@@ -1256,6 +1254,32 @@
         pair_sum(1, k)
     grad_proj[:, group : 2 * group] = (grad_key[...] * (HEAD_DIM**-0.5)).astype(low)
     grad_proj[:, 2 * group :] = grad_value[...].astype(low)
+
+    def partial(j):
+        own_rows = pl.ds(pl.multiple_of(j * tokens, tokens), tokens)
+        for n in range(width // TILE):
+            lanes = slice(n * TILE, (n + 1) * TILE)
+            back = times_transposed(grad_proj[own_rows, :], heads[lanes, :])
+            gain_sum[:, lanes] += jnp.sum(back * normed[own_rows, lanes].astype(jnp.float32), axis=0, keepdims=True)
+            part[j, :, lanes] = back.astype(low)
+
+    summed = {}
+
+    def send_part(side, order):
+        near = (one, two)[side]
+        block_of = near if order else both
+        summed[side, order] = remote(
+            "seq", near, part.at[block_of, pl.ds(side * half, half)], first.at[side, order],
+            c_send.at[side, order], c_recv.at[side, order],
+        )
+
+    partial(both)
+    send_part(0, 0)
+    send_part(1, 0)
+    partial(one)
+    send_part(0, 1)
+    partial(two)
+    send_part(1, 1)
     for s in range(4):
         lanes = slice(s * group, (s + 1) * group)
         weights[lanes, :] = transposed_times(normed[:, lanes], grad_proj[...]).astype(low)
@@ -1280,20 +1304,7 @@
                     "fsdp", owner, own_a.at[k, pl.ds(s * share, share)], got_a.at[k, pl.ds(s * share, share)],
                     z_send.at[s + 3, k], z_recv.at[s + 3, k],
                 )
-    for j in range(4):
-        own_rows = slice(j * tokens, (j + 1) * tokens)
-        for n in range(width // TILE):
-            lanes = slice(n * TILE, (n + 1) * TILE)
-            back = times_transposed(grad_proj[own_rows, :], heads[lanes, :])
-            gain_sum[:, lanes] += jnp.sum(back * normed[own_rows, lanes].astype(jnp.float32), axis=0, keepdims=True)
-            part[j, :, lanes] = back.astype(low)
-    summed = {}
-    for side, (near, rest) in enumerate(((one, two), (two, one))):
-        rows = pl.ds(side * half, half)
-        for order, to in enumerate((both, near)):
-            summed[side, order] = remote(
-                "seq", near, part.at[to, rows], first.at[side, order], c_send.at[side, order], c_recv.at[side, order]
-            )
+    partial(me)
     for b in range(width // 128):
         small[b // 2, b % 2, gain_row : gain_row + 1, :] = gain_sum[:, b * 128 : (b + 1) * 128]
     for k in order_of:

time: 301 us -> 298 us (0.990)
  no operation moved by 1% of the time
where the time goes in v5:
time: 298 us; the launch traced here: 294 us
  Pallas kernels  292 us (98%)
    pallas_call x1, Pallas kernels, moe(): pl.pallas_call(functools.partial(moe_kernel, chips, cap, experts_all, SPR...  136 us
    pallas_call x1, Pallas kernels, front(): pl.pallas_call(functools.partial(front_kernel, count, cap, experts_all, s...  79.1 us
    pallas_call x1, Pallas kernels, back(): pl.pallas_call(functools.partial(back_kernel, count, experts_all), out_sh...  65.1 us
    pallas_call x1, Pallas kernels, finish(): pl.pallas_call(functools.partial(finish_kernel, experts_all, len(wide)),...  11.8 us

profile of v5, /device:TPU:0, one launch (start us, length us, event | category | flops | bytes accessed | tf_op | source)
XLA Modules:
  0.0 293.6 jit_solution(12191399406438685591)
XLA Ops:
  1.3 79.1 %shard_map.178 = (bf16[1024,1024]{1,0:T(8,128)(2,1)}, bf16[4,8,32,768]{3,2,1,0:T(8,128)(2,1)}, bf16[4,2,32,1024]{3,2,1,0:T(8,128)(2,1)}, bf16[1024,128]{1,0:T(8,...) custom-call(bf16[256,1024]{1,0:T(8,128)(2,1)} %bitcast.14, ...), custom_call_target="tpu_custom_call" | custom-call | tf_op jit(solution)/shard_map/pallas_call | solution.py:910
  80.4 136.1 %shard_map.179 = (bf16[2,8,2,32,1024]{4,3,2,1,0:T(8,128)(2,1)}, bf16[2,1024,1024]{2,1,0:T(8,128)(2,1)}, bf16[2,1024,1024]{2,1,0:T(8,128)(2,1)}) custom-call(bf16[8,2,32,1024]{3,2,1,0:T(8,128)(2,1)} %get-tuple-element.40.send_rows, bf16[2,1024,1024]{2,1,0:T(8,128)(2,1)} %get-tuple-element.41.up_rows, bf16[1024,128]{1,0:T(8,128)(2,1)} %get-tuple-element.42.route.small_all, ...), custom_call_target="tpu_custom_call" | custom-call | flops 25769803776 | bytes 33554432 | tf_op jit(solution)/shard_map/pallas_call | solution.py:522
  216.5 65.1 %shard_map.180 = (bf16[256,1024]{1,0:T(8,128)(2,1)}, f32[256,1024]{1,0:T(8,128)}, bf16[32,3072]{1,0:T(8,128)(2,1)}, f32[32,1024]{1,0:T(8,128)}, f32[4,24,128]{2,1,0:T(8,128)}) custom-call(bf16[2,512,1024]{2,1,0:T(8,128)(2,1)} %bitcast.18, bf16[512,256]{1,0:T(8,128)(2,1)} %get-tuple-element.44.hit_in, f32[256,1024]{1,0:T(8,128)} %get-tuple-element.45.middle_in, ...), custom_call_target="tpu_custom_call" | custom-call | tf_op jit(solution)/shard_map/pallas_call | solution.py:1395
  281.7 11.8 %shard_map.181 = (bf16[256,1024]{1,0:T(8,128)(2,1)}, f32[256,1024]{1,0:T(8,128)}, f32[32,3072]{1,0:T(8,128)}, f32[32,1024]{1,0:T(8,128)}, f32[16,32]{1,0:T(8,128...) custom-call(bf16[256,1024]{1,0:T(8,128)(2,1)} %get-tuple-element.55.output, ...), custom_call_target="tpu_custom_call" | custom-call | tf_op jit(solution)/shard_map/pallas_call | solution.py:1004

commit v6 on v5

--- a/solution.py
+++ b/solution.py
@@ -466,10 +466,12 @@
         all_arrived(1, k)
         if k >= spread_first:
             all_arrived(0, k)
+        if n == 0:
+            relay(1, turn[1])
         experts(k, 0)
         collect_one(k, 0)
-        if n < 2:
-            relay(1, turn[n + 1 + (n > 0)])
+        if n == 1:
+            relay(1, turn[3])
         if n == 0:
             z_arrived(turn[3])
             spread_out(1, turn[3])
@@ -990,7 +992,7 @@
 
 def finish(output, input_grad, heads, mix, small, gain, experts_all, wide):
     S, f32 = jax.ShapeDtypeStruct, jnp.float32
-    steps = 8
+    steps = 4
     share = heads.shape[0]
 
     def part(x, dim):

time: 298 us -> 297 us (level)
  no operation moved by 1% of the time
where the time goes in v6:
time: 297 us; the launch traced here: 293 us
  Pallas kernels  291 us (98%)
    pallas_call x1, Pallas kernels, moe(): pl.pallas_call(functools.partial(moe_kernel, chips, cap, experts_all, SPR...  136 us
    pallas_call x1, Pallas kernels, front(): pl.pallas_call(functools.partial(front_kernel, count, cap, experts_all, s...  79.1 us
    pallas_call x1, Pallas kernels, back(): pl.pallas_call(functools.partial(back_kernel, count, experts_all), out_sh...  64.5 us
    pallas_call x1, Pallas kernels, finish(): pl.pallas_call(functools.partial(finish_kernel, experts_all, len(wide)),...  11.1 us

profile of v6, /device:TPU:0, one launch (start us, length us, event | category | flops | bytes accessed | tf_op | source)
XLA Modules:
  0.0 292.7 jit_solution(15520257874203461413)
XLA Ops:
  1.3 79.1 %shard_map.178 = (bf16[1024,1024]{1,0:T(8,128)(2,1)}, bf16[4,8,32,768]{3,2,1,0:T(8,128)(2,1)}, bf16[4,2,32,1024]{3,2,1,0:T(8,128)(2,1)}, bf16[1024,128]{1,0:T(8,...) custom-call(bf16[256,1024]{1,0:T(8,128)(2,1)} %bitcast.14, ...), custom_call_target="tpu_custom_call" | custom-call | tf_op jit(solution)/shard_map/pallas_call | solution.py:912
  80.4 136.5 %shard_map.179 = (bf16[2,8,2,32,1024]{4,3,2,1,0:T(8,128)(2,1)}, bf16[2,1024,1024]{2,1,0:T(8,128)(2,1)}, bf16[2,1024,1024]{2,1,0:T(8,128)(2,1)}) custom-call(bf16[8,2,32,1024]{3,2,1,0:T(8,128)(2,1)} %get-tuple-element.40.send_rows, bf16[2,1024,1024]{2,1,0:T(8,128)(2,1)} %get-tuple-element.41.up_rows, bf16[1024,128]{1,0:T(8,128)(2,1)} %get-tuple-element.42.route.small_all, ...), custom_call_target="tpu_custom_call" | custom-call | flops 25769803776 | bytes 33554432 | tf_op jit(solution)/shard_map/pallas_call | solution.py:524
  216.9 64.5 %shard_map.180 = (bf16[256,1024]{1,0:T(8,128)(2,1)}, f32[256,1024]{1,0:T(8,128)}, bf16[32,3072]{1,0:T(8,128)(2,1)}, f32[32,1024]{1,0:T(8,128)}, f32[4,24,128]{2,1,0:T(8,128)}) custom-call(bf16[2,512,1024]{2,1,0:T(8,128)(2,1)} %bitcast.18, bf16[512,256]{1,0:T(8,128)(2,1)} %get-tuple-element.44.hit_in, f32[256,1024]{1,0:T(8,128)} %get-tuple-element.45.middle_in, ...), custom_call_target="tpu_custom_call" | custom-call | tf_op jit(solution)/shard_map/pallas_call | solution.py:1397
  281.4 11.1 %shard_map.181 = (bf16[256,1024]{1,0:T(8,128)(2,1)}, f32[256,1024]{1,0:T(8,128)}, f32[32,3072]{1,0:T(8,128)}, f32[32,1024]{1,0:T(8,128)}, f32[16,32]{1,0:T(8,128...) custom-call(bf16[256,1024]{1,0:T(8,128)(2,1)} %get-tuple-element.55.output, ...), custom_call_target="tpu_custom_call" | custom-call | tf_op jit(solution)/shard_map/pallas_call | solution.py:1006
